TPU v7x, 512 devices: a whole 4x8x8 slice. The times are simulated.
512 devices in a mesh: wide: 64 (over z, y_hi, core), narrow: 8 (over y_lo, x).
Axes of the slice: x: 4, y: 8 (y_hi: 4, y_lo: 2; y = y_hi * 2 + y_lo), z: 8, core: 2. Of those that a mesh axis runs over, the one named last changes fastest.
Arguments:
- activations: bfloat16 [32768, 4096], P('wide', 'narrow'), may hold values from -3 to 3
- out_grads: bfloat16 [32768, 1536], P('wide'), may hold values from -8 to 8
- in_basis: bfloat16 [4096, 4096], P('wide', 'narrow'), may hold values from -8 to 8, as said below
- out_basis: bfloat16 [1536, 1536], P('narrow'), may hold values from -8 to 8, as said below
- valid: int32 [32768], P('wide'), may hold values 0 or 1
Outputs:
- corrected: float32 [1536, 4096], P('wide', 'narrow')
Inputs may be any that keep to these rules, and one draw needn't show every extreme that they name: in_basis is a square basis with a dominant diagonal. out_basis is a square basis with a dominant diagonal.
All inputs are finite; a program needn't handle non-finite values. No bound on the sum of `valid` on one device may be relied on, other than what follows from the above.
Results may differ from a plain program's by a relative error of at most 0.0012.
Values may be sent and summed in bfloat16 or wider, within the bound.
No kernel may reach another device: no remote copies, remote signals or barrier semaphores. Data moves between devices by JAX's collectives and lax.ppermute only.
A program may use at most 64 MiB of HBM per device.

v0:
```python
import jax
import jax.numpy as jnp
from jax import lax
from jax.sharding import PartitionSpec as P

SEQ = 128


def rotate_grads(grads, out_basis):
    folded = jnp.dot(
        grads,
        lax.all_gather(out_basis, "narrow", axis=0, tiled=True),
        preferred_element_type=jnp.float32,
    )
    return folded.astype(jnp.bfloat16)


def shards(activations, out_grads, in_basis, out_basis, valid):
    token_count = activations.shape[0]
    basis_rows = lax.all_gather(in_basis, "wide", axis=0, tiled=True)
    rotated_in = jnp.dot(
        lax.all_gather(activations, "narrow", axis=1, tiled=True),
        basis_rows,
        preferred_element_type=jnp.float32,
    ).astype(jnp.bfloat16)
    rotated_out = rotate_grads(out_grads, out_basis)
    routed = valid.astype(jnp.bfloat16)
    masked_in = rotated_in * routed[:, None]
    seq_count = token_count // SEQ
    seq_in = masked_in.reshape(seq_count, SEQ, masked_in.shape[1])
    seq_out = rotated_out.reshape(seq_count, SEQ, rotated_out.shape[1])
    own_rows = rotated_out.shape[1] // lax.axis_size("wide")

    def advance(which, running):
        grads_cols = seq_out[which]
        product = lax.dot_general(
            grads_cols, seq_in[which], (((0,), (0,)), ((), ())), preferred_element_type=jnp.float32
        )
        return running + product * product

    summed = lax.psum_scatter(
        lax.fori_loop(
            0,
            seq_count,
            advance,
            jnp.zeros((own_rows * lax.axis_size("wide"), seq_in.shape[2]), jnp.float32),
        ),
        "wide",
        scatter_dimension=0,
        tiled=True,
    )
    return summed / (seq_count * lax.axis_size("wide"))


def solution(mesh):
    in_specs = (
        P("wide", "narrow"),
        P("wide", None),
        P("wide", "narrow"),
        P("narrow", None),
        P("wide"),
    )
    out_specs = P("wide", "narrow")
    return jax.shard_map(shards, mesh=mesh, in_specs=in_specs, out_specs=out_specs, check_vma=False)
```

profile of v0, /device:TPU:6, one launch (start us, length us, event | category | flops | bytes accessed | tf_op | source)
XLA Modules:
  0.0 405.8 jit_solution(7426177946697507075)
XLA Ops:
  6.5 0.0 copy-start
  6.5 0.0 all-gather.4.cloned.1.call-start
  6.5 0.7 all-gather.4.cloned.1.call-update
  7.3 0.0 all-gather.6.cloned.1.call-start
  7.3 0.7 all-gather.6.cloned.1.call-update
  8.0 0.0 all-gather.8.cloned.1.call-start
  8.1 0.7 all-gather.8.cloned.1.call-update
  8.7 0.0 reduce-scatter.2.cloned.1.call-start
  8.8 0.7 convert_element_type.11
  9.5 65.2 %all-gather.4.cloned.1.call-done = bf16[1536,1536]{1,0:T(8,128)(2,1)} async-done(((bf16[192,1536]{1,0:T(8,128)(2,1)}), bf16[1536,1536]{1,0:T(8,128)(2,1)}) %all-gather.4.cloned.1.call-update) | async-done | bytes 4718608 | tf_op jit(solution)/shard_map/all_gather | solution.py:12
  74.7 0.0 copy-done
  74.7 4.9 %convolution_convert_fusion = bf16[512,1536]{1,0:T(8,128)(2,1)S(1)} fusion(bf16[512,1536]{1,0:T(8,128)(2,1)S(1)} %copy-done, bf16[1536,1536]{1,0:T(8,128)(2,1)} %all-gather.4.cloned.1.call-done), kind=kOutput, calls=%fused_computation.7 | convolution fusion | flops 2416705536 | bytes 7864320 | tf_op jit(solution)/shard_map/dot_general | solution.py:10
  79.7 53.9 %all-gather.6.cloned.1.call-done = bf16[512,4096]{1,0:T(8,128)(2,1)} async-done(((bf16[512,512]{1,0:T(8,128)(2,1)}), bf16[512,4096]{1,0:T(8,128)(2,1)}) %all-gather.6.cloned.1.call-update) | async-done | bytes 4194320 | tf_op jit(solution)/shard_map/all_gather | solution.py:22
  133.6 91.4 %all-gather.8.cloned.1.call-done = bf16[4096,512]{1,0:T(8,128)(2,1)} async-done(((bf16[64,512]{1,0:T(8,128)(2,1)}), bf16[4096,512]{1,0:T(8,128)(2,1)}) %all-gather.8.cloned.1.call-update) | async-done | bytes 4194320 | tf_op jit(solution)/shard_map/all_gather | solution.py:20
  225.0 6.6 %fusion.6 = bf16[512,512]{1,0:T(8,128)(2,1)} fusion(bf16[512,4096]{1,0:T(8,128)(2,1)} %all-gather.6.cloned.1.call-done, bf16[4096,512]{1,0:T(8,128)(2,1)} %all-gather.8.cloned.1.call-done, bf16[512]{0:T(512)(128)(2,1)S(1)} %convert_element_type.11), kind=kOutput, calls=%fused_computation.9 | convolution fusion | flops 2148007936 | bytes 8913920 | tf_op jit(solution)/shard_map/dot_general | solution.py:21
  231.6 15.8 %while.14 = (s32[]{:T(128)}, f32[1536,512]{1,0:T(8,128)}, bf16[4,128,1536]{2,1,0:T(8,128)(2,1)S(1)}, bf16[4,128,512]{2,1,0:T(8,128)(2,1)}, s32[]{:T(128)}, /*index=5*/s32[]{:T(128)}) while((s32[]{:T(128)}, f32[1536,512]{1,0:T(8,128)}, bf16[4,128,1536]{2,1,0:T(8,128)(2,1)S(1)}, bf16[4,128,512]{2,1,0:T(8,128)(2,1)}, s32[]{:T(128)}, ...), condition=%wide.region_1.0_spmd.clone, body=%wide.region_0.0_spmd.clone.sunk | while | flops 203685888 | bytes 6816847 | solution.py:42
  231.6 3.1 fusion.16
  234.7 4.2 %fusion.16 = f32[1536,512]{1,0:T(8,128)} fusion(f32[1536,512]{1,0:T(8,128)} %get-tuple-element.140, pred[]{:T(512)S(6)} %compare.3, bf16[4,128,1536]{2,1,0:T(8,128)(2,1)S(1)} %get-tuple-element.147, s32[]{:T(128)} %get-tuple-element.139, bf16[4,128,512]{2,1,0:T(8,128)(2,1)} %get-tuple-element.148), kind=kOutput, calls=%fused_computation.1.clone.1 | convolution fusion | flops 203685888 | bytes 6816769 | tf_op jit(solution)/shard_map/while/body/eval_jaxpr/dot_general | solution.py:36
  238.9 4.2 %fusion.16 = f32[1536,512]{1,0:T(8,128)} fusion(f32[1536,512]{1,0:T(8,128)} %get-tuple-element.140, pred[]{:T(512)S(6)} %compare.3, bf16[4,128,1536]{2,1,0:T(8,128)(2,1)S(1)} %get-tuple-element.147, s32[]{:T(128)} %get-tuple-element.139, bf16[4,128,512]{2,1,0:T(8,128)(2,1)} %get-tuple-element.148), kind=kOutput, calls=%fused_computation.1.clone.1 | convolution fusion | flops 203685888 | bytes 6816769 | tf_op jit(solution)/shard_map/while/body/eval_jaxpr/dot_general | solution.py:36
  243.1 4.2 %fusion.16 = f32[1536,512]{1,0:T(8,128)} fusion(f32[1536,512]{1,0:T(8,128)} %get-tuple-element.140, pred[]{:T(512)S(6)} %compare.3, bf16[4,128,1536]{2,1,0:T(8,128)(2,1)S(1)} %get-tuple-element.147, s32[]{:T(128)} %get-tuple-element.139, bf16[4,128,512]{2,1,0:T(8,128)(2,1)} %get-tuple-element.148), kind=kOutput, calls=%fused_computation.1.clone.1 | convolution fusion | flops 203685888 | bytes 6816769 | tf_op jit(solution)/shard_map/while/body/eval_jaxpr/dot_general | solution.py:36
  247.3 0.0 reduce-scatter.2.cloned.1.call-update
  247.4 150.4 %reduce-scatter.2.cloned.1.call-done = f32[24,512]{1,0:T(8,128)} async-done(((f32[1536,512]{1,0:T(8,128)}), f32[24,512]{1,0:T(8,128)}) %reduce-scatter.2.cloned.1.call-update) | async-done | bytes 49168 | tf_op jit(solution)/shard_map/reduce_scatter | solution.py:41
  397.8 1.4 broadcast_multiply_fusion
  (1 shorter events, 0.0 us)
Async XLA Ops:
  6.5 68.2 %copy-start = (bf16[512,1536]{1,0:T(8,128)(2,1)S(1)}, bf16[512,1536]{1,0:T(8,128)(2,1)}, u32[]{:S(2)}) copy-start(bf16[512,1536]{1,0:T(8,128)(2,1)} %param.8) | copy-start | bytes 4718596
  6.5 68.2 %all-gather.4.cloned.1.call-start = ((), (), s32[]{:S(2)}) async-start(), calls=%async_computation.1 | async-start | bytes 5308416 | tf_op jit(solution)/shard_map/all_gather | solution.py:12
  7.3 126.3 %all-gather.6.cloned.1.call-start = ((), (), s32[]{:S(2)}) async-start(), calls=%async_computation.2 | async-start | bytes 4718592 | tf_op jit(solution)/shard_map/all_gather | solution.py:22
  8.0 217.0 %all-gather.8.cloned.1.call-start = ((), (), s32[]{:S(2)}) async-start(), calls=%async_computation.3 | async-start | bytes 4259840 | tf_op jit(solution)/shard_map/all_gather | solution.py:20
  8.7 389.1 %reduce-scatter.2.cloned.1.call-start = ((), (), s32[]{:S(2)}) async-start(), calls=%async_computation.4 | async-start | bytes 3194880 | tf_op jit(solution)/shard_map/reduce_scatter | solution.py:41
Sparse Core Ops, SparseCore 0:
  9.4 65.2 all-gather.3
  76.8 56.7 all-gather.5
  136.9 87.9 all-gather.7
  247.5 150.2 reduce-scatter.1
where the time goes:
time: 406 us
  waiting for transfers between devices  363 us (89%)
  matrix products  27.3 us (7%)
  between operations  13.1 us (3%)
    reduce_scatter x1, waiting for transfers between devices, shards(): lax.psum_scatter(lax.fori_loop(0, seq_count, advance, jnp.zeros((own_rows...  150 us
    all_gather x1, waiting for transfers between devices, shards(): basis_rows = lax.all_gather(in_basis, 'wide', axis=0, tiled=True)  91.4 us
    all_gather x1, waiting for transfers between devices, rotate_grads(): lax.all_gather(out_basis, 'narrow', axis=0, tiled=True)  65.2 us
    all_gather x1, waiting for transfers between devices, shards(): lax.all_gather(activations, 'narrow', axis=1, tiled=True)  53.9 us
    dot_general x4, matrix products, advance(): lax.dot_general(grads_cols, seq_in[which], (((0,), (0,)), ((), ())), pref...  15.8 us
  transfers between devices with their start and end apart: 4, of which 4 were waited for; matrix products, arithmetic and copies ran while one was open for 1% of the time, Pallas kernels for 0%

commit v1 on v0

v1 whole, which is shorter than its diff:
```python
import functools

import jax
import jax.numpy as jnp
import numpy as np
from jax import lax
from jax.experimental import pallas as pl
from jax.experimental.pallas import tpu as pltpu
from jax.sharding import PartitionSpec as P

SEQ = 128
NZ, NYH, NC, NYL, NX = 8, 4, 2, 2, 4
BOTH = ("wide", "narrow")
F32, BF16, F16 = jnp.float32, jnp.bfloat16, jnp.float16
VMEM = pl.BlockSpec(memory_space=pltpu.VMEM)
SMEM = pl.BlockSpec(memory_space=pltpu.SMEM)
LIMIT = 48 * 1024 * 1024


def send(value, target):
    pairs = []
    for z, yh, c, yl, x in np.ndindex(NZ, NYH, NC, NYL, NX):
        z2, yh2, c2, yl2, x2 = target(z, yh, c, yl, x)
        z2, yh2, c2, yl2, x2 = z2 % NZ, yh2 % NYH, c2 % NC, yl2 % NYL, x2 % NX
        source = (((z * NYH + yh) * NC + c) * NYL + yl) * NX + x
        pairs.append((source, (((z2 * NYH + yh2) * NC + c2) * NYL + yl2) * NX + x2))
    return lax.ppermute(value, BOTH, pairs)


def other_core(value):
    return send(value, lambda z, yh, c, yl, x: (z, yh, c + 1, yl, x))


def cost(flops, nbytes):
    return pl.CostEstimate(flops=flops, bytes_accessed=nbytes, transcendentals=0)


def call(kernel, out, scratch, flops, nbytes, n_vmem):
    return pl.pallas_call(
        kernel,
        out_shape=out,
        in_specs=[SMEM] + [VMEM] * n_vmem,
        out_specs=VMEM,
        scratch_shapes=scratch,
        compiler_params=pltpu.CompilerParams(vmem_limit_bytes=LIMIT),
        cost_estimate=cost(flops, nbytes),
    )


def rotate_out_kernel(pos, grads, *refs):
    pieces, out, basis = refs[:NX], refs[NX], refs[NX + 1]
    rows = pieces[0].shape[0] // NYL
    yl, x = pos[1], pos[2]
    for d in range(NX):
        for flip in range(NYL):
            owner = lax.rem(yl + flip, NYL) * NX + lax.rem(x - d + NX, NX)
            at = pl.multiple_of(owner * rows, 64)
            basis[pl.ds(at, rows), :] = pieces[d][flip * rows : (flip + 1) * rows, :]
    width = 256
    for j in range(out.shape[1] // width):
        cols = slice(j * width, (j + 1) * width)
        out[:, cols] = jnp.dot(grads[...], basis[:, cols], preferred_element_type=F32).astype(out.dtype)


def rotate_out(pos, grads, pieces):
    tokens, depth = grads.shape
    width = pieces[0].shape[1]
    return call(
        rotate_out_kernel,
        jax.ShapeDtypeStruct((tokens, width), BF16),
        [pltpu.VMEM((depth, width), BF16)],
        2 * tokens * depth * width,
        2 * (tokens * depth + depth * width + tokens * width),
        1 + NX,
    )(pos, grads, *pieces)


def rotate_in_kernel(pos, acts, mask, mine, other, out):
    z, core = pos[0], pos[3]
    chunk = mine.shape[0] // NZ
    half = out.shape[0] // 2
    for part in range(2):
        rows = slice(part * half, (part + 1) * half)
        total = jnp.zeros((half, out.shape[1]), F32)
        for r in range(NZ):
            plane = lax.rem(z - r + NZ, NZ) * (2 * chunk)
            for ref, c in ((mine, core), (other, 1 - core)):
                at = pl.multiple_of(plane + c * chunk, chunk)
                total += jnp.dot(
                    acts[rows, pl.ds(at, chunk)],
                    ref[r * chunk : (r + 1) * chunk, :],
                    preferred_element_type=F32,
                )
        kept = total.astype(BF16).astype(F32) * mask[rows, :]
        out[rows, :] = kept.astype(BF16)


def rotate_in(pos, acts, mask, mine, other):
    tokens, depth = acts.shape
    width = mine.shape[1]
    return call(
        rotate_in_kernel,
        jax.ShapeDtypeStruct((tokens, width), BF16),
        [],
        2 * tokens * depth * width,
        2 * (tokens * depth + depth * width + tokens * width),
        4,
    )(pos, acts, mask, mine, other)


def squares_kernel(pos, outs, ins, out):
    width = 256
    for j in range(out.shape[0] // width):
        cols = slice(j * width, (j + 1) * width)
        total = None
        for s in range(outs.shape[0] // SEQ):
            rows = slice(s * SEQ, (s + 1) * SEQ)
            grad = lax.dot_general(
                outs[rows, cols], ins[rows, :], (((0,), (0,)), ((), ())), preferred_element_type=F32
            )
            total = grad * grad if total is None else total + grad * grad
        out[cols, :] = total


def squares(pos, outs, ins):
    tokens, width = outs.shape
    return call(
        squares_kernel,
        jax.ShapeDtypeStruct((width, ins.shape[1]), F32),
        [],
        2 * tokens * width * ins.shape[1],
        2 * tokens * (width + ins.shape[1]) + 4 * width * ins.shape[1],
        2,
    )(pos, outs, ins)


def gather_in_basis(in_basis, z, yh):
    rows = in_basis.shape[0]

    def to(j):
        def target(z, yh, c, yl, x):
            i = (yh % 2) * 2 + c
            return z, i - j, yh // 2, yl, x

        return target

    got = [send(in_basis, to(j)) for j in range(NYH)]
    chunk = lax.dynamic_slice_in_dim(
        jnp.concatenate(got + got, axis=0), lax.rem(NYH - yh, NYH) * rows, NYH * rows, 0
    )
    up = lambda z, yh, c, yl, x: (z + 1, yh, c, yl, x)
    down = lambda z, yh, c, yl, x: (z - 1, yh, c, yl, x)
    from_below, from_above = [chunk], [chunk]
    for _ in range(3):
        from_below.append(send(from_below[-1], up))
        from_above.append(send(from_above[-1], down))
    half = chunk.shape[0] // 2
    far = [send(from_below[-1][:half], up), send(from_above[-1][half:], down)]
    return jnp.concatenate(from_below + far + from_above[:0:-1], axis=0)


def gather_out_basis(out_basis, core):
    width = out_basis.shape[1]
    own = width // (NZ * NYH * NC)
    source = lax.broadcasted_iota(jnp.int32, (width, width // NC), 0)
    place = lax.broadcasted_iota(jnp.int32, (width, width // NC), 1)
    wanted = ((place // own) * NC + core) * own + place % own
    picked = jnp.dot(out_basis, (source == wanted).astype(BF16), preferred_element_type=F32).astype(BF16)
    pair = jnp.concatenate([picked, send(picked, lambda z, yh, c, yl, x: (z, yh, c, yl + 1, x))], axis=0)
    pieces = [pair]
    for d in range(1, NX):
        pieces.append(send(pair, functools.partial(lambda d, z, yh, c, yl, x: (z, yh, c, yl, x + d), d)))
    return pieces


def scatter_sum(total):
    blocks = NZ * NYH
    groups = [[zy * NC + c for zy in range(blocks)] for c in range(NC)]
    rows, columns = total.shape[0] // blocks, total.shape[1]
    tiles = (rows // 8, columns // 128)
    top = jnp.max(total)
    power = jnp.maximum(jnp.floor(jnp.log2(jnp.maximum(top, 1e-30))), -100.0)
    coded = (total * jnp.exp2(14.0 - power)).astype(F16)
    coded = coded.reshape(blocks, tiles[0], 8, tiles[1], 128).transpose(0, 1, 3, 2, 4).reshape(blocks, -1, 128)
    label = jnp.broadcast_to(power.astype(F16), (blocks, 8, 128))
    got = lax.all_to_all(
        jnp.concatenate([coded, label], axis=1), "wide", 0, 0, tiled=True, axis_index_groups=groups
    )
    scale = jnp.exp2(got[:, -8:-7, :1].astype(F32) - 14.0)
    summed = jnp.sum(got[:, :-8, :].astype(F32) * scale, axis=0)
    return summed.reshape(tiles[0], tiles[1], 8, 128).transpose(0, 2, 1, 3).reshape(rows, columns)


def shards(activations, out_grads, in_basis, out_basis, valid):
    wide, narrow = lax.axis_index("wide"), lax.axis_index("narrow")
    z, yh, core = wide // (NYH * NC), (wide // NC) % NYH, wide % NC
    yl, x = narrow // NX, narrow % NX
    pos = jnp.stack([z, yl, x, core]).astype(jnp.int32)
    sequences = activations.shape[0] // SEQ * lax.axis_size("wide")

    acts = lax.all_gather(activations, "narrow", axis=1, tiled=True)
    mine = gather_in_basis(in_basis, z, yh)
    other = other_core(mine)
    pieces = gather_out_basis(out_basis, core)
    pieces_other = [other_core(piece) for piece in [jnp.concatenate(pieces, axis=0)]][0]
    pieces_other = jnp.split(pieces_other, NX, axis=0)

    mask = valid.astype(F32)[:, None]
    masked_in = rotate_in(pos, acts, mask, mine, other)
    out_other = rotate_out(pos, out_grads, pieces_other)
    out_mine = rotate_out(pos, out_grads, pieces)
    total = other_core(squares(pos, out_other, masked_in)) + squares(pos, out_mine, masked_in)
    return scatter_sum(total) / sequences


def solution(mesh):
    in_specs = (
        P("wide", "narrow"),
        P("wide", None),
        P("wide", "narrow"),
        P("narrow", None),
        P("wide"),
    )
    out_specs = P("wide", "narrow")
    return jax.shard_map(shards, mesh=mesh, in_specs=in_specs, out_specs=out_specs, check_vma=False)
```

time: 406 us -> 183 us (0.45)
  the two profiles are of different devices: /device:TPU:6 before, /device:TPU:8 now
where the time goes in v1:
time: 183 us; the launch traced here: 182 us
  starting transfers between devices  71.2 us (39%)
  blocking collectives  38.5 us (21%)
  waiting for transfers between devices  26.1 us (14%)
  between operations  14.7 us (8%)
  local copies, waits for them, and re-layouts  14.2 us (8%)
  Pallas kernels  13.2 us (7%)
  other arithmetic  2.28 us (1%)
  matrix products  1.84 us (1%)
    ppermute x19, starting transfers between devices, send(): return lax.ppermute(value, BOTH, pairs)  71.2 us
    all_to_all x1, blocking collectives, scatter_sum(): lax.all_to_all(jnp.concatenate([coded, label], axis=1), 'wide', 0, 0, til...  38.5 us
    ppermute x19, waiting for transfers between devices, send(): return lax.ppermute(value, BOTH, pairs)  25.3 us
    unnamed x39, local copies, waits for them, and re-layouts  9.65 us
    pallas_call x1, Pallas kernels, rotate_in(): call(rotate_in_kernel, jax.ShapeDtypeStruct((tokens, width), BF16), [], 2...  5.82 us
    pallas_call x2, Pallas kernels, rotate_out(): call(rotate_out_kernel, jax.ShapeDtypeStruct((tokens, width), BF16), [plt...  4.18 us
  transfers between devices with their start and end apart: 20, of which 3 were waited for; matrix products, arithmetic and copies ran while one was open for 8% of the time, Pallas kernels for 3%

profile of v1, /device:TPU:8, one launch (start us, length us, event | category | flops | bytes accessed | tf_op | source)
XLA Modules:
  0.0 182.0 jit_solution(18368788476088875435)
XLA Ops:
  6.5 0.7 all-gather.2.cloned.1.call-update
  7.3 1.5 collective-permute-start.5
  8.8 7.3 %collective-permute-start.6 = (bf16[64,512]{1,0:T(8,128)(2,1)}, bf16[64,512]{1,0:T(8,128)(2,1)S(1)}, u32[]{:S(2)}, u32[]{:S(2)}) collective-permute-start(bf16[64,512]{1,0:T(8,128)(2,1)} %param.7), channel_id=1, source_target_pairs={{0,48},{1,49},{2,50},{3,51},{4,52},{5,53},{6,54},{7,55},{8,0},{9,1... | collective-permute-start | bytes 196616 | tf_op jit(solution)/shard_map/ppermute | solution.py:27
  16.0 2.4 %collective-permute-start.7 = (bf16[64,512]{1,0:T(8,128)(2,1)}, bf16[64,512]{1,0:T(8,128)(2,1)S(1)}, u32[]{:S(2)}, u32[]{:S(2)}) collective-permute-start(bf16[64,512]{1,0:T(8,128)(2,1)} %param.7), channel_id=1, source_target_pairs={{0,32},{1,33},{2,34},{3,35},{4,36},{5,37},{6,38},{7,39},{8,48},{9,... | collective-permute-start | bytes 196616 | tf_op jit(solution)/shard_map/ppermute | solution.py:27
  18.4 4.4 %collective-permute-start.8 = (bf16[64,512]{1,0:T(8,128)(2,1)}, bf16[64,512]{1,0:T(8,128)(2,1)S(1)}, u32[]{:S(2)}, u32[]{:S(2)}) collective-permute-start(bf16[64,512]{1,0:T(8,128)(2,1)} %param.7), channel_id=1, source_target_pairs={{0,16},{1,17},{2,18},{3,19},{4,20},{5,21},{6,22},{7,23},{8,32},{9,... | collective-permute-start | bytes 196616 | tf_op jit(solution)/shard_map/ppermute | solution.py:27
  22.8 1.8 %constant_dynamic-update-slice_fusion.4 = (bf16[1536,768]{1,0:T(8,128)(2,1)}, bf16[192,768]{1,0:T(8,128)(2,1)S(1)}) fusion(bf16[192,1536]{1,0:T(8,128)(2,1)S(1)} %copy-done, s32[768]{0:T(1024)S(1)} %get-tuple-element.16, s32[768]{0:T(1024)S(1)} %get-tuple-element.17, s32[]{:T(128)} %select_n.42, s32[768]{0:T(1024)S(1)} %get-tuple-element.15, ...), kind=kOutput, calls=%fused_computation.20 | convolution fusion | flops 461389824 | bytes 1193476 | tf_op jit(solution)/shard_map/dot_general | solution.py:168
  24.7 3.2 %collective-permute-start = (bf16[192,768]{1,0:T(8,128)(2,1)S(1)}, bf16[192,768]{1,0:T(8,128)(2,1)S(1)}, u32[]{:S(2)}, u32[]{:S(2)}) collective-permute-start(bf16[192,768]{1,0:T(8,128)(2,1)S(1)} %get-tuple-element.14), channel_id=1, source_target_pairs={{0,4},{1,5},{2,6},{3,7},{4,0},{5,1},{6,2},{7,3},{8,12},{9,13},{10,... | collective-permute-start | bytes 884744 | tf_op jit(solution)/shard_map/ppermute | solution.py:27
  28.0 0.0 collective-permute-done.5
  28.0 0.0 collective-permute-done.6
  28.0 0.0 collective-permute-done.7
  28.1 0.0 collective-permute-done.8
  28.1 0.7 constant_dynamic-update-slice_fusion.21
  28.9 4.3 %collective-permute-start.9 = (bf16[256,512]{1,0:T(8,128)(2,1)S(1)}, bf16[256,512]{1,0:T(8,128)(2,1)S(1)}, u32[]{:S(2)}, u32[]{:S(2)}) collective-permute-start(bf16[256,512]{1,0:T(8,128)(2,1)S(1)} %get-tuple-element.8), channel_id=1, source_target_pairs={{0,64},{1,65},{2,66},{3,67},{4,68},{5,69},{6,70},{7,71},{8,72},{9,... | collective-permute-start | bytes 786440 | tf_op jit(solution)/shard_map/ppermute | solution.py:27
  33.1 8.6 %collective-permute-start.13 = (bf16[256,512]{1,0:T(8,128)(2,1)S(1)}, bf16[256,512]{1,0:T(8,128)(2,1)S(1)}, u32[]{:S(2)}, u32[]{:S(2)}) collective-permute-start(bf16[256,512]{1,0:T(8,128)(2,1)S(1)} %get-tuple-element.8), channel_id=1, source_target_pairs={{0,448},{1,449},{2,450},{3,451},{4,452},{5,453},{6,454},{7,455},{8... | collective-permute-start | bytes 786440 | tf_op jit(solution)/shard_map/ppermute | solution.py:27
  41.7 4.1 %collective-permute-done.9 = bf16[256,512]{1,0:T(8,128)(2,1)S(1)} collective-permute-done((bf16[256,512]{1,0:T(8,128)(2,1)S(1)}, bf16[256,512]{1,0:T(8,128)(2,1)S(1)}, u32[]{:S(2)}, u32[]{:S(2)}) %collective-permute-start.9) | collective-permute-done | bytes 262176 | tf_op jit(solution)/shard_map/ppermute | solution.py:27
  45.9 1.9 %collective-permute-start.10 = (bf16[256,512]{1,0:T(8,128)(2,1)S(1)}, bf16[256,512]{1,0:T(8,128)(2,1)S(1)}, u32[]{:S(2)}, u32[]{:S(2)}) collective-permute-start(bf16[256,512]{1,0:T(8,128)(2,1)S(1)} %collective-permute-done.9), channel_id=1, source_target_pairs={{0,64},{1,65},{2,66},{3,67},{4,68},{5,69},{6,70},{7,71},{8,72},{9,... | collective-permute-start | bytes 786440 | tf_op jit(solution)/shard_map/ppermute | solution.py:27
  47.8 0.0 collective-permute-done.13
  47.8 5.4 %collective-permute-start.14 = (bf16[256,512]{1,0:T(8,128)(2,1)S(1)}, bf16[256,512]{1,0:T(8,128)(2,1)S(1)}, u32[]{:S(2)}, u32[]{:S(2)}) collective-permute-start(bf16[256,512]{1,0:T(8,128)(2,1)S(1)} %collective-permute-done.13), channel_id=1, source_target_pairs={{0,448},{1,449},{2,450},{3,451},{4,452},{5,453},{6,454},{7,455},{8... | collective-permute-start | bytes 786440 | tf_op jit(solution)/shard_map/ppermute | solution.py:27
  53.2 0.0 collective-permute-done
  53.3 3.9 %collective-permute-start.1 = (bf16[384,768]{1,0:T(8,128)(2,1)S(1)}, bf16[384,768]{1,0:T(8,128)(2,1)S(1)}, u32[]{:S(2)}, u32[]{:S(2)}) collective-permute-start(bf16[384,768]{1,0:T(8,128)(2,1)S(1)} %pad_maximum_fusion.refs_0_), channel_id=1, source_target_pairs={{0,1},{1,2},{2,3},{3,0},{4,5},{5,6},{6,7},{7,4},{8,9},{9,10},{10,1... | collective-permute-start | bytes 1769480 | tf_op jit(solution)/shard_map/ppermute | solution.py:27
  57.1 4.2 %collective-permute-start.2 = (bf16[384,768]{1,0:T(8,128)(2,1)S(1)}, bf16[384,768]{1,0:T(8,128)(2,1)S(1)}, u32[]{:S(2)}, u32[]{:S(2)}) collective-permute-start(bf16[384,768]{1,0:T(8,128)(2,1)S(1)} %pad_maximum_fusion.refs_0_), channel_id=1, source_target_pairs={{0,2},{1,3},{2,0},{3,1},{4,6},{5,7},{6,4},{7,5},{8,10},{9,11},{10,... | collective-permute-start | bytes 1769480 | tf_op jit(solution)/shard_map/ppermute | solution.py:27
  61.3 3.8 %collective-permute-start.3 = (bf16[384,768]{1,0:T(8,128)(2,1)S(1)}, bf16[384,768]{1,0:T(8,128)(2,1)S(1)}, u32[]{:S(2)}, u32[]{:S(2)}) collective-permute-start(bf16[384,768]{1,0:T(8,128)(2,1)S(1)} %pad_maximum_fusion.refs_0_), channel_id=1, source_target_pairs={{0,3},{1,0},{2,1},{3,2},{4,7},{5,4},{6,5},{7,6},{8,11},{9,8},{10,9... | collective-permute-start | bytes 1769480 | tf_op jit(solution)/shard_map/ppermute | solution.py:27
  65.1 0.0 collective-permute-done.10
  65.2 1.9 %collective-permute-start.11 = (bf16[256,512]{1,0:T(8,128)(2,1)S(1)}, bf16[256,512]{1,0:T(8,128)(2,1)S(1)}, u32[]{:S(2)}, u32[]{:S(2)}) collective-permute-start(bf16[256,512]{1,0:T(8,128)(2,1)S(1)} %collective-permute-done.10), channel_id=1, source_target_pairs={{0,64},{1,65},{2,66},{3,67},{4,68},{5,69},{6,70},{7,71},{8,72},{9,... | collective-permute-start | bytes 786440 | tf_op jit(solution)/shard_map/ppermute | solution.py:27
  67.1 5.1 %collective-permute-start.15 = (bf16[256,512]{1,0:T(8,128)(2,1)S(1)}, bf16[256,512]{1,0:T(8,128)(2,1)S(1)}, u32[]{:S(2)}, u32[]{:S(2)}) collective-permute-start(bf16[256,512]{1,0:T(8,128)(2,1)S(1)} %collective-permute-done.14), channel_id=1, source_target_pairs={{0,448},{1,449},{2,450},{3,451},{4,452},{5,453},{6,454},{7,455},{8... | collective-permute-start | bytes 786440 | tf_op jit(solution)/shard_map/ppermute | solution.py:27
  72.2 0.7 constant_dynamic-update-slice_fusion.3
  73.0 0.7 constant_dynamic-update-slice_fusion.20
  73.7 0.7 constant_dynamic-update-slice_fusion.19
  74.4 1.1 collective-permute-done.11
  75.5 1.9 %collective-permute-start.12 = (bf16[128,512]{1,0:T(8,128)(2,1)S(1)}, bf16[128,512]{1,0:T(8,128)(2,1)S(1)}, u32[]{:S(2)}, u32[]{:S(2)}) collective-permute-start(bf16[128,512]{1,0:T(8,128)(2,1)S(1)} %slice.16), channel_id=1, source_target_pairs={{0,64},{1,65},{2,66},{3,67},{4,68},{5,69},{6,70},{7,71},{8,72},{9,... | collective-permute-start | bytes 393224 | tf_op jit(solution)/shard_map/ppermute | solution.py:27
  77.4 0.0 collective-permute-done.15
  77.5 5.1 %collective-permute-start.16 = (bf16[128,512]{1,0:T(8,128)(2,1)S(1)}, bf16[128,512]{1,0:T(8,128)(2,1)S(1)}, u32[]{:S(2)}, u32[]{:S(2)}) collective-permute-start(bf16[128,512]{1,0:T(8,128)(2,1)S(1)} %slice.17), channel_id=1, source_target_pairs={{0,448},{1,449},{2,450},{3,451},{4,452},{5,453},{6,454},{7,455},{8... | collective-permute-start | bytes 393224 | tf_op jit(solution)/shard_map/ppermute | solution.py:27
  82.6 20.1 %collective-permute-done.1.refs_1_ = bf16[384,768]{1,0:T(8,128)(2,1)S(1)} collective-permute-done((bf16[384,768]{1,0:T(8,128)(2,1)S(1)}, bf16[384,768]{1,0:T(8,128)(2,1)S(1)}, u32[]{:S(2)}, u32[]{:S(2)}) %collective-permute-start.1) | collective-permute-done | bytes 589856 | tf_op jit(solution)/shard_map/ppermute | solution.py:27
  102.7 0.9 constant_dynamic-update-slice_fusion.2
  103.6 0.0 collective-permute-done.2.refs_2_
  103.6 1.0 constant_dynamic-update-slice_fusion.1
  104.6 0.9 constant_dynamic-update-slice_fusion
  105.5 2.0 %collective-permute-start.4 = (bf16[1536,768]{1,0:T(8,128)(2,1)}, bf16[1536,768]{1,0:T(8,128)(2,1)}, u32[]{:S(2)}, u32[]{:S(2)}) collective-permute-start(bf16[1536,768]{1,0:T(8,128)(2,1)} %constant_dynamic-update-slice_fusion), channel_id=1, source_target_pairs={{0,8},{1,9},{2,10},{3,11},{4,12},{5,13},{6,14},{7,15},{8,0},{9,1},... | collective-permute-start | bytes 7077896 | tf_op jit(solution)/shard_map/ppermute | solution.py:27
  107.5 0.7 constant_dynamic-update-slice_fusion.18
  108.2 0.7 constant_dynamic-update-slice_fusion.17
  108.9 0.7 constant_dynamic-update-slice_fusion.16
  109.6 0.7 constant_dynamic-update-slice_fusion.15
  110.3 0.7 constant_dynamic-update-slice_fusion.14
  111.0 0.7 constant_dynamic-update-slice_fusion.13.mine
  111.8 2.3 %collective-permute-start.17 = (bf16[2048,512]{1,0:T(8,128)(2,1)}, bf16[2048,512]{1,0:T(8,128)(2,1)}, u32[]{:S(2)}, u32[]{:S(2)}) collective-permute-start(bf16[2048,512]{1,0:T(8,128)(2,1)} %constant_dynamic-update-slice_fusion.13.mine), channel_id=1, source_target_pairs={{0,8},{1,9},{2,10},{3,11},{4,12},{5,13},{6,14},{7,15},{8,0},{9,1},... | collective-permute-start | bytes 6291464 | tf_op jit(solution)/shard_map/ppermute | solution.py:27
  114.1 0.9 copy.11.mask
  115.0 0.1 pad_add_fusion.pos
  115.1 1.9 %fusion.21 = (bf16[384,768]{1,0:T(8,128)(2,1)S(1)}, bf16[384,768]{1,0:T(8,128)(2,1)S(1)}, bf16[384,768]{1,0:T(8,128)(2,1)S(1)}, bf16[384,768]{1,0:T(8,128)(2,1)S(1)}) fusion(bf16[1536,768]{1,0:T(8,128)(2,1)} %collective-permute-done.4), kind=kLoop, calls=%fused_computation.55 | loop fusion | bytes 4718592 | tf_op jit(solution)/shard_map/split | solution.py:206
  117.0 0.2 copy-done.1
  117.2 2.1 %shard_map.55.outs = bf16[512,768]{1,0:T(8,128)(2,1)S(1)} custom-call(s32[4]{0:T(128)S(1)} %pad_add_fusion.pos, bf16[512,1536]{1,0:T(8,128)(2,1)S(1)} %copy-done.1, bf16[384,768]{1,0:T(8,128)(2,1)S(1)} %get-tuple-element.12.refs_0_, bf16[384,768]{1,0:T(8,128)(2,1)S(1)} %get-tuple-element.11.refs_1_, bf16[384,768]{1,0:T(8,128)(2,1)S(1)} %get-tuple-element.10.refs_2_, ...), custom_call_target="tpu_custom_call" | custom-call | flops 1207959552 | bytes 4718592 | tf_op jit(solution)/shard_map/pallas_call | solution.py:68
  119.3 0.0 all-gather.2.cloned.1.call-done.acts
  119.3 0.9 copy-done.8
  120.3 5.8 %shard_map.56.ins = bf16[512,512]{1,0:T(8,128)(2,1)S(1)} custom-call(s32[4]{0:T(128)S(1)} %pad_add_fusion.pos, bf16[512,4096]{1,0:T(8,128)(2,1)} %all-gather.2.cloned.1.call-done.acts, f32[512,1]{1,0:T(8,128)S(1)} %copy-done.8, bf16[2048,512]{1,0:T(8,128)(2,1)} %constant_dynamic-update-slice_fusion.13.mine, bf16[2048,512]{1,0:T(8,128)(2,1)} %collective-permute-done.17.other), custom_call_target="tpu_custom_call" | custom-call | flops 2147483648 | bytes 8912896 | tf_op jit(solution)/shard_map/pallas_call | solution.py:101
  126.1 1.6 shard_map.57
  127.7 2.0 %collective-permute-start.18 = (f32[768,512]{1,0:T(8,128)S(1)}, f32[768,512]{1,0:T(8,128)S(1)}, u32[]{:S(2)}, u32[]{:S(2)}) collective-permute-start(f32[768,512]{1,0:T(8,128)S(1)} %shard_map.57), channel_id=1, source_target_pairs={{0,8},{1,9},{2,10},{3,11},{4,12},{5,13},{6,14},{7,15},{8,0},{9,1},... | collective-permute-start | bytes 4718600 | tf_op jit(solution)/shard_map/ppermute | solution.py:27
  129.8 2.1 %shard_map.58.outs = bf16[512,768]{1,0:T(8,128)(2,1)S(1)} custom-call(s32[4]{0:T(128)S(1)} %pad_add_fusion.pos, bf16[512,1536]{1,0:T(8,128)(2,1)S(1)} %copy-done.1, bf16[384,768]{1,0:T(8,128)(2,1)S(1)} %pad_maximum_fusion.refs_0_, bf16[384,768]{1,0:T(8,128)(2,1)S(1)} %copy-done.3, bf16[384,768]{1,0:T(8,128)(2,1)S(1)} %copy-done.5, bf16[384,768]{1,0:T(8,128)(2,1)S(1)} %copy-done.7), custom_call_target="tpu_custom_call" | custom-call | flops 1207959552 | bytes 4718592 | tf_op jit(solution)/shard_map/pallas_call | solution.py:68
  131.9 1.6 shard_map.59
  133.5 1.1 fusion.20
  135.3 0.2 multiply_convert_fusion
  135.5 0.2 concatenate.20
  135.7 38.5 %all_to_all.5 = f16[32,104,128]{2,1,0:T(8,128)(2,1)S(1)} all-to-all(f16[32,104,128]{2,1,0:T(8,128)(2,1)S(1)} %concatenate.20), channel_id=1, replica_groups={{0,16,32,48,64,80,96,112,128,144,160,176,192,208,224,240,256,272,288,30..., dimensions={0} | all-to-all | bytes 1703936 | tf_op jit(solution)/shard_map/all_to_all | solution.py:186
  174.2 0.1 copy.13
  174.3 0.2 multiply_reduce_fusion
  174.5 0.6 broadcast_multiply_fusion
  (43 shorter events, 0.2 us)
Async XLA Ops:
  6.5 16.3 %copy-start = (bf16[192,1536]{1,0:T(8,128)(2,1)S(1)}, bf16[192,1536]{1,0:T(8,128)(2,1)}, u32[]{:S(2)}) copy-start(bf16[192,1536]{1,0:T(8,128)(2,1)} %param.8) | copy-start | bytes 1769476
  6.5 112.8 %all-gather.2.cloned.1.call-start = ((), (), s32[]{:S(2)}) async-start(), calls=%async_computation.1 | async-start | bytes 4718592 | tf_op jit(solution)/shard_map/all_gather | solution.py:201
  7.3 20.7 %collective-permute-start.5 = (bf16[64,512]{1,0:T(8,128)(2,1)}, bf16[64,512]{1,0:T(8,128)(2,1)S(1)}, u32[]{:S(2)}, u32[]{:S(2)}) collective-permute-start(bf16[64,512]{1,0:T(8,128)(2,1)} %param.7), channel_id=1, source_target_pairs={{0,0},{1,1},{2,2},{3,3},{4,4},{5,5},{6,6},{7,7},{8,16},{9,17},{10,... | collective-permute-start | bytes 196616 | tf_op jit(solution)/shard_map/ppermute | solution.py:27
  8.8 19.2 %collective-permute-start.6 = (bf16[64,512]{1,0:T(8,128)(2,1)}, bf16[64,512]{1,0:T(8,128)(2,1)S(1)}, u32[]{:S(2)}, u32[]{:S(2)}) collective-permute-start(bf16[64,512]{1,0:T(8,128)(2,1)} %param.7), channel_id=1, source_target_pairs={{0,48},{1,49},{2,50},{3,51},{4,52},{5,53},{6,54},{7,55},{8,0},{9,1... | collective-permute-start | bytes 196616 | tf_op jit(solution)/shard_map/ppermute | solution.py:27
  16.0 12.0 %collective-permute-start.7 = (bf16[64,512]{1,0:T(8,128)(2,1)}, bf16[64,512]{1,0:T(8,128)(2,1)S(1)}, u32[]{:S(2)}, u32[]{:S(2)}) collective-permute-start(bf16[64,512]{1,0:T(8,128)(2,1)} %param.7), channel_id=1, source_target_pairs={{0,32},{1,33},{2,34},{3,35},{4,36},{5,37},{6,38},{7,39},{8,48},{9,... | collective-permute-start | bytes 196616 | tf_op jit(solution)/shard_map/ppermute | solution.py:27
  18.4 9.7 %collective-permute-start.8 = (bf16[64,512]{1,0:T(8,128)(2,1)}, bf16[64,512]{1,0:T(8,128)(2,1)S(1)}, u32[]{:S(2)}, u32[]{:S(2)}) collective-permute-start(bf16[64,512]{1,0:T(8,128)(2,1)} %param.7), channel_id=1, source_target_pairs={{0,16},{1,17},{2,18},{3,19},{4,20},{5,21},{6,22},{7,23},{8,32},{9,... | collective-permute-start | bytes 196616 | tf_op jit(solution)/shard_map/ppermute | solution.py:27
  24.7 28.6 %collective-permute-start = (bf16[192,768]{1,0:T(8,128)(2,1)S(1)}, bf16[192,768]{1,0:T(8,128)(2,1)S(1)}, u32[]{:S(2)}, u32[]{:S(2)}) collective-permute-start(bf16[192,768]{1,0:T(8,128)(2,1)S(1)} %get-tuple-element.14), channel_id=1, source_target_pairs={{0,4},{1,5},{2,6},{3,7},{4,0},{5,1},{6,2},{7,3},{8,12},{9,13},{10,... | collective-permute-start | bytes 884744 | tf_op jit(solution)/shard_map/ppermute | solution.py:27
  28.9 17.0 %collective-permute-start.9 = (bf16[256,512]{1,0:T(8,128)(2,1)S(1)}, bf16[256,512]{1,0:T(8,128)(2,1)S(1)}, u32[]{:S(2)}, u32[]{:S(2)}) collective-permute-start(bf16[256,512]{1,0:T(8,128)(2,1)S(1)} %get-tuple-element.8), channel_id=1, source_target_pairs={{0,64},{1,65},{2,66},{3,67},{4,68},{5,69},{6,70},{7,71},{8,72},{9,... | collective-permute-start | bytes 786440 | tf_op jit(solution)/shard_map/ppermute | solution.py:27
  33.1 14.6 %collective-permute-start.13 = (bf16[256,512]{1,0:T(8,128)(2,1)S(1)}, bf16[256,512]{1,0:T(8,128)(2,1)S(1)}, u32[]{:S(2)}, u32[]{:S(2)}) collective-permute-start(bf16[256,512]{1,0:T(8,128)(2,1)S(1)} %get-tuple-element.8), channel_id=1, source_target_pairs={{0,448},{1,449},{2,450},{3,451},{4,452},{5,453},{6,454},{7,455},{8... | collective-permute-start | bytes 786440 | tf_op jit(solution)/shard_map/ppermute | solution.py:27
  45.9 19.3 %collective-permute-start.10 = (bf16[256,512]{1,0:T(8,128)(2,1)S(1)}, bf16[256,512]{1,0:T(8,128)(2,1)S(1)}, u32[]{:S(2)}, u32[]{:S(2)}) collective-permute-start(bf16[256,512]{1,0:T(8,128)(2,1)S(1)} %collective-permute-done.9), channel_id=1, source_target_pairs={{0,64},{1,65},{2,66},{3,67},{4,68},{5,69},{6,70},{7,71},{8,72},{9,... | collective-permute-start | bytes 786440 | tf_op jit(solution)/shard_map/ppermute | solution.py:27
  47.8 19.3 %collective-permute-start.14 = (bf16[256,512]{1,0:T(8,128)(2,1)S(1)}, bf16[256,512]{1,0:T(8,128)(2,1)S(1)}, u32[]{:S(2)}, u32[]{:S(2)}) collective-permute-start(bf16[256,512]{1,0:T(8,128)(2,1)S(1)} %collective-permute-done.13), channel_id=1, source_target_pairs={{0,448},{1,449},{2,450},{3,451},{4,452},{5,453},{6,454},{7,455},{8... | collective-permute-start | bytes 786440 | tf_op jit(solution)/shard_map/ppermute | solution.py:27
  53.3 49.4 %collective-permute-start.1 = (bf16[384,768]{1,0:T(8,128)(2,1)S(1)}, bf16[384,768]{1,0:T(8,128)(2,1)S(1)}, u32[]{:S(2)}, u32[]{:S(2)}) collective-permute-start(bf16[384,768]{1,0:T(8,128)(2,1)S(1)} %pad_maximum_fusion.refs_0_), channel_id=1, source_target_pairs={{0,1},{1,2},{2,3},{3,0},{4,5},{5,6},{6,7},{7,4},{8,9},{9,10},{10,1... | collective-permute-start | bytes 1769480 | tf_op jit(solution)/shard_map/ppermute | solution.py:27
  57.1 46.5 %collective-permute-start.2 = (bf16[384,768]{1,0:T(8,128)(2,1)S(1)}, bf16[384,768]{1,0:T(8,128)(2,1)S(1)}, u32[]{:S(2)}, u32[]{:S(2)}) collective-permute-start(bf16[384,768]{1,0:T(8,128)(2,1)S(1)} %pad_maximum_fusion.refs_0_), channel_id=1, source_target_pairs={{0,2},{1,3},{2,0},{3,1},{4,6},{5,7},{6,4},{7,5},{8,10},{9,11},{10,... | collective-permute-start | bytes 1769480 | tf_op jit(solution)/shard_map/ppermute | solution.py:27
  61.3 43.2 %collective-permute-start.3 = (bf16[384,768]{1,0:T(8,128)(2,1)S(1)}, bf16[384,768]{1,0:T(8,128)(2,1)S(1)}, u32[]{:S(2)}, u32[]{:S(2)}) collective-permute-start(bf16[384,768]{1,0:T(8,128)(2,1)S(1)} %pad_maximum_fusion.refs_0_), channel_id=1, source_target_pairs={{0,3},{1,0},{2,1},{3,2},{4,7},{5,4},{6,5},{7,6},{8,11},{9,8},{10,9... | collective-permute-start | bytes 1769480 | tf_op jit(solution)/shard_map/ppermute | solution.py:27
  65.2 10.4 %collective-permute-start.11 = (bf16[256,512]{1,0:T(8,128)(2,1)S(1)}, bf16[256,512]{1,0:T(8,128)(2,1)S(1)}, u32[]{:S(2)}, u32[]{:S(2)}) collective-permute-start(bf16[256,512]{1,0:T(8,128)(2,1)S(1)} %collective-permute-done.10), channel_id=1, source_target_pairs={{0,64},{1,65},{2,66},{3,67},{4,68},{5,69},{6,70},{7,71},{8,72},{9,... | collective-permute-start | bytes 786440 | tf_op jit(solution)/shard_map/ppermute | solution.py:27
  67.1 10.4 %collective-permute-start.15 = (bf16[256,512]{1,0:T(8,128)(2,1)S(1)}, bf16[256,512]{1,0:T(8,128)(2,1)S(1)}, u32[]{:S(2)}, u32[]{:S(2)}) collective-permute-start(bf16[256,512]{1,0:T(8,128)(2,1)S(1)} %collective-permute-done.14), channel_id=1, source_target_pairs={{0,448},{1,449},{2,450},{3,451},{4,452},{5,453},{6,454},{7,455},{8... | collective-permute-start | bytes 786440 | tf_op jit(solution)/shard_map/ppermute | solution.py:27
  75.5 32.7 %collective-permute-start.12 = (bf16[128,512]{1,0:T(8,128)(2,1)S(1)}, bf16[128,512]{1,0:T(8,128)(2,1)S(1)}, u32[]{:S(2)}, u32[]{:S(2)}) collective-permute-start(bf16[128,512]{1,0:T(8,128)(2,1)S(1)} %slice.16), channel_id=1, source_target_pairs={{0,64},{1,65},{2,66},{3,67},{4,68},{5,69},{6,70},{7,71},{8,72},{9,... | collective-permute-start | bytes 393224 | tf_op jit(solution)/shard_map/ppermute | solution.py:27
  77.5 31.4 %collective-permute-start.16 = (bf16[128,512]{1,0:T(8,128)(2,1)S(1)}, bf16[128,512]{1,0:T(8,128)(2,1)S(1)}, u32[]{:S(2)}, u32[]{:S(2)}) collective-permute-start(bf16[128,512]{1,0:T(8,128)(2,1)S(1)} %slice.17), channel_id=1, source_target_pairs={{0,448},{1,449},{2,450},{3,451},{4,452},{5,453},{6,454},{7,455},{8... | collective-permute-start | bytes 393224 | tf_op jit(solution)/shard_map/ppermute | solution.py:27
  102.7 6.2 %copy-start.2 = (bf16[384,768]{1,0:T(8,128)(2,1)}, bf16[384,768]{1,0:T(8,128)(2,1)S(1)}, u32[]{:S(2)}) copy-start(bf16[384,768]{1,0:T(8,128)(2,1)S(1)} %collective-permute-done.1.refs_1_) | copy-start | bytes 1769476
  103.6 7.4 %copy-start.4 = (bf16[384,768]{1,0:T(8,128)(2,1)}, bf16[384,768]{1,0:T(8,128)(2,1)S(1)}, u32[]{:S(2)}) copy-start(bf16[384,768]{1,0:T(8,128)(2,1)S(1)} %collective-permute-done.2.refs_2_) | copy-start | bytes 1769476
  104.6 9.5 %copy-start.9 = (s32[512]{0:T(512)S(1)}, s32[512]{0:T(512)}, u32[]{:S(2)}) copy-start(s32[512]{0:T(512)} %param.9) | copy-start | bytes 6148
  104.6 10.4 %copy-start.6 = (bf16[384,768]{1,0:T(8,128)(2,1)}, bf16[384,768]{1,0:T(8,128)(2,1)S(1)}, u32[]{:S(2)}) copy-start(bf16[384,768]{1,0:T(8,128)(2,1)S(1)} %collective-permute-done.3.refs_3_) | copy-start | bytes 1769476
  105.5 9.6 %collective-permute-start.4 = (bf16[1536,768]{1,0:T(8,128)(2,1)}, bf16[1536,768]{1,0:T(8,128)(2,1)}, u32[]{:S(2)}, u32[]{:S(2)}) collective-permute-start(bf16[1536,768]{1,0:T(8,128)(2,1)} %constant_dynamic-update-slice_fusion), channel_id=1, source_target_pairs={{0,8},{1,9},{2,10},{3,11},{4,12},{5,13},{6,14},{7,15},{8,0},{9,1},... | collective-permute-start | bytes 7077896 | tf_op jit(solution)/shard_map/ppermute | solution.py:27
  111.8 7.5 %collective-permute-start.17 = (bf16[2048,512]{1,0:T(8,128)(2,1)}, bf16[2048,512]{1,0:T(8,128)(2,1)}, u32[]{:S(2)}, u32[]{:S(2)}) collective-permute-start(bf16[2048,512]{1,0:T(8,128)(2,1)} %constant_dynamic-update-slice_fusion.13.mine), channel_id=1, source_target_pairs={{0,8},{1,9},{2,10},{3,11},{4,12},{5,13},{6,14},{7,15},{8,0},{9,1},... | collective-permute-start | bytes 6291464 | tf_op jit(solution)/shard_map/ppermute | solution.py:27
  115.1 2.1 %copy-start.1 = (bf16[512,1536]{1,0:T(8,128)(2,1)S(1)}, bf16[512,1536]{1,0:T(8,128)(2,1)}, u32[]{:S(2)}) copy-start(bf16[512,1536]{1,0:T(8,128)(2,1)} %grads.3) | copy-start | bytes 4718596
  119.3 1.0 copy-start.8
  126.1 3.6 %copy-start.3 = (bf16[384,768]{1,0:T(8,128)(2,1)S(1)}, bf16[384,768]{1,0:T(8,128)(2,1)}, u32[]{:S(2)}) copy-start(bf16[384,768]{1,0:T(8,128)(2,1)} %copy-done.2) | copy-start | bytes 1769476
  126.1 3.6 %copy-start.5 = (bf16[384,768]{1,0:T(8,128)(2,1)S(1)}, bf16[384,768]{1,0:T(8,128)(2,1)}, u32[]{:S(2)}) copy-start(bf16[384,768]{1,0:T(8,128)(2,1)} %copy-done.4) | copy-start | bytes 1769476
  126.1 3.6 %copy-start.7 = (bf16[384,768]{1,0:T(8,128)(2,1)S(1)}, bf16[384,768]{1,0:T(8,128)(2,1)}, u32[]{:S(2)}) copy-start(bf16[384,768]{1,0:T(8,128)(2,1)} %copy-done.6) | copy-start | bytes 1769476
  127.7 5.7 %collective-permute-start.18 = (f32[768,512]{1,0:T(8,128)S(1)}, f32[768,512]{1,0:T(8,128)S(1)}, u32[]{:S(2)}, u32[]{:S(2)}) collective-permute-start(f32[768,512]{1,0:T(8,128)S(1)} %shard_map.57), channel_id=1, source_target_pairs={{0,8},{1,9},{2,10},{3,11},{4,12},{5,13},{6,14},{7,15},{8,0},{9,1},... | collective-permute-start | bytes 4718600 | tf_op jit(solution)/shard_map/ppermute | solution.py:27
Sparse Core Ops, SparseCore 0:
  9.4 81.6 all-gather.1

commit v2 on v1

--- a/solution.py
+++ b/solution.py
@@ -75,37 +75,51 @@
     )(pos, grads, *pieces)
 
 
-def rotate_in_kernel(pos, acts, mask, mine, other, out):
-    z, core = pos[0], pos[3]
-    chunk = mine.shape[0] // NZ
-    half = out.shape[0] // 2
-    for part in range(2):
-        rows = slice(part * half, (part + 1) * half)
-        total = jnp.zeros((half, out.shape[1]), F32)
-        for r in range(NZ):
-            plane = lax.rem(z - r + NZ, NZ) * (2 * chunk)
-            for ref, c in ((mine, core), (other, 1 - core)):
-                at = pl.multiple_of(plane + c * chunk, chunk)
-                total += jnp.dot(
-                    acts[rows, pl.ds(at, chunk)],
-                    ref[r * chunk : (r + 1) * chunk, :],
-                    preferred_element_type=F32,
-                )
-        kept = total.astype(BF16).astype(F32) * mask[rows, :]
-        out[rows, :] = kept.astype(BF16)
-
-
-def rotate_in(pos, acts, mask, mine, other):
-    tokens, depth = acts.shape
+def arrange_kernel(pos, *refs):
+    pieces, out = refs[:NX], refs[NX]
+    x = pos[2]
+    half = out.shape[2] // NX
+    for d in range(NX):
+        at = pl.multiple_of(lax.rem(x - d + NX, NX) * half, half)
+        for c in range(NC):
+            out[c, :, pl.ds(at, half)] = pieces[d][:, c * half : (c + 1) * half]
+
+
+def arrange(pos, pieces):
+    tokens, width = pieces[0].shape
+    return call(
+        arrange_kernel,
+        jax.ShapeDtypeStruct((NC, tokens, NX * width // NC), BF16),
+        [],
+        0,
+        4 * tokens * NX * width,
+        NX,
+    )(pos, *pieces)
+
+
+def partial_kernel(flip, pos, acts, mine, other, out):
+    core = pos[3]
+    depth = acts.shape[2]
+    rows = pl.ds(pl.multiple_of(lax.rem(pos[1] + flip, NYL) * depth, depth), depth)
+    width = 256
+    for j in range(out.shape[1] // width):
+        cols = slice(j * width, (j + 1) * width)
+        out[:, cols] = jnp.dot(acts[core], mine[rows, cols], preferred_element_type=F32) + jnp.dot(
+            acts[1 - core], other[rows, cols], preferred_element_type=F32
+        )
+
+
+def partial(flip, pos, acts, mine, other):
+    tokens, depth = acts.shape[1], NC * acts.shape[2]
     width = mine.shape[1]
     return call(
-        rotate_in_kernel,
-        jax.ShapeDtypeStruct((tokens, width), BF16),
+        functools.partial(partial_kernel, flip),
+        jax.ShapeDtypeStruct((tokens, width), F32),
         [],
         2 * tokens * depth * width,
-        2 * (tokens * depth + depth * width + tokens * width),
-        4,
-    )(pos, acts, mask, mine, other)
+        2 * (tokens * depth + depth * width) + 4 * tokens * width,
+        3,
+    )(pos, acts, mine, other)
 
 
 def squares_kernel(pos, outs, ins, out):
@@ -134,43 +148,54 @@
     )(pos, outs, ins)
 
 
-def gather_in_basis(in_basis, z, yh):
+def place_in_basis(in_basis, yh):
     rows = in_basis.shape[0]
 
     def to(j):
         def target(z, yh, c, yl, x):
             i = (yh % 2) * 2 + c
-            return z, i - j, yh // 2, yl, x
+            return yl * (NZ // 2) + z % (NZ // 2), i - j, yh // 2, z // (NZ // 2), x
 
         return target
 
     got = [send(in_basis, to(j)) for j in range(NYH)]
-    chunk = lax.dynamic_slice_in_dim(
+    return lax.dynamic_slice_in_dim(
         jnp.concatenate(got + got, axis=0), lax.rem(NYH - yh, NYH) * rows, NYH * rows, 0
     )
-    up = lambda z, yh, c, yl, x: (z + 1, yh, c, yl, x)
-    down = lambda z, yh, c, yl, x: (z - 1, yh, c, yl, x)
-    from_below, from_above = [chunk], [chunk]
-    for _ in range(3):
-        from_below.append(send(from_below[-1], up))
-        from_above.append(send(from_above[-1], down))
-    half = chunk.shape[0] // 2
-    far = [send(from_below[-1][:half], up), send(from_above[-1][half:], down)]
-    return jnp.concatenate(from_below + far + from_above[:0:-1], axis=0)
-
-
-def gather_out_basis(out_basis, core):
+
+
+def gather_in_basis(chunk):
+    groups = [[z * NYH * NC + r for z in range(NZ)] for r in range(NYH * NC)]
+    return lax.all_gather(chunk, "wide", axis=0, tiled=True, axis_index_groups=groups)
+
+
+def along_x(value):
+    pieces = [value]
+    for d in range(1, NX):
+        pieces.append(send(value, functools.partial(lambda d, z, yh, c, yl, x: (z, yh, c, yl, x + d), d)))
+    return pieces
+
+
+def power_of(top):
+    return jnp.maximum(jnp.floor(jnp.log2(jnp.maximum(top, 1e-30))), -100.0)
+
+
+def swap_partial(value):
+    power = power_of(jnp.max(jnp.abs(value)))
+    coded = (value * jnp.exp2(14.0 - power)).astype(F16)
+    label = jnp.broadcast_to(power.astype(F16), (8, value.shape[1]))
+    got = send(jnp.concatenate([coded, label], axis=0), lambda z, yh, c, yl, x: (z, yh, c, yl + 1, x))
+    return got[:-8].astype(F32) * jnp.exp2(got[-8:-7, :1].astype(F32) - 14.0)
+
+
+def pair_out_basis(out_basis, core):
     width = out_basis.shape[1]
     own = width // (NZ * NYH * NC)
     source = lax.broadcasted_iota(jnp.int32, (width, width // NC), 0)
     place = lax.broadcasted_iota(jnp.int32, (width, width // NC), 1)
     wanted = ((place // own) * NC + core) * own + place % own
     picked = jnp.dot(out_basis, (source == wanted).astype(BF16), preferred_element_type=F32).astype(BF16)
-    pair = jnp.concatenate([picked, send(picked, lambda z, yh, c, yl, x: (z, yh, c, yl + 1, x))], axis=0)
-    pieces = [pair]
-    for d in range(1, NX):
-        pieces.append(send(pair, functools.partial(lambda d, z, yh, c, yl, x: (z, yh, c, yl, x + d), d)))
-    return pieces
+    return jnp.concatenate([picked, send(picked, lambda z, yh, c, yl, x: (z, yh, c, yl + 1, x))], axis=0)
 
 
 def scatter_sum(total):
@@ -178,8 +203,7 @@
     groups = [[zy * NC + c for zy in range(blocks)] for c in range(NC)]
     rows, columns = total.shape[0] // blocks, total.shape[1]
     tiles = (rows // 8, columns // 128)
-    top = jnp.max(total)
-    power = jnp.maximum(jnp.floor(jnp.log2(jnp.maximum(top, 1e-30))), -100.0)
+    power = power_of(jnp.max(total))
     coded = (total * jnp.exp2(14.0 - power)).astype(F16)
     coded = coded.reshape(blocks, tiles[0], 8, tiles[1], 128).transpose(0, 1, 3, 2, 4).reshape(blocks, -1, 128)
     label = jnp.broadcast_to(power.astype(F16), (blocks, 8, 128))
@@ -198,15 +222,21 @@
     pos = jnp.stack([z, yl, x, core]).astype(jnp.int32)
     sequences = activations.shape[0] // SEQ * lax.axis_size("wide")
 
-    acts = lax.all_gather(activations, "narrow", axis=1, tiled=True)
-    mine = gather_in_basis(in_basis, z, yh)
+    chunk = place_in_basis(in_basis, yh)
+    pair = pair_out_basis(out_basis, core)
+    activations, chunk, pair = lax.optimization_barrier((activations, chunk, pair))
+    mine = gather_in_basis(chunk)
+    acts_pieces = along_x(activations)
+    *acts_pieces, pair = lax.optimization_barrier((*acts_pieces, pair))
+    acts = arrange(pos, acts_pieces)
+    pieces = along_x(pair)
+    mine, *pieces = lax.optimization_barrier((mine, *pieces))
     other = other_core(mine)
-    pieces = gather_out_basis(out_basis, core)
-    pieces_other = [other_core(piece) for piece in [jnp.concatenate(pieces, axis=0)]][0]
-    pieces_other = jnp.split(pieces_other, NX, axis=0)
-
-    mask = valid.astype(F32)[:, None]
-    masked_in = rotate_in(pos, acts, mask, mine, other)
+    pieces_other = jnp.split(other_core(jnp.concatenate(pieces, axis=0)), NX, axis=0)
+
+    theirs = swap_partial(partial(1, pos, acts, mine, other))
+    rotated_in = (partial(0, pos, acts, mine, other) + theirs).astype(BF16)
+    masked_in = rotated_in * valid.astype(BF16)[:, None]
     out_other = rotate_out(pos, out_grads, pieces_other)
     out_mine = rotate_out(pos, out_grads, pieces)
     total = other_core(squares(pos, out_other, masked_in)) + squares(pos, out_mine, masked_in)

time: 183 us -> 204 us (1.11)
  waiting for transfers between devices: 26.1 us -> 57.2 us
  starting transfers between devices: 71.2 us -> 60 us
  other arithmetic: 2.28 us -> 6.26 us
  blocking collectives: 38.5 us -> 35.1 us
    ppermute x19 -> x15, waiting for transfers between devices: 25.3 us -> 57.1 us  [send(): return lax.ppermute(value, BOTH, pairs)]
    ppermute x19 -> x15, starting transfers between devices: 71.2 us -> 60 us  [send(): return lax.ppermute(value, BOTH, pairs)]
    all_to_all x1, blocking collectives: 38.5 us -> 35.1 us  [scatter_sum(): lax.all_to_all(jnp.concatenate([coded, label], axis=1), 'wide', 0, 0, til...]
    pallas_call x1 -> x3, Pallas kernels: 5.82 us -> 6.52 us  [the longest x2 5.7 us: partial(): call(functools.partial(partial_kernel, flip), jax.ShapeDtypeStruct((token...]
    unnamed x39 -> x48, local copies, waits for them, and re-layouts: 9.65 us -> 9.48 us
  transfers between devices with their start and end apart: 20 -> 16, of which waited for: 3 -> 8; matrix products, arithmetic and copies ran while one was open for 8% -> 4% of each run, Pallas kernels for 3% -> 6%
where the time goes in v2:
time: 204 us; the launch traced here: 203 us
  starting transfers between devices  60 us (29%)
  waiting for transfers between devices  57.2 us (28%)
  blocking collectives  35.1 us (17%)
  between operations  16.2 us (8%)
  Pallas kernels  13.9 us (7%)
  local copies, waits for them, and re-layouts  12.9 us (6%)
  other arithmetic  6.26 us (3%)
    ppermute x15, starting transfers between devices, send(): return lax.ppermute(value, BOTH, pairs)  60 us
    ppermute x15, waiting for transfers between devices, send(): return lax.ppermute(value, BOTH, pairs)  57.1 us
    all_to_all x1, blocking collectives, scatter_sum(): lax.all_to_all(jnp.concatenate([coded, label], axis=1), 'wide', 0, 0, til...  35.1 us
    unnamed x48, local copies, waits for them, and re-layouts  9.48 us
    pallas_call x2, Pallas kernels, partial(): call(functools.partial(partial_kernel, flip), jax.ShapeDtypeStruct((token...  5.7 us
    pallas_call x2, Pallas kernels, rotate_out(): call(rotate_out_kernel, jax.ShapeDtypeStruct((tokens, width), BF16), [plt...  4.18 us
  transfers between devices with their start and end apart: 16, of which 8 were waited for; matrix products, arithmetic and copies ran while one was open for 4% of the time, Pallas kernels for 6%

profile of v2, /device:TPU:8, one launch (start us, length us, event | category | flops | bytes accessed | tf_op | source)
XLA Modules:
  0.0 202.6 jit_solution(1065677269314735490)
XLA Ops:
  6.5 10.9 %collective-permute-start = (bf16[64,512]{1,0:T(8,128)(2,1)}, bf16[64,512]{1,0:T(8,128)(2,1)S(1)}, u32[]{:S(2)}, u32[]{:S(2)}) collective-permute-start(bf16[64,512]{1,0:T(8,128)(2,1)} %param.7), channel_id=1, source_target_pairs={{0,0},{1,1},{2,2},{3,3},{4,256},{5,257},{6,258},{7,259},{8,16},{9,... | collective-permute-start | bytes 196616 | tf_op jit(solution)/shard_map/ppermute | solution.py:27
  17.5 5.6 %collective-permute-start.1 = (bf16[64,512]{1,0:T(8,128)(2,1)}, bf16[64,512]{1,0:T(8,128)(2,1)S(1)}, u32[]{:S(2)}, u32[]{:S(2)}) collective-permute-start(bf16[64,512]{1,0:T(8,128)(2,1)} %param.7), channel_id=1, source_target_pairs={{0,48},{1,49},{2,50},{3,51},{4,304},{5,305},{6,306},{7,307},{8,0},... | collective-permute-start | bytes 196616 | tf_op jit(solution)/shard_map/ppermute | solution.py:27
  23.1 8.8 %collective-permute-start.2 = (bf16[64,512]{1,0:T(8,128)(2,1)}, bf16[64,512]{1,0:T(8,128)(2,1)S(1)}, u32[]{:S(2)}, u32[]{:S(2)}) collective-permute-start(bf16[64,512]{1,0:T(8,128)(2,1)} %param.7), channel_id=1, source_target_pairs={{0,32},{1,33},{2,34},{3,35},{4,288},{5,289},{6,290},{7,291},{8,48}... | collective-permute-start | bytes 196616 | tf_op jit(solution)/shard_map/ppermute | solution.py:27
  31.9 1.9 collective-permute-start.3
  33.9 1.1 fusion.11
  35.0 0.0 copy-start.11
  35.0 2.1 %collective-permute-start.4 = (bf16[192,768]{1,0:T(8,128)(2,1)S(1)}, bf16[192,768]{1,0:T(8,128)(2,1)S(1)}, u32[]{:S(2)}, u32[]{:S(2)}) collective-permute-start(bf16[192,768]{1,0:T(8,128)(2,1)S(1)} %fusion.11), channel_id=1, source_target_pairs={{0,4},{1,5},{2,6},{3,7},{4,0},{5,1},{6,2},{7,3},{8,12},{9,13},{10,... | collective-permute-start | bytes 884744 | tf_op jit(solution)/shard_map/ppermute | solution.py:27
  37.1 0.0 collective-permute-done
  37.2 6.0 %collective-permute-done.3 = bf16[64,512]{1,0:T(8,128)(2,1)S(1)} collective-permute-done((bf16[64,512]{1,0:T(8,128)(2,1)}, bf16[64,512]{1,0:T(8,128)(2,1)S(1)}, u32[]{:S(2)}, u32[]{:S(2)}) %collective-permute-start.3) | collective-permute-done | bytes 65568 | tf_op jit(solution)/shard_map/ppermute | solution.py:27
  43.2 0.7 constant_dynamic-slice_fusion
  44.0 1.1 collective-permute-done.4
  45.1 0.0 all-gather.2.cloned.1.call-update
  45.1 3.4 %collective-permute-start.5 = (bf16[512,512]{1,0:T(8,128)(2,1)S(1)}, bf16[512,512]{1,0:T(8,128)(2,1)S(1)}, u32[]{:S(2)}, u32[]{:S(2)}) collective-permute-start(bf16[512,512]{1,0:T(8,128)(2,1)S(1)} %copy-done.11), channel_id=1, source_target_pairs={{0,1},{1,2},{2,3},{3,0},{4,5},{5,6},{6,7},{7,4},{8,9},{9,10},{10,1... | collective-permute-start | bytes 1572872 | tf_op jit(solution)/shard_map/ppermute | solution.py:27
  48.5 4.6 %collective-permute-start.6 = (bf16[512,512]{1,0:T(8,128)(2,1)S(1)}, bf16[512,512]{1,0:T(8,128)(2,1)S(1)}, u32[]{:S(2)}, u32[]{:S(2)}) collective-permute-start(bf16[512,512]{1,0:T(8,128)(2,1)S(1)} %copy-done.11), channel_id=1, source_target_pairs={{0,2},{1,3},{2,0},{3,1},{4,6},{5,7},{6,4},{7,5},{8,10},{9,11},{10,... | collective-permute-start | bytes 1572872 | tf_op jit(solution)/shard_map/ppermute | solution.py:27
  53.1 3.3 %collective-permute-start.7 = (bf16[512,512]{1,0:T(8,128)(2,1)S(1)}, bf16[512,512]{1,0:T(8,128)(2,1)S(1)}, u32[]{:S(2)}, u32[]{:S(2)}) collective-permute-start(bf16[512,512]{1,0:T(8,128)(2,1)S(1)} %copy-done.11), channel_id=1, source_target_pairs={{0,3},{1,0},{2,1},{3,2},{4,7},{5,4},{6,5},{7,6},{8,11},{9,8},{10,9... | collective-permute-start | bytes 1572872 | tf_op jit(solution)/shard_map/ppermute | solution.py:27
  56.5 3.1 %collective-permute-done.5.refs_1_ = bf16[512,512]{1,0:T(8,128)(2,1)S(1)} collective-permute-done((bf16[512,512]{1,0:T(8,128)(2,1)S(1)}, bf16[512,512]{1,0:T(8,128)(2,1)S(1)}, u32[]{:S(2)}, u32[]{:S(2)}) %collective-permute-start.5) | collective-permute-done | bytes 524320 | tf_op jit(solution)/shard_map/ppermute | solution.py:27
  59.6 0.8 copy-done.13
  60.4 11.4 %collective-permute-done.6.refs_2_ = bf16[512,512]{1,0:T(8,128)(2,1)S(1)} collective-permute-done((bf16[512,512]{1,0:T(8,128)(2,1)S(1)}, bf16[512,512]{1,0:T(8,128)(2,1)S(1)}, u32[]{:S(2)}, u32[]{:S(2)}) %collective-permute-start.6) | collective-permute-done | bytes 524320 | tf_op jit(solution)/shard_map/ppermute | solution.py:27
  71.9 0.8 copy-done.15
  72.6 3.3 %collective-permute-done.7.refs_3_ = bf16[512,512]{1,0:T(8,128)(2,1)S(1)} collective-permute-done((bf16[512,512]{1,0:T(8,128)(2,1)S(1)}, bf16[512,512]{1,0:T(8,128)(2,1)S(1)}, u32[]{:S(2)}, u32[]{:S(2)}) %collective-permute-start.7) | collective-permute-done | bytes 524320 | tf_op jit(solution)/shard_map/ppermute | solution.py:27
  75.9 0.8 copy-done.17
  76.7 5.6 %collective-permute-start.10 = (bf16[384,768]{1,0:T(8,128)(2,1)S(1)}, bf16[384,768]{1,0:T(8,128)(2,1)S(1)}, u32[]{:S(2)}, u32[]{:S(2)}) collective-permute-start(bf16[384,768]{1,0:T(8,128)(2,1)S(1)} %pad_maximum_fusion.1.refs_0_), channel_id=1, source_target_pairs={{0,3},{1,0},{2,1},{3,2},{4,7},{5,4},{6,5},{7,6},{8,11},{9,8},{10,9... | collective-permute-start | bytes 1769480 | tf_op jit(solution)/shard_map/ppermute | solution.py:27
  82.3 1.9 collective-permute-start.8
  84.2 3.7 %collective-permute-start.9 = (bf16[384,768]{1,0:T(8,128)(2,1)S(1)}, bf16[384,768]{1,0:T(8,128)(2,1)S(1)}, u32[]{:S(2)}, u32[]{:S(2)}) collective-permute-start(bf16[384,768]{1,0:T(8,128)(2,1)S(1)} %pad_maximum_fusion.1.refs_0_), channel_id=1, source_target_pairs={{0,2},{1,3},{2,0},{3,1},{4,6},{5,7},{6,4},{7,5},{8,10},{9,11},{10,... | collective-permute-start | bytes 1769480 | tf_op jit(solution)/shard_map/ppermute | solution.py:27
  87.9 20.1 %collective-permute-done.10.refs_3_ = bf16[384,768]{1,0:T(8,128)(2,1)S(1)} collective-permute-done((bf16[384,768]{1,0:T(8,128)(2,1)S(1)}, bf16[384,768]{1,0:T(8,128)(2,1)S(1)}, u32[]{:S(2)}, u32[]{:S(2)}) %collective-permute-start.10) | collective-permute-done | bytes 589856 | tf_op jit(solution)/shard_map/ppermute | solution.py:27
  108.0 5.3 %collective-permute-done.8.refs_1_ = bf16[384,768]{1,0:T(8,128)(2,1)S(1)} collective-permute-done((bf16[384,768]{1,0:T(8,128)(2,1)S(1)}, bf16[384,768]{1,0:T(8,128)(2,1)S(1)}, u32[]{:S(2)}, u32[]{:S(2)}) %collective-permute-start.8) | collective-permute-done | bytes 589856 | tf_op jit(solution)/shard_map/ppermute | solution.py:27
  113.3 0.0 all-gather.2.cloned.1.call-done.mine
  113.3 1.9 collective-permute-start.12
  115.3 1.6 pad_maximum_fusion
  116.8 2.4 %collective-permute-start.11 = (bf16[1536,768]{1,0:T(8,128)(2,1)}, bf16[1536,768]{1,0:T(8,128)(2,1)}, u32[]{:S(2)}, u32[]{:S(2)}) collective-permute-start(bf16[1536,768]{1,0:T(8,128)(2,1)} %pad_maximum_fusion), channel_id=1, source_target_pairs={{0,8},{1,9},{2,10},{3,11},{4,12},{5,13},{6,14},{7,15},{8,0},{9,1},... | collective-permute-start | bytes 7077896 | tf_op jit(solution)/shard_map/ppermute | solution.py:27
  119.3 0.1 pad_add_fusion.pos
  119.4 1.0 copy-done.12
  120.4 1.0 copy-done.14
  121.5 1.0 copy-done.16
  122.5 1.0 copy-done.18
  123.5 0.8 shard_map.56.acts
  124.4 1.6 copy-done.2
  126.0 2.8 %shard_map.58 = f32[512,512]{1,0:T(8,128)S(1)} custom-call(s32[4]{0:T(128)S(1)} %pad_add_fusion.pos, bf16[2,512,1024]{2,1,0:T(8,128)(2,1)S(1)} %shard_map.56.acts, bf16[2048,512]{1,0:T(8,128)(2,1)S(1)} %copy-done.2, bf16[2048,512]{1,0:T(8,128)(2,1)} %collective-permute-done.12.other), custom_call_target="tpu_custom_call" | custom-call | flops 1073741824 | bytes 5242880 | tf_op jit(solution)/shard_map/pallas_call | solution.py:115
  128.8 1.0 copy-done.1
  129.8 0.7 abs_reduce_fusion
  131.2 1.5 multiply_convert_fusion.1
  132.7 0.1 concatenate.18
  132.8 1.9 collective-permute-start.13
  134.8 2.9 %shard_map.57 = f32[512,512]{1,0:T(8,128)S(1)} custom-call(s32[4]{0:T(128)S(1)} %pad_add_fusion.pos, bf16[2,512,1024]{2,1,0:T(8,128)(2,1)S(1)} %shard_map.56.acts, bf16[2048,512]{1,0:T(8,128)(2,1)S(1)} %copy-done.3, bf16[2048,512]{1,0:T(8,128)(2,1)} %collective-permute-done.12.other), custom_call_target="tpu_custom_call" | custom-call | flops 1073741824 | bytes 5242880 | tf_op jit(solution)/shard_map/pallas_call | solution.py:115
  137.7 0.0 copy-start.4
  137.7 0.0 collective-permute-done.11
  137.7 1.9 fusion.22
  139.6 0.2 copy-done.4
  139.8 2.1 %shard_map.55.outs = bf16[512,768]{1,0:T(8,128)(2,1)S(1)} custom-call(s32[4]{0:T(128)S(1)} %pad_add_fusion.pos, bf16[512,1536]{1,0:T(8,128)(2,1)S(1)} %copy-done.4, bf16[384,768]{1,0:T(8,128)(2,1)S(1)} %get-tuple-element.36.refs_0_, bf16[384,768]{1,0:T(8,128)(2,1)S(1)} %get-tuple-element.35.refs_1_, bf16[384,768]{1,0:T(8,128)(2,1)S(1)} %get-tuple-element.34.refs_2_, ...), custom_call_target="tpu_custom_call" | custom-call | flops 1207959552 | bytes 4718592 | tf_op jit(solution)/shard_map/pallas_call | solution.py:68
  141.9 6.9 %collective-permute-done.13 = f16[520,512]{1,0:T(8,128)(2,1)S(1)} collective-permute-done((f16[520,512]{1,0:T(8,128)(2,1)S(1)}, f16[520,512]{1,0:T(8,128)(2,1)S(1)}, u32[]{:S(2)}, u32[]{:S(2)}) %collective-permute-start.13) | collective-permute-done | bytes 532512 | tf_op jit(solution)/shard_map/ppermute | solution.py:27
  148.8 0.5 slice.17
  150.0 0.2 fusion.12.ins
  150.2 1.6 shard_map.59
  151.8 1.9 collective-permute-start.14
  153.8 2.1 %shard_map.60.outs = bf16[512,768]{1,0:T(8,128)(2,1)S(1)} custom-call(s32[4]{0:T(128)S(1)} %pad_add_fusion.pos, bf16[512,1536]{1,0:T(8,128)(2,1)S(1)} %copy-done.4, bf16[384,768]{1,0:T(8,128)(2,1)S(1)} %pad_maximum_fusion.1.refs_0_, bf16[384,768]{1,0:T(8,128)(2,1)S(1)} %copy-done.8, bf16[384,768]{1,0:T(8,128)(2,1)S(1)} %copy-done.10, ...), custom_call_target="tpu_custom_call" | custom-call | flops 1207959552 | bytes 4718592 | tf_op jit(solution)/shard_map/pallas_call | solution.py:68
  155.9 1.6 shard_map.61
  157.5 0.0 collective-permute-done.14
  157.5 1.1 fusion.21
  159.3 0.2 multiply_convert_fusion
  159.5 0.2 concatenate.19
  159.7 35.1 %all_to_all.5 = f16[32,104,128]{2,1,0:T(8,128)(2,1)S(1)} all-to-all(f16[32,104,128]{2,1,0:T(8,128)(2,1)S(1)} %concatenate.19), channel_id=1, replica_groups={{0,16,32,48,64,80,96,112,128,144,160,176,192,208,224,240,256,272,288,30..., dimensions={0} | all-to-all | bytes 1703936 | tf_op jit(solution)/shard_map/all_to_all | solution.py:210
  194.8 0.1 copy.8
  194.9 0.2 multiply_reduce_fusion
  195.2 0.6 broadcast_multiply_fusion
  (48 shorter events, 0.2 us)
Async XLA Ops:
  6.5 27.3 %copy-start = (bf16[192,1536]{1,0:T(8,128)(2,1)S(1)}, bf16[192,1536]{1,0:T(8,128)(2,1)}, u32[]{:S(2)}) copy-start(bf16[192,1536]{1,0:T(8,128)(2,1)} %param.8) | copy-start | bytes 1769476
  6.5 106.8 %all-gather.2.cloned.1.call-start = ((), (), s32[]{:S(2)}) async-start(), calls=%async_computation.1 | async-start | bytes 2359296 | tf_op jit(solution)/shard_map/all_gather | solution.py:169
  6.5 30.6 %collective-permute-start = (bf16[64,512]{1,0:T(8,128)(2,1)}, bf16[64,512]{1,0:T(8,128)(2,1)S(1)}, u32[]{:S(2)}, u32[]{:S(2)}) collective-permute-start(bf16[64,512]{1,0:T(8,128)(2,1)} %param.7), channel_id=1, source_target_pairs={{0,0},{1,1},{2,2},{3,3},{4,256},{5,257},{6,258},{7,259},{8,16},{9,... | collective-permute-start | bytes 196616 | tf_op jit(solution)/shard_map/ppermute | solution.py:27
  17.5 19.6 %collective-permute-start.1 = (bf16[64,512]{1,0:T(8,128)(2,1)}, bf16[64,512]{1,0:T(8,128)(2,1)S(1)}, u32[]{:S(2)}, u32[]{:S(2)}) collective-permute-start(bf16[64,512]{1,0:T(8,128)(2,1)} %param.7), channel_id=1, source_target_pairs={{0,48},{1,49},{2,50},{3,51},{4,304},{5,305},{6,306},{7,307},{8,0},... | collective-permute-start | bytes 196616 | tf_op jit(solution)/shard_map/ppermute | solution.py:27
  23.1 14.1 %collective-permute-start.2 = (bf16[64,512]{1,0:T(8,128)(2,1)}, bf16[64,512]{1,0:T(8,128)(2,1)S(1)}, u32[]{:S(2)}, u32[]{:S(2)}) collective-permute-start(bf16[64,512]{1,0:T(8,128)(2,1)} %param.7), channel_id=1, source_target_pairs={{0,32},{1,33},{2,34},{3,35},{4,288},{5,289},{6,290},{7,291},{8,48}... | collective-permute-start | bytes 196616 | tf_op jit(solution)/shard_map/ppermute | solution.py:27
  31.9 11.3 %collective-permute-start.3 = (bf16[64,512]{1,0:T(8,128)(2,1)}, bf16[64,512]{1,0:T(8,128)(2,1)S(1)}, u32[]{:S(2)}, u32[]{:S(2)}) collective-permute-start(bf16[64,512]{1,0:T(8,128)(2,1)} %param.7), channel_id=1, source_target_pairs={{0,16},{1,17},{2,18},{3,19},{4,272},{5,273},{6,274},{7,275},{8,32}... | collective-permute-start | bytes 196616 | tf_op jit(solution)/shard_map/ppermute | solution.py:27
  35.0 10.1 %copy-start.11 = (bf16[512,512]{1,0:T(8,128)(2,1)S(1)}, bf16[512,512]{1,0:T(8,128)(2,1)}, u32[]{:S(2)}) copy-start(bf16[512,512]{1,0:T(8,128)(2,1)} %refs_0_) | copy-start | bytes 1572868
  35.0 10.0 %collective-permute-start.4 = (bf16[192,768]{1,0:T(8,128)(2,1)S(1)}, bf16[192,768]{1,0:T(8,128)(2,1)S(1)}, u32[]{:S(2)}, u32[]{:S(2)}) collective-permute-start(bf16[192,768]{1,0:T(8,128)(2,1)S(1)} %fusion.11), channel_id=1, source_target_pairs={{0,4},{1,5},{2,6},{3,7},{4,0},{5,1},{6,2},{7,3},{8,12},{9,13},{10,... | collective-permute-start | bytes 884744 | tf_op jit(solution)/shard_map/ppermute | solution.py:27
  45.1 14.5 %collective-permute-start.5 = (bf16[512,512]{1,0:T(8,128)(2,1)S(1)}, bf16[512,512]{1,0:T(8,128)(2,1)S(1)}, u32[]{:S(2)}, u32[]{:S(2)}) collective-permute-start(bf16[512,512]{1,0:T(8,128)(2,1)S(1)} %copy-done.11), channel_id=1, source_target_pairs={{0,1},{1,2},{2,3},{3,0},{4,5},{5,6},{6,7},{7,4},{8,9},{9,10},{10,1... | collective-permute-start | bytes 1572872 | tf_op jit(solution)/shard_map/ppermute | solution.py:27
  48.5 23.4 %collective-permute-start.6 = (bf16[512,512]{1,0:T(8,128)(2,1)S(1)}, bf16[512,512]{1,0:T(8,128)(2,1)S(1)}, u32[]{:S(2)}, u32[]{:S(2)}) collective-permute-start(bf16[512,512]{1,0:T(8,128)(2,1)S(1)} %copy-done.11), channel_id=1, source_target_pairs={{0,2},{1,3},{2,0},{3,1},{4,6},{5,7},{6,4},{7,5},{8,10},{9,11},{10,... | collective-permute-start | bytes 1572872 | tf_op jit(solution)/shard_map/ppermute | solution.py:27
  53.1 22.7 %collective-permute-start.7 = (bf16[512,512]{1,0:T(8,128)(2,1)S(1)}, bf16[512,512]{1,0:T(8,128)(2,1)S(1)}, u32[]{:S(2)}, u32[]{:S(2)}) collective-permute-start(bf16[512,512]{1,0:T(8,128)(2,1)S(1)} %copy-done.11), channel_id=1, source_target_pairs={{0,3},{1,0},{2,1},{3,2},{4,7},{5,4},{6,5},{7,6},{8,11},{9,8},{10,9... | collective-permute-start | bytes 1572872 | tf_op jit(solution)/shard_map/ppermute | solution.py:27
  59.6 0.8 copy-start.13
  71.9 0.8 copy-start.15
  75.9 0.8 copy-start.17
  76.7 31.3 %collective-permute-start.10 = (bf16[384,768]{1,0:T(8,128)(2,1)S(1)}, bf16[384,768]{1,0:T(8,128)(2,1)S(1)}, u32[]{:S(2)}, u32[]{:S(2)}) collective-permute-start(bf16[384,768]{1,0:T(8,128)(2,1)S(1)} %pad_maximum_fusion.1.refs_0_), channel_id=1, source_target_pairs={{0,3},{1,0},{2,1},{3,2},{4,7},{5,4},{6,5},{7,6},{8,11},{9,8},{10,9... | collective-permute-start | bytes 1769480 | tf_op jit(solution)/shard_map/ppermute | solution.py:27
  82.3 31.0 %collective-permute-start.8 = (bf16[384,768]{1,0:T(8,128)(2,1)S(1)}, bf16[384,768]{1,0:T(8,128)(2,1)S(1)}, u32[]{:S(2)}, u32[]{:S(2)}) collective-permute-start(bf16[384,768]{1,0:T(8,128)(2,1)S(1)} %pad_maximum_fusion.1.refs_0_), channel_id=1, source_target_pairs={{0,1},{1,2},{2,3},{3,0},{4,5},{5,6},{6,7},{7,4},{8,9},{9,10},{10,1... | collective-permute-start | bytes 1769480 | tf_op jit(solution)/shard_map/ppermute | solution.py:27
  84.2 29.1 %collective-permute-start.9 = (bf16[384,768]{1,0:T(8,128)(2,1)S(1)}, bf16[384,768]{1,0:T(8,128)(2,1)S(1)}, u32[]{:S(2)}, u32[]{:S(2)}) collective-permute-start(bf16[384,768]{1,0:T(8,128)(2,1)S(1)} %pad_maximum_fusion.1.refs_0_), channel_id=1, source_target_pairs={{0,2},{1,3},{2,0},{3,1},{4,6},{5,7},{6,4},{7,5},{8,10},{9,11},{10,... | collective-permute-start | bytes 1769480 | tf_op jit(solution)/shard_map/ppermute | solution.py:27
  108.0 11.2 %copy-start.5 = (bf16[384,768]{1,0:T(8,128)(2,1)}, bf16[384,768]{1,0:T(8,128)(2,1)S(1)}, u32[]{:S(2)}) copy-start(bf16[384,768]{1,0:T(8,128)(2,1)S(1)} %collective-permute-done.10.refs_3_) | copy-start | bytes 1769476
  113.3 6.0 %copy-start.7 = (bf16[384,768]{1,0:T(8,128)(2,1)}, bf16[384,768]{1,0:T(8,128)(2,1)S(1)}, u32[]{:S(2)}) copy-start(bf16[384,768]{1,0:T(8,128)(2,1)S(1)} %collective-permute-done.8.refs_1_) | copy-start | bytes 1769476
  113.3 6.0 %copy-start.9 = (bf16[384,768]{1,0:T(8,128)(2,1)}, bf16[384,768]{1,0:T(8,128)(2,1)S(1)}, u32[]{:S(2)}) copy-start(bf16[384,768]{1,0:T(8,128)(2,1)S(1)} %collective-permute-done.9.refs_2_) | copy-start | bytes 1769476
  113.3 11.1 %collective-permute-start.12 = (bf16[2048,512]{1,0:T(8,128)(2,1)}, bf16[2048,512]{1,0:T(8,128)(2,1)}, u32[]{:S(2)}, u32[]{:S(2)}) collective-permute-start(bf16[2048,512]{1,0:T(8,128)(2,1)} %all-gather.2.cloned.1.call-done.mine), channel_id=1, source_target_pairs={{0,8},{1,9},{2,10},{3,11},{4,12},{5,13},{6,14},{7,15},{8,0},{9,1},... | collective-permute-start | bytes 6291464 | tf_op jit(solution)/shard_map/ppermute | solution.py:27
  116.8 20.8 %collective-permute-start.11 = (bf16[1536,768]{1,0:T(8,128)(2,1)}, bf16[1536,768]{1,0:T(8,128)(2,1)}, u32[]{:S(2)}, u32[]{:S(2)}) collective-permute-start(bf16[1536,768]{1,0:T(8,128)(2,1)} %pad_maximum_fusion), channel_id=1, source_target_pairs={{0,8},{1,9},{2,10},{3,11},{4,12},{5,13},{6,14},{7,15},{8,0},{9,1},... | collective-permute-start | bytes 7077896 | tf_op jit(solution)/shard_map/ppermute | solution.py:27
  119.4 1.0 copy-start.12
  120.4 1.0 copy-start.14
  121.5 1.0 copy-start.16
  122.5 1.0 copy-start.18
  124.4 1.6 copy-start.2
  128.8 1.0 copy-start.1
  129.8 5.0 %copy-start.19 = (s32[512]{0:T(512)S(1)}, s32[512]{0:T(512)}, u32[]{:S(2)}) copy-start(s32[512]{0:T(512)} %param.9) | copy-start | bytes 6148
  131.2 3.6 %copy-start.3 = (bf16[2048,512]{1,0:T(8,128)(2,1)S(1)}, bf16[2048,512]{1,0:T(8,128)(2,1)}, u32[]{:S(2)}) copy-start(bf16[2048,512]{1,0:T(8,128)(2,1)} %all-gather.2.cloned.1.call-done.mine) | copy-start | bytes 6291460
  132.8 15.9 %collective-permute-start.13 = (f16[520,512]{1,0:T(8,128)(2,1)S(1)}, f16[520,512]{1,0:T(8,128)(2,1)S(1)}, u32[]{:S(2)}, u32[]{:S(2)}) collective-permute-start(f16[520,512]{1,0:T(8,128)(2,1)S(1)} %concatenate.18), channel_id=1, source_target_pairs={{0,4},{1,5},{2,6},{3,7},{4,0},{5,1},{6,2},{7,3},{8,12},{9,13},{10,... | collective-permute-start | bytes 1597448 | tf_op jit(solution)/shard_map/ppermute | solution.py:27
  137.7 2.1 %copy-start.4 = (bf16[512,1536]{1,0:T(8,128)(2,1)S(1)}, bf16[512,1536]{1,0:T(8,128)(2,1)}, u32[]{:S(2)}) copy-start(bf16[512,1536]{1,0:T(8,128)(2,1)} %grads.3) | copy-start | bytes 4718596
  150.0 3.8 %copy-start.6 = (bf16[384,768]{1,0:T(8,128)(2,1)S(1)}, bf16[384,768]{1,0:T(8,128)(2,1)}, u32[]{:S(2)}) copy-start(bf16[384,768]{1,0:T(8,128)(2,1)} %copy-done.5) | copy-start | bytes 1769476
  150.0 3.8 %copy-start.8 = (bf16[384,768]{1,0:T(8,128)(2,1)S(1)}, bf16[384,768]{1,0:T(8,128)(2,1)}, u32[]{:S(2)}) copy-start(bf16[384,768]{1,0:T(8,128)(2,1)} %copy-done.7) | copy-start | bytes 1769476
  150.0 3.8 %copy-start.10 = (bf16[384,768]{1,0:T(8,128)(2,1)S(1)}, bf16[384,768]{1,0:T(8,128)(2,1)}, u32[]{:S(2)}) copy-start(bf16[384,768]{1,0:T(8,128)(2,1)} %copy-done.9) | copy-start | bytes 1769476
  151.8 5.7 %collective-permute-start.14 = (f32[768,512]{1,0:T(8,128)S(1)}, f32[768,512]{1,0:T(8,128)S(1)}, u32[]{:S(2)}, u32[]{:S(2)}) collective-permute-start(f32[768,512]{1,0:T(8,128)S(1)} %shard_map.59), channel_id=1, source_target_pairs={{0,8},{1,9},{2,10},{3,11},{4,12},{5,13},{6,14},{7,15},{8,0},{9,1},... | collective-permute-start | bytes 4718600 | tf_op jit(solution)/shard_map/ppermute | solution.py:27
Sparse Core Ops, SparseCore 0:
  45.2 44.5 all-gather.1

commit v3 on v2

--- a/solution.py
+++ b/solution.py
@@ -47,79 +47,90 @@
     )
 
 
-def rotate_out_kernel(pos, grads, *refs):
-    pieces, out, basis = refs[:NX], refs[NX], refs[NX + 1]
-    rows = pieces[0].shape[0] // NYL
-    yl, x = pos[1], pos[2]
-    for d in range(NX):
-        for flip in range(NYL):
-            owner = lax.rem(yl + flip, NYL) * NX + lax.rem(x - d + NX, NX)
-            at = pl.multiple_of(owner * rows, 64)
-            basis[pl.ds(at, rows), :] = pieces[d][flip * rows : (flip + 1) * rows, :]
+def rotate_out_kernel(pos, grads, own, flipped, out, basis):
+    rows = own.shape[0] // NX
+    for ref, yl in ((own, pos[1]), (flipped, 1 - pos[1])):
+        for d in range(NX):
+            at = pl.multiple_of((yl * NX + lax.rem(pos[2] - d + NX, NX)) * rows, 64)
+            basis[pl.ds(at, rows), :] = ref[d * rows : (d + 1) * rows, :]
     width = 256
     for j in range(out.shape[1] // width):
         cols = slice(j * width, (j + 1) * width)
         out[:, cols] = jnp.dot(grads[...], basis[:, cols], preferred_element_type=F32).astype(out.dtype)
 
 
-def rotate_out(pos, grads, pieces):
+def rotate_out(pos, grads, own, flipped):
     tokens, depth = grads.shape
-    width = pieces[0].shape[1]
+    width = own.shape[1]
     return call(
         rotate_out_kernel,
         jax.ShapeDtypeStruct((tokens, width), BF16),
         [pltpu.VMEM((depth, width), BF16)],
         2 * tokens * depth * width,
         2 * (tokens * depth + depth * width + tokens * width),
-        1 + NX,
-    )(pos, grads, *pieces)
-
-
-def arrange_kernel(pos, *refs):
-    pieces, out = refs[:NX], refs[NX]
-    x = pos[2]
-    half = out.shape[2] // NX
-    for d in range(NX):
-        at = pl.multiple_of(lax.rem(x - d + NX, NX) * half, half)
+        3,
+    )(pos, grads, own, flipped)
+
+
+def arrange_kernel(pos, acts, out):
+    half = acts.shape[1] // (NZ * NC)
+    for z in range(NZ):
         for c in range(NC):
-            out[c, :, pl.ds(at, half)] = pieces[d][:, c * half : (c + 1) * half]
-
-
-def arrange(pos, pieces):
-    tokens, width = pieces[0].shape
+            at = (z * NC + c) * half
+            out[c, :, z * half : (z + 1) * half] = acts[:, at : at + half]
+
+
+def arrange(pos, acts):
+    tokens, depth = acts.shape
     return call(
         arrange_kernel,
-        jax.ShapeDtypeStruct((NC, tokens, NX * width // NC), BF16),
+        jax.ShapeDtypeStruct((NC, tokens, depth // NC), BF16),
         [],
         0,
-        4 * tokens * NX * width,
-        NX,
-    )(pos, *pieces)
-
-
-def partial_kernel(flip, pos, acts, mine, other, out):
-    core = pos[3]
-    depth = acts.shape[2]
-    rows = pl.ds(pl.multiple_of(lax.rem(pos[1] + flip, NYL) * depth, depth), depth)
-    width = 256
+        4 * tokens * depth,
+        1,
+    )(pos, acts)
+
+
+def first_half_kernel(pos, acts, mine, out):
+    core, width = pos[3], 256
     for j in range(out.shape[1] // width):
         cols = slice(j * width, (j + 1) * width)
-        out[:, cols] = jnp.dot(acts[core], mine[rows, cols], preferred_element_type=F32) + jnp.dot(
-            acts[1 - core], other[rows, cols], preferred_element_type=F32
-        )
-
-
-def partial(flip, pos, acts, mine, other):
-    tokens, depth = acts.shape[1], NC * acts.shape[2]
+        out[:, cols] = jnp.dot(acts[core], mine[:, cols], preferred_element_type=F32)
+
+
+def first_half(pos, acts, mine):
+    _, tokens, depth = acts.shape
     width = mine.shape[1]
     return call(
-        functools.partial(partial_kernel, flip),
+        first_half_kernel,
         jax.ShapeDtypeStruct((tokens, width), F32),
         [],
         2 * tokens * depth * width,
         2 * (tokens * depth + depth * width) + 4 * tokens * width,
-        3,
-    )(pos, acts, mine, other)
+        2,
+    )(pos, acts, mine)
+
+
+def masked_kernel(pos, acts, other, first, mask, out):
+    core, width = pos[3], 256
+    for j in range(out.shape[1] // width):
+        cols = slice(j * width, (j + 1) * width)
+        total = first[:, cols] + jnp.dot(acts[1 - core], other[:, cols], preferred_element_type=F32)
+        out[:, cols] = (total.astype(BF16).astype(F32) * mask[...]).astype(BF16)
+
+
+def masked(pos, acts, other, first, mask):
+    _, tokens, depth = acts.shape
+    width = other.shape[1]
+    return call(
+        masked_kernel,
+        jax.ShapeDtypeStruct((tokens, width), BF16),
+        [],
+        2 * tokens * depth * width,
+        2 * (tokens * depth + depth * width) + 6 * tokens * width,
+        4,
+    )(pos, acts, other, first, mask)
 
 
 def squares_kernel(pos, outs, ins, out):
@@ -154,7 +165,7 @@
     def to(j):
         def target(z, yh, c, yl, x):
             i = (yh % 2) * 2 + c
-            return yl * (NZ // 2) + z % (NZ // 2), i - j, yh // 2, z // (NZ // 2), x
+            return z, i - j, yh // 2, yl, x
 
         return target
 
@@ -166,36 +177,35 @@
 
 def gather_in_basis(chunk):
     groups = [[z * NYH * NC + r for z in range(NZ)] for r in range(NYH * NC)]
-    return lax.all_gather(chunk, "wide", axis=0, tiled=True, axis_index_groups=groups)
-
-
-def along_x(value):
+    copies = jnp.concatenate([chunk] * NZ, axis=0)
+    return lax.all_to_all(copies, "wide", 0, 0, tiled=True, axis_index_groups=groups)
+
+
+def from_x(value):
     pieces = [value]
     for d in range(1, NX):
         pieces.append(send(value, functools.partial(lambda d, z, yh, c, yl, x: (z, yh, c, yl, x + d), d)))
     return pieces
 
 
+def other_yl(value):
+    half = value.shape[0] // 2
+    up = lambda z, yh, c, yl, x: (z, yh + yl, c, yl + 1, x)
+    down = lambda z, yh, c, yl, x: (z, yh + yl - 1, c, yl + 1, x)
+    return jnp.concatenate([send(value[:half], up), send(value[half:], down)], axis=0)
+
+
 def power_of(top):
     return jnp.maximum(jnp.floor(jnp.log2(jnp.maximum(top, 1e-30))), -100.0)
 
 
-def swap_partial(value):
-    power = power_of(jnp.max(jnp.abs(value)))
-    coded = (value * jnp.exp2(14.0 - power)).astype(F16)
-    label = jnp.broadcast_to(power.astype(F16), (8, value.shape[1]))
-    got = send(jnp.concatenate([coded, label], axis=0), lambda z, yh, c, yl, x: (z, yh, c, yl + 1, x))
-    return got[:-8].astype(F32) * jnp.exp2(got[-8:-7, :1].astype(F32) - 14.0)
-
-
-def pair_out_basis(out_basis, core):
+def pick(out_basis, core):
     width = out_basis.shape[1]
     own = width // (NZ * NYH * NC)
     source = lax.broadcasted_iota(jnp.int32, (width, width // NC), 0)
     place = lax.broadcasted_iota(jnp.int32, (width, width // NC), 1)
     wanted = ((place // own) * NC + core) * own + place % own
-    picked = jnp.dot(out_basis, (source == wanted).astype(BF16), preferred_element_type=F32).astype(BF16)
-    return jnp.concatenate([picked, send(picked, lambda z, yh, c, yl, x: (z, yh, c, yl + 1, x))], axis=0)
+    return jnp.dot(out_basis, (source == wanted).astype(BF16), preferred_element_type=F32).astype(BF16)
 
 
 def scatter_sum(total):
@@ -222,23 +232,22 @@
     pos = jnp.stack([z, yl, x, core]).astype(jnp.int32)
     sequences = activations.shape[0] // SEQ * lax.axis_size("wide")
 
+    acts = lax.all_gather(activations, "narrow", axis=1, tiled=True)
     chunk = place_in_basis(in_basis, yh)
-    pair = pair_out_basis(out_basis, core)
-    activations, chunk, pair = lax.optimization_barrier((activations, chunk, pair))
     mine = gather_in_basis(chunk)
-    acts_pieces = along_x(activations)
-    *acts_pieces, pair = lax.optimization_barrier((*acts_pieces, pair))
-    acts = arrange(pos, acts_pieces)
-    pieces = along_x(pair)
-    mine, *pieces = lax.optimization_barrier((mine, *pieces))
+    picked, _ = lax.optimization_barrier((pick(out_basis, core), chunk))
+    basis_own = jnp.concatenate(from_x(picked), axis=0)
+    basis_flipped = other_yl(basis_own)
+    basis = jnp.concatenate([basis_own, basis_flipped], axis=0)
+    basis_other = other_core(basis)
+    half = basis.shape[0] // 2
+    out_mine = rotate_out(pos, out_grads, basis_own, basis_flipped)
+    out_other = rotate_out(pos, out_grads, basis_other[:half], basis_other[half:])
+    acts = arrange(pos, acts)
+    mask = valid.astype(F32)[:, None]
+    mine, acts, mask, out_mine, out_other = lax.optimization_barrier((mine, acts, mask, out_mine, out_other))
     other = other_core(mine)
-    pieces_other = jnp.split(other_core(jnp.concatenate(pieces, axis=0)), NX, axis=0)
-
-    theirs = swap_partial(partial(1, pos, acts, mine, other))
-    rotated_in = (partial(0, pos, acts, mine, other) + theirs).astype(BF16)
-    masked_in = rotated_in * valid.astype(BF16)[:, None]
-    out_other = rotate_out(pos, out_grads, pieces_other)
-    out_mine = rotate_out(pos, out_grads, pieces)
+    masked_in = masked(pos, acts, other, first_half(pos, acts, mine), mask)
     total = other_core(squares(pos, out_other, masked_in)) + squares(pos, out_mine, masked_in)
     return scatter_sum(total) / sequences
 

time: 204 us -> 193 us (0.946)
  the two profiles are of different devices: /device:TPU:8 before, /device:TPU:32 now
where the time goes in v3:
time: 193 us; the launch traced here: 192 us
  starting transfers between devices  52 us (27%)
  blocking collectives  44.7 us (23%)
  waiting for transfers between devices  37 us (19%)
  local copies, waits for them, and re-layouts  20.5 us (11%)
  Pallas kernels  17.8 us (9%)
  between operations  14.6 us (8%)
  other arithmetic  4.73 us (2%)
    all_to_all x1, blocking collectives, scatter_sum(): lax.all_to_all(jnp.concatenate([coded, label], axis=1), 'wide', 0, 0, til...  44.7 us
    ppermute x12, starting transfers between devices, send(): return lax.ppermute(value, BOTH, pairs)  40.8 us
    ppermute x12, waiting for transfers between devices, send(): return lax.ppermute(value, BOTH, pairs)  36.3 us
    unnamed x42, local copies, waits for them, and re-layouts  16.1 us
    all_to_all x1, starting transfers between devices, gather_in_basis(): lax.all_to_all(copies, 'wide', 0, 0, tiled=True, axis_index_groups=groups)  11.1 us
    pallas_call x1, Pallas kernels, masked(): call(masked_kernel, jax.ShapeDtypeStruct((tokens, width), BF16), [], 2 *...  4.19 us
    pallas_call x2, Pallas kernels, rotate_out(): call(rotate_out_kernel, jax.ShapeDtypeStruct((tokens, width), BF16), [plt...  4.18 us
  transfers between devices with their start and end apart: 14, of which 8 were waited for; matrix products, arithmetic and copies ran while one was open for 10% of the time, Pallas kernels for 6%

profile of v3, /device:TPU:32, one launch (start us, length us, event | category | flops | bytes accessed | tf_op | source)
XLA Modules:
  0.0 192.4 jit_solution(11263119350506844274)
XLA Ops:
  6.5 0.7 all-gather.2.cloned.1.call-update
  7.3 1.9 collective-permute-start
  9.2 1.9 collective-permute-start.1
  11.1 4.4 %collective-permute-start.2 = (bf16[64,512]{1,0:T(8,128)(2,1)}, bf16[64,512]{1,0:T(8,128)(2,1)S(1)}, u32[]{:S(2)}, u32[]{:S(2)}) collective-permute-start(bf16[64,512]{1,0:T(8,128)(2,1)} %param.7), channel_id=1, source_target_pairs={{0,32},{1,33},{2,34},{3,35},{4,36},{5,37},{6,38},{7,39},{8,48},{9,... | collective-permute-start | bytes 196616 | tf_op jit(solution)/shard_map/ppermute | solution.py:27
  15.5 3.5 %collective-permute-start.3 = (bf16[64,512]{1,0:T(8,128)(2,1)}, bf16[64,512]{1,0:T(8,128)(2,1)S(1)}, u32[]{:S(2)}, u32[]{:S(2)}) collective-permute-start(bf16[64,512]{1,0:T(8,128)(2,1)} %param.7), channel_id=1, source_target_pairs={{0,16},{1,17},{2,18},{3,19},{4,20},{5,21},{6,22},{7,23},{8,32},{9,... | collective-permute-start | bytes 196616 | tf_op jit(solution)/shard_map/ppermute | solution.py:27
  19.1 1.1 fusion.11
  20.3 0.0 collective-permute-done.1
  20.3 1.1 collective-permute-done.2
  21.4 5.8 %collective-permute-done.3 = bf16[64,512]{1,0:T(8,128)(2,1)S(1)} collective-permute-done((bf16[64,512]{1,0:T(8,128)(2,1)}, bf16[64,512]{1,0:T(8,128)(2,1)S(1)}, u32[]{:S(2)}, u32[]{:S(2)}) %collective-permute-start.3) | collective-permute-done | bytes 65568 | tf_op jit(solution)/shard_map/ppermute | solution.py:27
  27.3 0.8 constant_dynamic-update-slice_fusion.15
  28.1 3.4 %collective-permute-start.4 = (bf16[192,768]{1,0:T(8,128)(2,1)S(1)}, bf16[192,768]{1,0:T(8,128)(2,1)S(1)}, u32[]{:S(2)}, u32[]{:S(2)}) collective-permute-start(bf16[192,768]{1,0:T(8,128)(2,1)S(1)} %fusion.11), channel_id=1, source_target_pairs={{0,1},{1,2},{2,3},{3,0},{4,5},{5,6},{6,7},{7,4},{8,9},{9,10},{10,1... | collective-permute-start | bytes 884744 | tf_op jit(solution)/shard_map/ppermute | solution.py:27
  31.5 4.6 %collective-permute-start.5 = (bf16[192,768]{1,0:T(8,128)(2,1)S(1)}, bf16[192,768]{1,0:T(8,128)(2,1)}, u32[]{:S(2)}, u32[]{:S(2)}) collective-permute-start(bf16[192,768]{1,0:T(8,128)(2,1)S(1)} %fusion.11), channel_id=1, source_target_pairs={{0,2},{1,3},{2,0},{3,1},{4,6},{5,7},{6,4},{7,5},{8,10},{9,11},{10,... | collective-permute-start | bytes 884744 | tf_op jit(solution)/shard_map/ppermute | solution.py:27
  36.1 3.3 %collective-permute-start.6 = (bf16[192,768]{1,0:T(8,128)(2,1)S(1)}, bf16[192,768]{1,0:T(8,128)(2,1)}, u32[]{:S(2)}, u32[]{:S(2)}) collective-permute-start(bf16[192,768]{1,0:T(8,128)(2,1)S(1)} %fusion.11), channel_id=1, source_target_pairs={{0,3},{1,0},{2,1},{3,2},{4,7},{5,4},{6,5},{7,6},{8,11},{9,8},{10,9... | collective-permute-start | bytes 884744 | tf_op jit(solution)/shard_map/ppermute | solution.py:27
  39.5 0.7 constant_dynamic-update-slice_fusion.14
  40.2 0.7 constant_dynamic-update-slice_fusion.13
  40.9 0.7 constant_dynamic-update-slice_fusion.12
  41.7 0.7 constant_dynamic-update-slice_fusion.11
  42.4 0.7 constant_dynamic-update-slice_fusion.10
  43.1 0.7 constant_dynamic-update-slice_fusion.9
  43.9 0.7 constant_dynamic-update-slice_fusion.8
  44.6 11.1 %all-to-all-start = ((bf16[8,256,512]{2,1,0:T(8,128)(2,1)}), bf16[8,256,512]{2,1,0:T(8,128)(2,1)S(1)}, u32[]{:S(2)}, u32[]{:S(2)}) async-start(bf16[8,256,512]{2,1,0:T(8,128)(2,1)} %bitcast.4), calls=%async_computation | async-start | bytes 4194304 | tf_op jit(solution)/shard_map/all_to_all | solution.py:181
  55.7 12.9 %collective-permute-done.4 = bf16[192,768]{1,0:T(8,128)(2,1)S(1)} collective-permute-done((bf16[192,768]{1,0:T(8,128)(2,1)S(1)}, bf16[192,768]{1,0:T(8,128)(2,1)S(1)}, u32[]{:S(2)}, u32[]{:S(2)}) %collective-permute-start.4) | collective-permute-done | bytes 294944 | tf_op jit(solution)/shard_map/ppermute | solution.py:27
  68.7 1.9 collective-permute-start.7
  70.6 7.0 %collective-permute-done.6 = bf16[192,768]{1,0:T(8,128)(2,1)} collective-permute-done((bf16[192,768]{1,0:T(8,128)(2,1)S(1)}, bf16[192,768]{1,0:T(8,128)(2,1)}, u32[]{:S(2)}, u32[]{:S(2)}) %collective-permute-start.6) | collective-permute-done | bytes 294944 | tf_op jit(solution)/shard_map/ppermute | solution.py:27
  77.6 1.1 pad_maximum_fusion.3
  78.7 9.6 %collective-permute-start.8 = (bf16[384,768]{1,0:T(8,128)(2,1)S(1)}, bf16[384,768]{1,0:T(8,128)(2,1)S(1)}, u32[]{:S(2)}, u32[]{:S(2)}) collective-permute-start(bf16[384,768]{1,0:T(8,128)(2,1)S(1)} %pad_maximum_fusion.3), channel_id=1, source_target_pairs={{0,52},{1,53},{2,54},{3,55},{4,0},{5,1},{6,2},{7,3},{8,60},{9,61},... | collective-permute-start | bytes 1769480 | tf_op jit(solution)/shard_map/ppermute | solution.py:27
  88.3 0.8 constant_dynamic-update-slice_fusion.21
  89.0 0.7 constant_dynamic-update-slice_fusion.20
  89.8 1.7 constant_dynamic-update-slice_fusion.19
  91.5 1.7 constant_dynamic-update-slice_fusion.18
  93.2 5.6 %collective-permute-done.7 = bf16[384,768]{1,0:T(8,128)(2,1)S(1)} collective-permute-done((bf16[384,768]{1,0:T(8,128)(2,1)S(1)}, bf16[384,768]{1,0:T(8,128)(2,1)S(1)}, u32[]{:S(2)}, u32[]{:S(2)}) %collective-permute-start.7) | collective-permute-done | bytes 589856 | tf_op jit(solution)/shard_map/ppermute | solution.py:27
  98.7 0.8 copy-done.6
  99.6 0.9 constant_dynamic-update-slice_fusion.17
  100.5 1.7 collective-permute-done.8
  102.2 0.8 copy-done.8
  103.0 0.9 constant_dynamic-update-slice_fusion.16
  103.9 1.9 collective-permute-start.9
  105.9 0.1 pad_add_fusion.pos
  106.0 1.3 pad_maximum_fusion.own
  107.3 0.0 copy-done.9
  107.3 0.1 pad_maximum_fusion.1.flipped
  107.4 0.5 copy-done.2
  107.9 2.1 %shard_map.56.outs = bf16[512,768]{1,0:T(8,128)(2,1)S(1)} custom-call(s32[4]{0:T(128)S(1)} %pad_add_fusion.pos, bf16[512,1536]{1,0:T(8,128)(2,1)S(1)} %copy-done.2, bf16[768,768]{1,0:T(8,128)(2,1)S(1)} %pad_maximum_fusion.own, bf16[768,768]{1,0:T(8,128)(2,1)S(1)} %pad_maximum_fusion.1.flipped), custom_call_target="tpu_custom_call" | custom-call | flops 1207959552 | bytes 4718592 | tf_op jit(solution)/shard_map/pallas_call | solution.py:65
  110.0 0.7 collective-permute-done.9
  110.7 1.8 fusion.21
  112.5 2.1 %shard_map.57.outs = bf16[512,768]{1,0:T(8,128)(2,1)S(1)} custom-call(s32[4]{0:T(128)S(1)} %pad_add_fusion.pos, bf16[512,1536]{1,0:T(8,128)(2,1)S(1)} %copy-done.2, bf16[768,768]{1,0:T(8,128)(2,1)S(1)} %get-tuple-element.22.own, bf16[768,768]{1,0:T(8,128)(2,1)S(1)} %get-tuple-element.21.flipped), custom_call_target="tpu_custom_call" | custom-call | flops 1207959552 | bytes 4718592 | tf_op jit(solution)/shard_map/pallas_call | solution.py:65
  114.6 0.9 copy-done.3
  115.4 2.8 %shard_map.55.acts = bf16[2,512,2048]{2,1,0:T(8,128)(2,1)S(1)} custom-call(s32[4]{0:T(128)S(1)} %pad_add_fusion.pos, bf16[512,4096]{1,0:T(8,128)(2,1)} %all-gather.2.cloned.1.call-done.acts), custom_call_target="tpu_custom_call" | custom-call | bytes 8388608 | tf_op jit(solution)/shard_map/pallas_call | solution.py:85
  118.2 1.9 %copy-done.1 = bf16[2,512,2048]{2,1,0:T(8,128)(2,1)} copy-done((bf16[2,512,2048]{2,1,0:T(8,128)(2,1)}, bf16[2,512,2048]{2,1,0:T(8,128)(2,1)S(1)}, u32[]{:S(2)}) %copy-start.1) | copy-done | bytes 4194328
  120.2 2.0 %collective-permute-start.10 = (bf16[2048,512]{1,0:T(8,128)(2,1)S(1)}, bf16[2048,512]{1,0:T(8,128)(2,1)}, u32[]{:S(2)}, u32[]{:S(2)}) collective-permute-start(bf16[2048,512]{1,0:T(8,128)(2,1)S(1)} %bitcast.22), channel_id=1, source_target_pairs={{0,8},{1,9},{2,10},{3,11},{4,12},{5,13},{6,14},{7,15},{8,0},{9,1},... | collective-permute-start | bytes 6291464 | tf_op jit(solution)/shard_map/ppermute | solution.py:27
  122.2 0.8 copy.11.mask
  123.1 3.5 %shard_map.58.first = f32[512,512]{1,0:T(8,128)S(1)} custom-call(s32[4]{0:T(128)S(1)} %pad_add_fusion.pos, bf16[2,512,2048]{2,1,0:T(8,128)(2,1)} %copy-done.1, bf16[2048,512]{1,0:T(8,128)(2,1)S(1)} %bitcast.23), custom_call_target="tpu_custom_call" | custom-call | flops 1073741824 | bytes 5242880 | tf_op jit(solution)/shard_map/pallas_call | solution.py:105
  126.6 4.2 %shard_map.59.ins = bf16[512,512]{1,0:T(8,128)(2,1)S(1)} custom-call(s32[4]{0:T(128)S(1)} %pad_add_fusion.pos, bf16[2,512,2048]{2,1,0:T(8,128)(2,1)} %copy-done.1, bf16[2048,512]{1,0:T(8,128)(2,1)} %collective-permute-done.10.other, f32[512,512]{1,0:T(8,128)S(1)} %shard_map.58.first, f32[512,1]{1,0:T(8,128)S(1)} %copy-done.5), custom_call_target="tpu_custom_call" | custom-call | flops 1073741824 | bytes 5767168 | tf_op jit(solution)/shard_map/pallas_call | solution.py:126
  130.8 1.6 shard_map.60
  132.4 2.3 %collective-permute-start.11 = (f32[768,512]{1,0:T(8,128)S(1)}, f32[768,512]{1,0:T(8,128)S(1)}, u32[]{:S(2)}, u32[]{:S(2)}) collective-permute-start(f32[768,512]{1,0:T(8,128)S(1)} %shard_map.60), channel_id=1, source_target_pairs={{0,8},{1,9},{2,10},{3,11},{4,12},{5,13},{6,14},{7,15},{8,0},{9,1},... | collective-permute-start | bytes 4718600 | tf_op jit(solution)/shard_map/ppermute | solution.py:27
  134.7 1.6 shard_map.61
  136.3 1.4 collective-permute-done.11
  137.7 1.1 fusion.20
  139.5 0.2 multiply_convert_fusion
  139.7 0.2 concatenate.32
  139.9 44.7 %all_to_all.17 = f16[32,104,128]{2,1,0:T(8,128)(2,1)S(1)} all-to-all(f16[32,104,128]{2,1,0:T(8,128)(2,1)S(1)} %concatenate.32), channel_id=1, replica_groups={{0,16,32,48,64,80,96,112,128,144,160,176,192,208,224,240,256,272,288,30..., dimensions={0} | all-to-all | bytes 1703936 | tf_op jit(solution)/shard_map/all_to_all | solution.py:220
  184.6 0.1 copy.13
  184.7 0.2 multiply_reduce_fusion
  184.9 0.6 broadcast_multiply_fusion
  (37 shorter events, 0.2 us)
Async XLA Ops:
  6.5 12.6 %copy-start = (bf16[192,1536]{1,0:T(8,128)(2,1)S(1)}, bf16[192,1536]{1,0:T(8,128)(2,1)}, u32[]{:S(2)}) copy-start(bf16[192,1536]{1,0:T(8,128)(2,1)} %param.8) | copy-start | bytes 1769476
  6.5 108.9 %all-gather.2.cloned.1.call-start = ((), (), s32[]{:S(2)}) async-start(), calls=%async_computation.2 | async-start | bytes 4718592 | tf_op jit(solution)/shard_map/all_gather | solution.py:235
  7.3 13.0 %collective-permute-start = (bf16[64,512]{1,0:T(8,128)(2,1)}, bf16[64,512]{1,0:T(8,128)(2,1)S(1)}, u32[]{:S(2)}, u32[]{:S(2)}) collective-permute-start(bf16[64,512]{1,0:T(8,128)(2,1)} %param.7), channel_id=1, source_target_pairs={{0,0},{1,1},{2,2},{3,3},{4,4},{5,5},{6,6},{7,7},{8,16},{9,17},{10,... | collective-permute-start | bytes 196616 | tf_op jit(solution)/shard_map/ppermute | solution.py:27
  9.2 11.1 %collective-permute-start.1 = (bf16[64,512]{1,0:T(8,128)(2,1)}, bf16[64,512]{1,0:T(8,128)(2,1)S(1)}, u32[]{:S(2)}, u32[]{:S(2)}) collective-permute-start(bf16[64,512]{1,0:T(8,128)(2,1)} %param.7), channel_id=1, source_target_pairs={{0,48},{1,49},{2,50},{3,51},{4,52},{5,53},{6,54},{7,55},{8,0},{9,1... | collective-permute-start | bytes 196616 | tf_op jit(solution)/shard_map/ppermute | solution.py:27
  11.1 10.3 %collective-permute-start.2 = (bf16[64,512]{1,0:T(8,128)(2,1)}, bf16[64,512]{1,0:T(8,128)(2,1)S(1)}, u32[]{:S(2)}, u32[]{:S(2)}) collective-permute-start(bf16[64,512]{1,0:T(8,128)(2,1)} %param.7), channel_id=1, source_target_pairs={{0,32},{1,33},{2,34},{3,35},{4,36},{5,37},{6,38},{7,39},{8,48},{9,... | collective-permute-start | bytes 196616 | tf_op jit(solution)/shard_map/ppermute | solution.py:27
  15.5 11.7 %collective-permute-start.3 = (bf16[64,512]{1,0:T(8,128)(2,1)}, bf16[64,512]{1,0:T(8,128)(2,1)S(1)}, u32[]{:S(2)}, u32[]{:S(2)}) collective-permute-start(bf16[64,512]{1,0:T(8,128)(2,1)} %param.7), channel_id=1, source_target_pairs={{0,16},{1,17},{2,18},{3,19},{4,20},{5,21},{6,22},{7,23},{8,32},{9,... | collective-permute-start | bytes 196616 | tf_op jit(solution)/shard_map/ppermute | solution.py:27
  28.1 40.6 %collective-permute-start.4 = (bf16[192,768]{1,0:T(8,128)(2,1)S(1)}, bf16[192,768]{1,0:T(8,128)(2,1)S(1)}, u32[]{:S(2)}, u32[]{:S(2)}) collective-permute-start(bf16[192,768]{1,0:T(8,128)(2,1)S(1)} %fusion.11), channel_id=1, source_target_pairs={{0,1},{1,2},{2,3},{3,0},{4,5},{5,6},{6,7},{7,4},{8,9},{9,10},{10,1... | collective-permute-start | bytes 884744 | tf_op jit(solution)/shard_map/ppermute | solution.py:27
  31.5 39.2 %collective-permute-start.5 = (bf16[192,768]{1,0:T(8,128)(2,1)S(1)}, bf16[192,768]{1,0:T(8,128)(2,1)}, u32[]{:S(2)}, u32[]{:S(2)}) collective-permute-start(bf16[192,768]{1,0:T(8,128)(2,1)S(1)} %fusion.11), channel_id=1, source_target_pairs={{0,2},{1,3},{2,0},{3,1},{4,6},{5,7},{6,4},{7,5},{8,10},{9,11},{10,... | collective-permute-start | bytes 884744 | tf_op jit(solution)/shard_map/ppermute | solution.py:27
  36.1 41.5 %collective-permute-start.6 = (bf16[192,768]{1,0:T(8,128)(2,1)S(1)}, bf16[192,768]{1,0:T(8,128)(2,1)}, u32[]{:S(2)}, u32[]{:S(2)}) collective-permute-start(bf16[192,768]{1,0:T(8,128)(2,1)S(1)} %fusion.11), channel_id=1, source_target_pairs={{0,3},{1,0},{2,1},{3,2},{4,7},{5,4},{6,5},{7,6},{8,11},{9,8},{10,9... | collective-permute-start | bytes 884744 | tf_op jit(solution)/shard_map/ppermute | solution.py:27
  44.6 75.6 %all-to-all-start = ((bf16[8,256,512]{2,1,0:T(8,128)(2,1)}), bf16[8,256,512]{2,1,0:T(8,128)(2,1)S(1)}, u32[]{:S(2)}, u32[]{:S(2)}) async-start(bf16[8,256,512]{2,1,0:T(8,128)(2,1)} %bitcast.4), calls=%async_computation | async-start | bytes 4194304 | tf_op jit(solution)/shard_map/all_to_all | solution.py:181
  68.7 30.1 %collective-permute-start.7 = (bf16[384,768]{1,0:T(8,128)(2,1)S(1)}, bf16[384,768]{1,0:T(8,128)(2,1)S(1)}, u32[]{:S(2)}, u32[]{:S(2)}) collective-permute-start(bf16[384,768]{1,0:T(8,128)(2,1)S(1)} %pad_maximum_fusion.2), channel_id=1, source_target_pairs={{0,4},{1,5},{2,6},{3,7},{4,16},{5,17},{6,18},{7,19},{8,12},{9,13},... | collective-permute-start | bytes 1769480 | tf_op jit(solution)/shard_map/ppermute | solution.py:27
  78.7 23.5 %collective-permute-start.8 = (bf16[384,768]{1,0:T(8,128)(2,1)S(1)}, bf16[384,768]{1,0:T(8,128)(2,1)S(1)}, u32[]{:S(2)}, u32[]{:S(2)}) collective-permute-start(bf16[384,768]{1,0:T(8,128)(2,1)S(1)} %pad_maximum_fusion.3), channel_id=1, source_target_pairs={{0,52},{1,53},{2,54},{3,55},{4,0},{5,1},{6,2},{7,3},{8,60},{9,61},... | collective-permute-start | bytes 1769480 | tf_op jit(solution)/shard_map/ppermute | solution.py:27
  89.0 16.8 %copy-start.10 = (s32[512]{0:T(512)S(1)}, s32[512]{0:T(512)}, u32[]{:S(2)}) copy-start(s32[512]{0:T(512)} %param.9) | copy-start | bytes 6148
  98.7 0.8 copy-start.6
  102.2 0.8 copy-start.8
  103.9 6.8 %collective-permute-start.9 = (bf16[1536,768]{1,0:T(8,128)(2,1)}, bf16[1536,768]{1,0:T(8,128)(2,1)}, u32[]{:S(2)}, u32[]{:S(2)}) collective-permute-start(bf16[1536,768]{1,0:T(8,128)(2,1)} %constant_dynamic-update-slice_fusion.16), channel_id=1, source_target_pairs={{0,8},{1,9},{2,10},{3,11},{4,12},{5,13},{6,14},{7,15},{8,0},{9,1},... | collective-permute-start | bytes 7077896 | tf_op jit(solution)/shard_map/ppermute | solution.py:27
  105.9 1.4 copy-start.7
  105.9 1.4 copy-start.9
  106.0 1.9 copy-start.2
  114.5 0.9 copy-start.3
  118.2 2.0 %copy-start.1 = (bf16[2,512,2048]{2,1,0:T(8,128)(2,1)}, bf16[2,512,2048]{2,1,0:T(8,128)(2,1)S(1)}, u32[]{:S(2)}) copy-start(bf16[2,512,2048]{2,1,0:T(8,128)(2,1)S(1)} %shard_map.55.acts) | copy-start | bytes 12582916
  120.2 6.4 %collective-permute-start.10 = (bf16[2048,512]{1,0:T(8,128)(2,1)S(1)}, bf16[2048,512]{1,0:T(8,128)(2,1)}, u32[]{:S(2)}, u32[]{:S(2)}) collective-permute-start(bf16[2048,512]{1,0:T(8,128)(2,1)S(1)} %bitcast.22), channel_id=1, source_target_pairs={{0,8},{1,9},{2,10},{3,11},{4,12},{5,13},{6,14},{7,15},{8,0},{9,1},... | collective-permute-start | bytes 6291464 | tf_op jit(solution)/shard_map/ppermute | solution.py:27
  123.1 3.5 %copy-start.5 = (f32[512,1]{1,0:T(8,128)S(1)}, f32[512,1]{1,0:T(8,128)}, u32[]{:S(2)}) copy-start(f32[512,1]{1,0:T(8,128)} %copy.11.mask) | copy-start | bytes 6148
  126.5 4.2 %copy-start.4 = (bf16[512,768]{1,0:T(8,128)(2,1)S(1)}, bf16[512,768]{1,0:T(8,128)(2,1)}, u32[]{:S(2)}) copy-start(bf16[512,768]{1,0:T(8,128)(2,1)} %copy-done.3) | copy-start | bytes 2359300
  132.4 5.3 %collective-permute-start.11 = (f32[768,512]{1,0:T(8,128)S(1)}, f32[768,512]{1,0:T(8,128)S(1)}, u32[]{:S(2)}, u32[]{:S(2)}) collective-permute-start(f32[768,512]{1,0:T(8,128)S(1)} %shard_map.60), channel_id=1, source_target_pairs={{0,8},{1,9},{2,10},{3,11},{4,12},{5,13},{6,14},{7,15},{8,0},{9,1},... | collective-permute-start | bytes 4718600 | tf_op jit(solution)/shard_map/ppermute | solution.py:27
Sparse Core Ops, SparseCore 0:
  9.4 72.9 all-gather.1

commit v4 on v2

--- a/solution.py
+++ b/solution.py
@@ -47,32 +47,29 @@
     )
 
 
-def rotate_out_kernel(pos, grads, *refs):
-    pieces, out, basis = refs[:NX], refs[NX], refs[NX + 1]
-    rows = pieces[0].shape[0] // NYL
-    yl, x = pos[1], pos[2]
-    for d in range(NX):
-        for flip in range(NYL):
-            owner = lax.rem(yl + flip, NYL) * NX + lax.rem(x - d + NX, NX)
-            at = pl.multiple_of(owner * rows, 64)
-            basis[pl.ds(at, rows), :] = pieces[d][flip * rows : (flip + 1) * rows, :]
+def rotate_out_kernel(pos, grads, own, flipped, out, basis):
+    rows = own.shape[0] // NX
+    for ref, yl in ((own, pos[1]), (flipped, 1 - pos[1])):
+        for d in range(NX):
+            at = pl.multiple_of((yl * NX + lax.rem(pos[2] - d + NX, NX)) * rows, 64)
+            basis[pl.ds(at, rows), :] = ref[d * rows : (d + 1) * rows, :]
     width = 256
     for j in range(out.shape[1] // width):
         cols = slice(j * width, (j + 1) * width)
         out[:, cols] = jnp.dot(grads[...], basis[:, cols], preferred_element_type=F32).astype(out.dtype)
 
 
-def rotate_out(pos, grads, pieces):
+def rotate_out(pos, grads, own, flipped):
     tokens, depth = grads.shape
-    width = pieces[0].shape[1]
+    width = own.shape[1]
     return call(
         rotate_out_kernel,
         jax.ShapeDtypeStruct((tokens, width), BF16),
         [pltpu.VMEM((depth, width), BF16)],
         2 * tokens * depth * width,
         2 * (tokens * depth + depth * width + tokens * width),
-        1 + NX,
-    )(pos, grads, *pieces)
+        3,
+    )(pos, grads, own, flipped)
 
 
 def arrange_kernel(pos, *refs):
@@ -97,23 +94,23 @@
     )(pos, *pieces)
 
 
-def partial_kernel(flip, pos, acts, mine, other, out):
+def partial_kernel(flip, start, pos, acts, mine, other, out):
     core = pos[3]
     depth = acts.shape[2]
     rows = pl.ds(pl.multiple_of(lax.rem(pos[1] + flip, NYL) * depth, depth), depth)
     width = 256
     for j in range(out.shape[1] // width):
-        cols = slice(j * width, (j + 1) * width)
-        out[:, cols] = jnp.dot(acts[core], mine[rows, cols], preferred_element_type=F32) + jnp.dot(
+        here = slice(j * width, (j + 1) * width)
+        cols = slice(start + j * width, start + (j + 1) * width)
+        out[:, here] = jnp.dot(acts[core], mine[rows, cols], preferred_element_type=F32) + jnp.dot(
             acts[1 - core], other[rows, cols], preferred_element_type=F32
         )
 
 
-def partial(flip, pos, acts, mine, other):
+def partial(flip, start, width, pos, acts, mine, other):
     tokens, depth = acts.shape[1], NC * acts.shape[2]
-    width = mine.shape[1]
-    return call(
-        functools.partial(partial_kernel, flip),
+    return call(
+        functools.partial(partial_kernel, flip, start),
         jax.ShapeDtypeStruct((tokens, width), F32),
         [],
         2 * tokens * depth * width,
@@ -169,33 +166,35 @@
     return lax.all_gather(chunk, "wide", axis=0, tiled=True, axis_index_groups=groups)
 
 
-def along_x(value):
+def from_x(value):
     pieces = [value]
     for d in range(1, NX):
         pieces.append(send(value, functools.partial(lambda d, z, yh, c, yl, x: (z, yh, c, yl, x + d), d)))
     return pieces
 
 
+def flip_yl(value):
+    return send(value, lambda z, yh, c, yl, x: (z, yh, c, yl + 1, x))
+
+
+def other_yl(value):
+    half = value.shape[0] // 2
+    up = lambda z, yh, c, yl, x: (z, yh + yl, c, yl + 1, x)
+    down = lambda z, yh, c, yl, x: (z, yh + yl - 1, c, yl + 1, x)
+    return jnp.concatenate([send(value[:half], up), send(value[half:], down)], axis=0)
+
+
 def power_of(top):
     return jnp.maximum(jnp.floor(jnp.log2(jnp.maximum(top, 1e-30))), -100.0)
 
 
-def swap_partial(value):
-    power = power_of(jnp.max(jnp.abs(value)))
-    coded = (value * jnp.exp2(14.0 - power)).astype(F16)
-    label = jnp.broadcast_to(power.astype(F16), (8, value.shape[1]))
-    got = send(jnp.concatenate([coded, label], axis=0), lambda z, yh, c, yl, x: (z, yh, c, yl + 1, x))
-    return got[:-8].astype(F32) * jnp.exp2(got[-8:-7, :1].astype(F32) - 14.0)
-
-
-def pair_out_basis(out_basis, core):
+def pick(out_basis, core):
     width = out_basis.shape[1]
     own = width // (NZ * NYH * NC)
     source = lax.broadcasted_iota(jnp.int32, (width, width // NC), 0)
     place = lax.broadcasted_iota(jnp.int32, (width, width // NC), 1)
     wanted = ((place // own) * NC + core) * own + place % own
-    picked = jnp.dot(out_basis, (source == wanted).astype(BF16), preferred_element_type=F32).astype(BF16)
-    return jnp.concatenate([picked, send(picked, lambda z, yh, c, yl, x: (z, yh, c, yl + 1, x))], axis=0)
+    return jnp.dot(out_basis, (source == wanted).astype(BF16), preferred_element_type=F32).astype(BF16)
 
 
 def scatter_sum(total):
@@ -223,22 +222,35 @@
     sequences = activations.shape[0] // SEQ * lax.axis_size("wide")
 
     chunk = place_in_basis(in_basis, yh)
-    pair = pair_out_basis(out_basis, core)
-    activations, chunk, pair = lax.optimization_barrier((activations, chunk, pair))
+    activations, chunk, picked = lax.optimization_barrier((activations, chunk, pick(out_basis, core)))
     mine = gather_in_basis(chunk)
-    acts_pieces = along_x(activations)
-    *acts_pieces, pair = lax.optimization_barrier((*acts_pieces, pair))
+    basis_own = jnp.concatenate(from_x(picked), axis=0)
+    basis_flipped = other_yl(basis_own)
+    acts_pieces = from_x(activations)
+
+    top = jnp.max(jnp.abs(jnp.stack([jnp.max(jnp.abs(piece)) for piece in acts_pieces])))
+    depth = NX * activations.shape[1]
+    power = power_of(top.astype(F32) * (8.0 * depth))
+    power_theirs = flip_yl(jnp.broadcast_to(power, (8, 128)))[0, 0]
     acts = arrange(pos, acts_pieces)
-    pieces = along_x(pair)
-    mine, *pieces = lax.optimization_barrier((mine, *pieces))
+    mine, acts, basis_flipped, power_theirs = lax.optimization_barrier((mine, acts, basis_flipped, power_theirs))
+
     other = other_core(mine)
-    pieces_other = jnp.split(other_core(jnp.concatenate(pieces, axis=0)), NX, axis=0)
-
-    theirs = swap_partial(partial(1, pos, acts, mine, other))
-    rotated_in = (partial(0, pos, acts, mine, other) + theirs).astype(BF16)
-    masked_in = rotated_in * valid.astype(BF16)[:, None]
-    out_other = rotate_out(pos, out_grads, pieces_other)
-    out_mine = rotate_out(pos, out_grads, pieces)
+    basis = jnp.concatenate([basis_own, basis_flipped], axis=0)
+    basis_other = other_core(basis)
+    half = basis.shape[0] // 2
+    out_mine = rotate_out(pos, out_grads, basis_own, basis_flipped)
+    out_other = rotate_out(pos, out_grads, basis_other[:half], basis_other[half:])
+
+    columns = mine.shape[1]
+    width = columns // 2
+    theirs = []
+    for start in range(0, columns, width):
+        given = partial(1, start, width, pos, acts, mine, other)
+        got = flip_yl((given * jnp.exp2(14.0 - power)).astype(F16))
+        theirs.append(got.astype(F32) * jnp.exp2(power_theirs - 14.0))
+    rotated_in = partial(0, 0, columns, pos, acts, mine, other) + jnp.concatenate(theirs, axis=1)
+    masked_in = rotated_in.astype(BF16) * valid.astype(BF16)[:, None]
     total = other_core(squares(pos, out_other, masked_in)) + squares(pos, out_mine, masked_in)
     return scatter_sum(total) / sequences
 

time: 204 us -> 189 us (0.926)
  the two profiles are of different devices: /device:TPU:8 before, /device:TPU:48 now
where the time goes in v4:
time: 189 us; the launch traced here: 188 us
  starting transfers between devices  80.3 us (42%)
  blocking collectives  37.2 us (20%)
  between operations  16.2 us (9%)
  other arithmetic  15.9 us (8%)
  Pallas kernels  15.6 us (8%)
  local copies, waits for them, and re-layouts  14.4 us (8%)
  waiting for transfers between devices  7.62 us (4%)
    ppermute x18, starting transfers between devices, send(): return lax.ppermute(value, BOTH, pairs)  80.3 us
    all_to_all x1, blocking collectives, scatter_sum(): lax.all_to_all(jnp.concatenate([coded, label], axis=1), 'wide', 0, 0, til...  37.2 us
    unnamed x42, local copies, waits for them, and re-layouts  9.97 us
    ppermute x18, waiting for transfers between devices, send(): return lax.ppermute(value, BOTH, pairs)  7.6 us
    pallas_call x3, Pallas kernels, partial(): call(functools.partial(partial_kernel, flip, start), jax.ShapeDtypeStruct...  7.52 us
    concatenate x3, other arithmetic, shards(): basis_own = jnp.concatenate(from_x(picked), axis=0)  4.79 us
    pallas_call x2, Pallas kernels, rotate_out(): call(rotate_out_kernel, jax.ShapeDtypeStruct((tokens, width), BF16), [plt...  4.18 us
  transfers between devices with their start and end apart: 19, of which 3 were waited for; matrix products, arithmetic and copies ran while one was open for 12% of the time, Pallas kernels for 7%

profile of v4, /device:TPU:48, one launch (start us, length us, event | category | flops | bytes accessed | tf_op | source)
XLA Modules:
  0.0 188.2 jit_solution(13474856280960049495)
XLA Ops:
  6.5 3.6 %collective-permute-start = (bf16[64,512]{1,0:T(8,128)(2,1)}, bf16[64,512]{1,0:T(8,128)(2,1)S(1)}, u32[]{:S(2)}, u32[]{:S(2)}) collective-permute-start(bf16[64,512]{1,0:T(8,128)(2,1)} %param.7), channel_id=1, source_target_pairs={{0,0},{1,1},{2,2},{3,3},{4,256},{5,257},{6,258},{7,259},{8,16},{9,... | collective-permute-start | bytes 196616 | tf_op jit(solution)/shard_map/ppermute | solution.py:27
  10.1 6.0 %collective-permute-start.1 = (bf16[64,512]{1,0:T(8,128)(2,1)}, bf16[64,512]{1,0:T(8,128)(2,1)S(1)}, u32[]{:S(2)}, u32[]{:S(2)}) collective-permute-start(bf16[64,512]{1,0:T(8,128)(2,1)} %param.7), channel_id=1, source_target_pairs={{0,48},{1,49},{2,50},{3,51},{4,304},{5,305},{6,306},{7,307},{8,0},... | collective-permute-start | bytes 196616 | tf_op jit(solution)/shard_map/ppermute | solution.py:27
  16.1 1.9 %collective-permute-start.2 = (bf16[64,512]{1,0:T(8,128)(2,1)}, bf16[64,512]{1,0:T(8,128)(2,1)S(1)}, u32[]{:S(2)}, u32[]{:S(2)}) collective-permute-start(bf16[64,512]{1,0:T(8,128)(2,1)} %param.7), channel_id=1, source_target_pairs={{0,32},{1,33},{2,34},{3,35},{4,288},{5,289},{6,290},{7,291},{8,48}... | collective-permute-start | bytes 196616 | tf_op jit(solution)/shard_map/ppermute | solution.py:27
  18.1 2.0 %collective-permute-start.3 = (bf16[64,512]{1,0:T(8,128)(2,1)}, bf16[64,512]{1,0:T(8,128)(2,1)S(1)}, u32[]{:S(2)}, u32[]{:S(2)}) collective-permute-start(bf16[64,512]{1,0:T(8,128)(2,1)} %param.7), channel_id=1, source_target_pairs={{0,16},{1,17},{2,18},{3,19},{4,272},{5,273},{6,274},{7,275},{8,32}... | collective-permute-start | bytes 196616 | tf_op jit(solution)/shard_map/ppermute | solution.py:27
  20.2 1.1 fusion.11
  21.4 2.8 %collective-permute-done.2 = bf16[64,512]{1,0:T(8,128)(2,1)S(1)} collective-permute-done((bf16[64,512]{1,0:T(8,128)(2,1)}, bf16[64,512]{1,0:T(8,128)(2,1)S(1)}, u32[]{:S(2)}, u32[]{:S(2)}) %collective-permute-start.2) | collective-permute-done | bytes 65568 | tf_op jit(solution)/shard_map/ppermute | solution.py:27
  24.2 4.4 %collective-permute-done.3 = bf16[64,512]{1,0:T(8,128)(2,1)S(1)} collective-permute-done((bf16[64,512]{1,0:T(8,128)(2,1)}, bf16[64,512]{1,0:T(8,128)(2,1)S(1)}, u32[]{:S(2)}, u32[]{:S(2)}) %collective-permute-start.3) | collective-permute-done | bytes 65568 | tf_op jit(solution)/shard_map/ppermute | solution.py:27
  28.7 0.8 constant_dynamic-slice_fusion
  29.4 0.0 all-gather.2.cloned.1.call-update
  29.5 4.9 %collective-permute-start.5 = (bf16[192,768]{1,0:T(8,128)(2,1)S(1)}, bf16[192,768]{1,0:T(8,128)(2,1)S(1)}, u32[]{:S(2)}, u32[]{:S(2)}) collective-permute-start(bf16[192,768]{1,0:T(8,128)(2,1)S(1)} %fusion.11), channel_id=1, source_target_pairs={{0,2},{1,3},{2,0},{3,1},{4,6},{5,7},{6,4},{7,5},{8,10},{9,11},{10,... | collective-permute-start | bytes 884744 | tf_op jit(solution)/shard_map/ppermute | solution.py:27
  34.4 3.0 %collective-permute-start.6 = (bf16[192,768]{1,0:T(8,128)(2,1)S(1)}, bf16[192,768]{1,0:T(8,128)(2,1)}, u32[]{:S(2)}, u32[]{:S(2)}) collective-permute-start(bf16[192,768]{1,0:T(8,128)(2,1)S(1)} %fusion.11), channel_id=1, source_target_pairs={{0,3},{1,0},{2,1},{3,2},{4,7},{5,4},{6,5},{7,6},{8,11},{9,8},{10,9... | collective-permute-start | bytes 884744 | tf_op jit(solution)/shard_map/ppermute | solution.py:27
  37.4 2.8 %collective-permute-start.4 = (bf16[192,768]{1,0:T(8,128)(2,1)S(1)}, bf16[192,768]{1,0:T(8,128)(2,1)}, u32[]{:S(2)}, u32[]{:S(2)}) collective-permute-start(bf16[192,768]{1,0:T(8,128)(2,1)S(1)} %fusion.11), channel_id=1, source_target_pairs={{0,1},{1,2},{2,3},{3,0},{4,5},{5,6},{6,7},{7,4},{8,9},{9,10},{10,1... | collective-permute-start | bytes 884744 | tf_op jit(solution)/shard_map/ppermute | solution.py:27
  40.3 2.5 %collective-permute-start.7 = (bf16[512,512]{1,0:T(8,128)(2,1)S(1)}, bf16[512,512]{1,0:T(8,128)(2,1)S(1)}, u32[]{:S(2)}, u32[]{:S(2)}) collective-permute-start(bf16[512,512]{1,0:T(8,128)(2,1)S(1)} %copy-done.5), channel_id=1, source_target_pairs={{0,1},{1,2},{2,3},{3,0},{4,5},{5,6},{6,7},{7,4},{8,9},{9,10},{10,1... | collective-permute-start | bytes 1572872 | tf_op jit(solution)/shard_map/ppermute | solution.py:27
  42.8 0.1 pad_add_fusion.pos
  42.9 5.1 %collective-permute-start.8 = (bf16[512,512]{1,0:T(8,128)(2,1)S(1)}, bf16[512,512]{1,0:T(8,128)(2,1)S(1)}, u32[]{:S(2)}, u32[]{:S(2)}) collective-permute-start(bf16[512,512]{1,0:T(8,128)(2,1)S(1)} %copy-done.5), channel_id=1, source_target_pairs={{0,2},{1,3},{2,0},{3,1},{4,6},{5,7},{6,4},{7,5},{8,10},{9,11},{10,... | collective-permute-start | bytes 1572872 | tf_op jit(solution)/shard_map/ppermute | solution.py:27
  48.0 1.9 %collective-permute-start.9 = (bf16[512,512]{1,0:T(8,128)(2,1)S(1)}, bf16[512,512]{1,0:T(8,128)(2,1)S(1)}, u32[]{:S(2)}, u32[]{:S(2)}) collective-permute-start(bf16[512,512]{1,0:T(8,128)(2,1)S(1)} %copy-done.5), channel_id=1, source_target_pairs={{0,3},{1,0},{2,1},{3,2},{4,7},{5,4},{6,5},{7,6},{8,11},{9,8},{10,9... | collective-permute-start | bytes 1572872 | tf_op jit(solution)/shard_map/ppermute | solution.py:27
  50.0 1.8 pad_maximum_fusion.3
  51.8 17.6 %collective-permute-start.11 = (bf16[384,768]{1,0:T(8,128)(2,1)}, bf16[384,768]{1,0:T(8,128)(2,1)}, u32[]{:S(2)}, u32[]{:S(2)}) collective-permute-start(bf16[384,768]{1,0:T(8,128)(2,1)} %pad_maximum_fusion.3), channel_id=1, source_target_pairs={{0,52},{1,53},{2,54},{3,55},{4,0},{5,1},{6,2},{7,3},{8,60},{9,61},... | collective-permute-start | bytes 1769480 | tf_op jit(solution)/shard_map/ppermute | solution.py:27
  69.4 1.8 pad_maximum_fusion.2
  71.2 1.9 %collective-permute-start.10 = (bf16[384,768]{1,0:T(8,128)(2,1)}, bf16[384,768]{1,0:T(8,128)(2,1)}, u32[]{:S(2)}, u32[]{:S(2)}) collective-permute-start(bf16[384,768]{1,0:T(8,128)(2,1)} %pad_maximum_fusion.2), channel_id=1, source_target_pairs={{0,4},{1,5},{2,6},{3,7},{4,16},{5,17},{6,18},{7,19},{8,12},{9,13},... | collective-permute-start | bytes 1769480 | tf_op jit(solution)/shard_map/ppermute | solution.py:27
  73.1 0.8 abs_reduce_fusion.3
  73.9 0.7 abs_reduce_fusion.2
  74.6 0.7 abs_reduce_fusion.1
  75.3 0.7 abs_reduce_fusion
  76.0 3.3 %fusion.20 = bf16[]{:T(256)} fusion(bf16[1]{0:T(256)(128)(2,1)} %bitcast.8, bf16[1]{0:T(256)(128)(2,1)} %bitcast.7, bf16[1]{0:T(256)(128)(2,1)} %bitcast.6, bf16[1]{0:T(256)(128)(2,1)} %bitcast.5), kind=kLoop, calls=%fused_computation.56 | loop fusion | flops 39 | bytes 10 | tf_op jit(solution)/shard_map/reduce_max | solution.py:231
  80.0 14.8 %collective-permute-start.12 = (f32[8,128]{1,0:T(8,128)S(1)}, f32[8,128]{1,0:T(8,128)S(1)}, u32[]{:S(2)}, u32[]{:S(2)}) collective-permute-start(f32[8,128]{1,0:T(8,128)S(1)} %broadcast_in_dim.2), channel_id=1, source_target_pairs={{0,4},{1,5},{2,6},{3,7},{4,0},{5,1},{6,2},{7,3},{8,12},{9,13},{10,... | collective-permute-start | bytes 12296 | tf_op jit(solution)/shard_map/ppermute | solution.py:27
  94.8 0.7 constant_dynamic-update-slice_fusion.12
  95.5 1.0 copy-done.7
  96.5 1.0 copy-done.9
  97.6 1.0 copy-done.11
  98.6 0.8 shard_map.55.acts
  99.5 0.5 slice.19
  100.0 2.3 %pad_maximum_fusion.flipped = bf16[768,768]{1,0:T(8,128)(2,1)} fusion(bf16[384,768]{1,0:T(8,128)(2,1)} %collective-permute-done.11, bf16[384,768]{1,0:T(8,128)(2,1)} %collective-permute-done.10), kind=kLoop, calls=%fused_computation.14 | loop fusion | flops 2359296 | bytes 2359296 | tf_op jit(solution)/shard_map/concatenate | solution.py:184
  102.3 2.0 %collective-permute-start.14 = (bf16[2048,512]{1,0:T(8,128)(2,1)}, bf16[2048,512]{1,0:T(8,128)(2,1)}, u32[]{:S(2)}, u32[]{:S(2)}) collective-permute-start(bf16[2048,512]{1,0:T(8,128)(2,1)} %all-gather.2.cloned.1.call-done.mine), channel_id=1, source_target_pairs={{0,8},{1,9},{2,10},{3,11},{4,12},{5,13},{6,14},{7,15},{8,0},{9,1},... | collective-permute-start | bytes 6291464 | tf_op jit(solution)/shard_map/ppermute | solution.py:27
  104.4 1.7 constant_dynamic-update-slice_fusion.11
  106.1 0.7 constant_dynamic-update-slice_fusion.10
  106.8 1.7 constant_dynamic-update-slice_fusion.9
  108.5 1.1 constant_dynamic-update-slice_fusion.8
  109.6 2.4 %collective-permute-start.13 = (bf16[1536,768]{1,0:T(8,128)(2,1)}, bf16[1536,768]{1,0:T(8,128)(2,1)}, u32[]{:S(2)}, u32[]{:S(2)}) collective-permute-start(bf16[1536,768]{1,0:T(8,128)(2,1)} %constant_dynamic-update-slice_fusion.8), channel_id=1, source_target_pairs={{0,8},{1,9},{2,10},{3,11},{4,12},{5,13},{6,14},{7,15},{8,0},{9,1},... | collective-permute-start | bytes 7077896 | tf_op jit(solution)/shard_map/ppermute | solution.py:27
  112.8 1.6 copy-done.1
  114.4 2.3 %shard_map.58 = f32[512,256]{1,0:T(8,128)S(1)} custom-call(s32[4]{0:T(128)S(1)} %pad_add_fusion.pos, bf16[2,512,1024]{2,1,0:T(8,128)(2,1)S(1)} %shard_map.55.acts, bf16[2048,512]{1,0:T(8,128)(2,1)S(1)} %copy-done.1, bf16[2048,512]{1,0:T(8,128)(2,1)} %collective-permute-done.14.other), custom_call_target="tpu_custom_call" | custom-call | flops 536870912 | bytes 3670016 | tf_op jit(solution)/shard_map/pallas_call | solution.py:112
  116.7 0.1 multiply_convert_fusion.2
  116.7 1.9 %collective-permute-start.15 = (f16[512,256]{1,0:T(8,128)(2,1)S(1)}, f16[512,256]{1,0:T(8,128)(2,1)S(1)}, u32[]{:S(2)}, u32[]{:S(2)}) collective-permute-start(f16[512,256]{1,0:T(8,128)(2,1)S(1)} %multiply_convert_fusion.2), channel_id=1, source_target_pairs={{0,4},{1,5},{2,6},{3,7},{4,0},{5,1},{6,2},{7,3},{8,12},{9,13},{10,... | collective-permute-start | bytes 786440 | tf_op jit(solution)/shard_map/ppermute | solution.py:27
  118.7 2.3 %shard_map.59 = f32[512,256]{1,0:T(8,128)S(1)} custom-call(s32[4]{0:T(128)S(1)} %pad_add_fusion.pos, bf16[2,512,1024]{2,1,0:T(8,128)(2,1)S(1)} %shard_map.55.acts, bf16[2048,512]{1,0:T(8,128)(2,1)S(1)} %copy-done.1, bf16[2048,512]{1,0:T(8,128)(2,1)} %collective-permute-done.14.other), custom_call_target="tpu_custom_call" | custom-call | flops 536870912 | bytes 3670016 | tf_op jit(solution)/shard_map/pallas_call | solution.py:112
  121.0 0.1 multiply_convert_fusion.1
  121.1 3.9 %collective-permute-start.16 = (f16[512,256]{1,0:T(8,128)(2,1)S(1)}, f16[512,256]{1,0:T(8,128)(2,1)S(1)}, u32[]{:S(2)}, u32[]{:S(2)}) collective-permute-start(f16[512,256]{1,0:T(8,128)(2,1)S(1)} %multiply_convert_fusion.1), channel_id=1, source_target_pairs={{0,4},{1,5},{2,6},{3,7},{4,0},{5,1},{6,2},{7,3},{8,12},{9,13},{10,... | collective-permute-start | bytes 786440 | tf_op jit(solution)/shard_map/ppermute | solution.py:27
  125.0 2.9 %shard_map.57 = f32[512,512]{1,0:T(8,128)S(1)} custom-call(s32[4]{0:T(128)S(1)} %pad_add_fusion.pos, bf16[2,512,1024]{2,1,0:T(8,128)(2,1)S(1)} %shard_map.55.acts, bf16[2048,512]{1,0:T(8,128)(2,1)S(1)} %copy-done.1, bf16[2048,512]{1,0:T(8,128)(2,1)} %collective-permute-done.14.other), custom_call_target="tpu_custom_call" | custom-call | flops 1073741824 | bytes 5242880 | tf_op jit(solution)/shard_map/pallas_call | solution.py:112
  127.9 1.9 %fusion.24 = (bf16[768,768]{1,0:T(8,128)(2,1)S(1)}, bf16[768,768]{1,0:T(8,128)(2,1)S(1)}) fusion(bf16[1536,768]{1,0:T(8,128)(2,1)} %collective-permute-done.13), kind=kLoop, calls=%fused_computation.62 | loop fusion | bytes 4718592 | tf_op jit(solution)/shard_map/slice | solution.py:243
  129.8 0.2 copy-done.4
  130.0 2.1 %shard_map.56.outs = bf16[512,768]{1,0:T(8,128)(2,1)S(1)} custom-call(s32[4]{0:T(128)S(1)} %pad_add_fusion.pos, bf16[512,1536]{1,0:T(8,128)(2,1)S(1)} %copy-done.4, bf16[768,768]{1,0:T(8,128)(2,1)S(1)} %get-tuple-element.22.own, bf16[768,768]{1,0:T(8,128)(2,1)S(1)} %get-tuple-element.21.flipped), custom_call_target="tpu_custom_call" | custom-call | flops 1207959552 | bytes 4718592 | tf_op jit(solution)/shard_map/pallas_call | solution.py:65
  132.1 0.3 collective-permute-done.16
  132.5 0.2 fusion.13.ins
  132.7 1.5 shard_map.60
  134.3 1.9 %collective-permute-start.17 = (f32[768,512]{1,0:T(8,128)S(1)}, f32[768,512]{1,0:T(8,128)S(1)}, u32[]{:S(2)}, u32[]{:S(2)}) collective-permute-start(f32[768,512]{1,0:T(8,128)S(1)} %shard_map.60), channel_id=1, source_target_pairs={{0,8},{1,9},{2,10},{3,11},{4,12},{5,13},{6,14},{7,15},{8,0},{9,1},... | collective-permute-start | bytes 4718600 | tf_op jit(solution)/shard_map/ppermute | solution.py:27
  136.2 1.1 pad_maximum_fusion.1.own
  137.4 2.1 %shard_map.61.outs = bf16[512,768]{1,0:T(8,128)(2,1)S(1)} custom-call(s32[4]{0:T(128)S(1)} %pad_add_fusion.pos, bf16[512,1536]{1,0:T(8,128)(2,1)S(1)} %copy-done.4, bf16[768,768]{1,0:T(8,128)(2,1)S(1)} %pad_maximum_fusion.1.own, bf16[768,768]{1,0:T(8,128)(2,1)S(1)} %copy-done.3), custom_call_target="tpu_custom_call" | custom-call | flops 1207959552 | bytes 4718592 | tf_op jit(solution)/shard_map/pallas_call | solution.py:65
  139.5 1.5 shard_map.62
  141.0 1.1 fusion.23
  142.8 0.2 multiply_convert_fusion
  143.1 0.2 concatenate.32
  143.2 37.2 %all_to_all.5 = f16[32,104,128]{2,1,0:T(8,128)(2,1)S(1)} all-to-all(f16[32,104,128]{2,1,0:T(8,128)(2,1)S(1)} %concatenate.32), channel_id=1, replica_groups={{0,16,32,48,64,80,96,112,128,144,160,176,192,208,224,240,256,272,288,30..., dimensions={0} | all-to-all | bytes 1703936 | tf_op jit(solution)/shard_map/all_to_all | solution.py:209
  180.4 0.1 copy.8
  180.5 0.2 multiply_reduce_fusion
  180.7 0.6 broadcast_multiply_fusion
  (59 shorter events, 0.3 us)
Async XLA Ops:
  6.5 13.6 %copy-start = (bf16[192,1536]{1,0:T(8,128)(2,1)S(1)}, bf16[192,1536]{1,0:T(8,128)(2,1)}, u32[]{:S(2)}) copy-start(bf16[192,1536]{1,0:T(8,128)(2,1)} %param.8) | copy-start | bytes 1769476
  6.5 95.8 %all-gather.2.cloned.1.call-start = ((), (), s32[]{:S(2)}) async-start(), calls=%async_computation.1 | async-start | bytes 2359296 | tf_op jit(solution)/shard_map/all_gather | solution.py:166
  6.5 14.8 %collective-permute-start = (bf16[64,512]{1,0:T(8,128)(2,1)}, bf16[64,512]{1,0:T(8,128)(2,1)S(1)}, u32[]{:S(2)}, u32[]{:S(2)}) collective-permute-start(bf16[64,512]{1,0:T(8,128)(2,1)} %param.7), channel_id=1, source_target_pairs={{0,0},{1,1},{2,2},{3,3},{4,256},{5,257},{6,258},{7,259},{8,16},{9,... | collective-permute-start | bytes 196616 | tf_op jit(solution)/shard_map/ppermute | solution.py:27
  10.1 11.2 %collective-permute-start.1 = (bf16[64,512]{1,0:T(8,128)(2,1)}, bf16[64,512]{1,0:T(8,128)(2,1)S(1)}, u32[]{:S(2)}, u32[]{:S(2)}) collective-permute-start(bf16[64,512]{1,0:T(8,128)(2,1)} %param.7), channel_id=1, source_target_pairs={{0,48},{1,49},{2,50},{3,51},{4,304},{5,305},{6,306},{7,307},{8,0},... | collective-permute-start | bytes 196616 | tf_op jit(solution)/shard_map/ppermute | solution.py:27
  16.1 8.0 %collective-permute-start.2 = (bf16[64,512]{1,0:T(8,128)(2,1)}, bf16[64,512]{1,0:T(8,128)(2,1)S(1)}, u32[]{:S(2)}, u32[]{:S(2)}) collective-permute-start(bf16[64,512]{1,0:T(8,128)(2,1)} %param.7), channel_id=1, source_target_pairs={{0,32},{1,33},{2,34},{3,35},{4,288},{5,289},{6,290},{7,291},{8,48}... | collective-permute-start | bytes 196616 | tf_op jit(solution)/shard_map/ppermute | solution.py:27
  18.1 10.5 %collective-permute-start.3 = (bf16[64,512]{1,0:T(8,128)(2,1)}, bf16[64,512]{1,0:T(8,128)(2,1)S(1)}, u32[]{:S(2)}, u32[]{:S(2)}) collective-permute-start(bf16[64,512]{1,0:T(8,128)(2,1)} %param.7), channel_id=1, source_target_pairs={{0,16},{1,17},{2,18},{3,19},{4,272},{5,273},{6,274},{7,275},{8,32}... | collective-permute-start | bytes 196616 | tf_op jit(solution)/shard_map/ppermute | solution.py:27
  20.2 20.1 %copy-start.5 = (bf16[512,512]{1,0:T(8,128)(2,1)S(1)}, bf16[512,512]{1,0:T(8,128)(2,1)}, u32[]{:S(2)}) copy-start(bf16[512,512]{1,0:T(8,128)(2,1)} %refs_0_) | copy-start | bytes 1572868
  29.5 18.6 %collective-permute-start.5 = (bf16[192,768]{1,0:T(8,128)(2,1)S(1)}, bf16[192,768]{1,0:T(8,128)(2,1)S(1)}, u32[]{:S(2)}, u32[]{:S(2)}) collective-permute-start(bf16[192,768]{1,0:T(8,128)(2,1)S(1)} %fusion.11), channel_id=1, source_target_pairs={{0,2},{1,3},{2,0},{3,1},{4,6},{5,7},{6,4},{7,5},{8,10},{9,11},{10,... | collective-permute-start | bytes 884744 | tf_op jit(solution)/shard_map/ppermute | solution.py:27
  34.4 15.6 %collective-permute-start.6 = (bf16[192,768]{1,0:T(8,128)(2,1)S(1)}, bf16[192,768]{1,0:T(8,128)(2,1)}, u32[]{:S(2)}, u32[]{:S(2)}) collective-permute-start(bf16[192,768]{1,0:T(8,128)(2,1)S(1)} %fusion.11), channel_id=1, source_target_pairs={{0,3},{1,0},{2,1},{3,2},{4,7},{5,4},{6,5},{7,6},{8,11},{9,8},{10,9... | collective-permute-start | bytes 884744 | tf_op jit(solution)/shard_map/ppermute | solution.py:27
  37.4 31.9 %collective-permute-start.4 = (bf16[192,768]{1,0:T(8,128)(2,1)S(1)}, bf16[192,768]{1,0:T(8,128)(2,1)}, u32[]{:S(2)}, u32[]{:S(2)}) collective-permute-start(bf16[192,768]{1,0:T(8,128)(2,1)S(1)} %fusion.11), channel_id=1, source_target_pairs={{0,1},{1,2},{2,3},{3,0},{4,5},{5,6},{6,7},{7,4},{8,9},{9,10},{10,1... | collective-permute-start | bytes 884744 | tf_op jit(solution)/shard_map/ppermute | solution.py:27
  40.3 33.6 %collective-permute-start.7 = (bf16[512,512]{1,0:T(8,128)(2,1)S(1)}, bf16[512,512]{1,0:T(8,128)(2,1)S(1)}, u32[]{:S(2)}, u32[]{:S(2)}) collective-permute-start(bf16[512,512]{1,0:T(8,128)(2,1)S(1)} %copy-done.5), channel_id=1, source_target_pairs={{0,1},{1,2},{2,3},{3,0},{4,5},{5,6},{6,7},{7,4},{8,9},{9,10},{10,1... | collective-permute-start | bytes 1572872 | tf_op jit(solution)/shard_map/ppermute | solution.py:27
  42.9 31.7 %collective-permute-start.8 = (bf16[512,512]{1,0:T(8,128)(2,1)S(1)}, bf16[512,512]{1,0:T(8,128)(2,1)S(1)}, u32[]{:S(2)}, u32[]{:S(2)}) collective-permute-start(bf16[512,512]{1,0:T(8,128)(2,1)S(1)} %copy-done.5), channel_id=1, source_target_pairs={{0,2},{1,3},{2,0},{3,1},{4,6},{5,7},{6,4},{7,5},{8,10},{9,11},{10,... | collective-permute-start | bytes 1572872 | tf_op jit(solution)/shard_map/ppermute | solution.py:27
  48.0 28.0 %copy-start.12 = (bf16[192,768]{1,0:T(8,128)(2,1)}, bf16[192,768]{1,0:T(8,128)(2,1)S(1)}, u32[]{:S(2)}) copy-start(bf16[192,768]{1,0:T(8,128)(2,1)S(1)} %collective-permute-done.5) | copy-start | bytes 884740
  48.0 27.3 %collective-permute-start.9 = (bf16[512,512]{1,0:T(8,128)(2,1)S(1)}, bf16[512,512]{1,0:T(8,128)(2,1)S(1)}, u32[]{:S(2)}, u32[]{:S(2)}) collective-permute-start(bf16[512,512]{1,0:T(8,128)(2,1)S(1)} %copy-done.5), channel_id=1, source_target_pairs={{0,3},{1,0},{2,1},{3,2},{4,7},{5,4},{6,5},{7,6},{8,11},{9,8},{10,9... | collective-permute-start | bytes 1572872 | tf_op jit(solution)/shard_map/ppermute | solution.py:27
  51.8 48.2 %collective-permute-start.11 = (bf16[384,768]{1,0:T(8,128)(2,1)}, bf16[384,768]{1,0:T(8,128)(2,1)}, u32[]{:S(2)}, u32[]{:S(2)}) collective-permute-start(bf16[384,768]{1,0:T(8,128)(2,1)} %pad_maximum_fusion.3), channel_id=1, source_target_pairs={{0,52},{1,53},{2,54},{3,55},{4,0},{5,1},{6,2},{7,3},{8,60},{9,61},... | collective-permute-start | bytes 1769480 | tf_op jit(solution)/shard_map/ppermute | solution.py:27
  71.2 28.8 %collective-permute-start.10 = (bf16[384,768]{1,0:T(8,128)(2,1)}, bf16[384,768]{1,0:T(8,128)(2,1)}, u32[]{:S(2)}, u32[]{:S(2)}) collective-permute-start(bf16[384,768]{1,0:T(8,128)(2,1)} %pad_maximum_fusion.2), channel_id=1, source_target_pairs={{0,4},{1,5},{2,6},{3,7},{4,16},{5,17},{6,18},{7,19},{8,12},{9,13},... | collective-permute-start | bytes 1769480 | tf_op jit(solution)/shard_map/ppermute | solution.py:27
  73.9 20.9 %copy-start.6 = (bf16[512,512]{1,0:T(8,128)(2,1)}, bf16[512,512]{1,0:T(8,128)(2,1)S(1)}, u32[]{:S(2)}) copy-start(bf16[512,512]{1,0:T(8,128)(2,1)S(1)} %collective-permute-done.7.refs_1_) | copy-start | bytes 1572868
  74.6 20.2 %copy-start.8 = (bf16[512,512]{1,0:T(8,128)(2,1)}, bf16[512,512]{1,0:T(8,128)(2,1)S(1)}, u32[]{:S(2)}) copy-start(bf16[512,512]{1,0:T(8,128)(2,1)S(1)} %collective-permute-done.8.refs_2_) | copy-start | bytes 1572868
  75.3 19.4 %copy-start.10 = (bf16[512,512]{1,0:T(8,128)(2,1)}, bf16[512,512]{1,0:T(8,128)(2,1)S(1)}, u32[]{:S(2)}) copy-start(bf16[512,512]{1,0:T(8,128)(2,1)S(1)} %collective-permute-done.9.refs_3_) | copy-start | bytes 1572868
  80.0 19.5 %collective-permute-start.12 = (f32[8,128]{1,0:T(8,128)S(1)}, f32[8,128]{1,0:T(8,128)S(1)}, u32[]{:S(2)}, u32[]{:S(2)}) collective-permute-start(f32[8,128]{1,0:T(8,128)S(1)} %broadcast_in_dim.2), channel_id=1, source_target_pairs={{0,4},{1,5},{2,6},{3,7},{4,0},{5,1},{6,2},{7,3},{8,12},{9,13},{10,... | collective-permute-start | bytes 12296 | tf_op jit(solution)/shard_map/ppermute | solution.py:27
  95.5 1.0 copy-start.7
  96.5 1.0 copy-start.9
  97.6 1.0 copy-start.11
  99.5 6.6 %copy-start.13 = (bf16[192,768]{1,0:T(8,128)(2,1)S(1)}, bf16[192,768]{1,0:T(8,128)(2,1)}, u32[]{:S(2)}) copy-start(bf16[192,768]{1,0:T(8,128)(2,1)} %copy-done.12) | copy-start | bytes 884740
  102.3 9.7 %copy-start.14 = (s32[512]{0:T(512)S(1)}, s32[512]{0:T(512)}, u32[]{:S(2)}) copy-start(s32[512]{0:T(512)} %param.9) | copy-start | bytes 6148
  102.3 6.2 %copy-start.2 = (bf16[768,768]{1,0:T(8,128)(2,1)S(1)}, bf16[768,768]{1,0:T(8,128)(2,1)}, u32[]{:S(2)}) copy-start(bf16[768,768]{1,0:T(8,128)(2,1)} %pad_maximum_fusion.flipped) | copy-start | bytes 3538948
  102.3 10.4 %collective-permute-start.14 = (bf16[2048,512]{1,0:T(8,128)(2,1)}, bf16[2048,512]{1,0:T(8,128)(2,1)}, u32[]{:S(2)}, u32[]{:S(2)}) collective-permute-start(bf16[2048,512]{1,0:T(8,128)(2,1)} %all-gather.2.cloned.1.call-done.mine), channel_id=1, source_target_pairs={{0,8},{1,9},{2,10},{3,11},{4,12},{5,13},{6,14},{7,15},{8,0},{9,1},... | collective-permute-start | bytes 6291464 | tf_op jit(solution)/shard_map/ppermute | solution.py:27
  109.6 18.3 %collective-permute-start.13 = (bf16[1536,768]{1,0:T(8,128)(2,1)}, bf16[1536,768]{1,0:T(8,128)(2,1)}, u32[]{:S(2)}, u32[]{:S(2)}) collective-permute-start(bf16[1536,768]{1,0:T(8,128)(2,1)} %constant_dynamic-update-slice_fusion.8), channel_id=1, source_target_pairs={{0,8},{1,9},{2,10},{3,11},{4,12},{5,13},{6,14},{7,15},{8,0},{9,1},... | collective-permute-start | bytes 7077896 | tf_op jit(solution)/shard_map/ppermute | solution.py:27
  112.8 1.6 copy-start.1
  116.7 15.3 %collective-permute-start.15 = (f16[512,256]{1,0:T(8,128)(2,1)S(1)}, f16[512,256]{1,0:T(8,128)(2,1)S(1)}, u32[]{:S(2)}, u32[]{:S(2)}) collective-permute-start(f16[512,256]{1,0:T(8,128)(2,1)S(1)} %multiply_convert_fusion.2), channel_id=1, source_target_pairs={{0,4},{1,5},{2,6},{3,7},{4,0},{5,1},{6,2},{7,3},{8,12},{9,13},{10,... | collective-permute-start | bytes 786440 | tf_op jit(solution)/shard_map/ppermute | solution.py:27
  121.1 11.4 %collective-permute-start.16 = (f16[512,256]{1,0:T(8,128)(2,1)S(1)}, f16[512,256]{1,0:T(8,128)(2,1)S(1)}, u32[]{:S(2)}, u32[]{:S(2)}) collective-permute-start(f16[512,256]{1,0:T(8,128)(2,1)S(1)} %multiply_convert_fusion.1), channel_id=1, source_target_pairs={{0,4},{1,5},{2,6},{3,7},{4,0},{5,1},{6,2},{7,3},{8,12},{9,13},{10,... | collective-permute-start | bytes 786440 | tf_op jit(solution)/shard_map/ppermute | solution.py:27
  127.9 2.1 %copy-start.4 = (bf16[512,1536]{1,0:T(8,128)(2,1)S(1)}, bf16[512,1536]{1,0:T(8,128)(2,1)}, u32[]{:S(2)}) copy-start(bf16[512,1536]{1,0:T(8,128)(2,1)} %grads.3) | copy-start | bytes 4718596
  132.7 4.6 %copy-start.3 = (bf16[768,768]{1,0:T(8,128)(2,1)S(1)}, bf16[768,768]{1,0:T(8,128)(2,1)}, u32[]{:S(2)}) copy-start(bf16[768,768]{1,0:T(8,128)(2,1)} %pad_maximum_fusion.flipped) | copy-start | bytes 3538948
  134.3 6.7 %collective-permute-start.17 = (f32[768,512]{1,0:T(8,128)S(1)}, f32[768,512]{1,0:T(8,128)S(1)}, u32[]{:S(2)}, u32[]{:S(2)}) collective-permute-start(f32[768,512]{1,0:T(8,128)S(1)} %shard_map.60), channel_id=1, source_target_pairs={{0,8},{1,9},{2,10},{3,11},{4,12},{5,13},{6,14},{7,15},{8,0},{9,1},... | collective-permute-start | bytes 4718600 | tf_op jit(solution)/shard_map/ppermute | solution.py:27
Sparse Core Ops, SparseCore 0:
  29.6 57.0 all-gather.1

commit v5 on v3

--- a/solution.py
+++ b/solution.py
@@ -72,63 +72,48 @@
     )(pos, grads, own, flipped)
 
 
-def arrange_kernel(pos, acts, out):
-    half = acts.shape[1] // (NZ * NC)
+def half_product(acts, basis, core):
+    chunk = basis.shape[0] // NZ
+    total = jnp.zeros((acts.shape[0], basis.shape[1]), F32)
     for z in range(NZ):
-        for c in range(NC):
-            at = (z * NC + c) * half
-            out[c, :, z * half : (z + 1) * half] = acts[:, at : at + half]
-
-
-def arrange(pos, acts):
+        at = pl.multiple_of((z * NC + core) * chunk, chunk)
+        total += jnp.dot(
+            acts[:, pl.ds(at, chunk)], basis[z * chunk : (z + 1) * chunk, :], preferred_element_type=F32
+        )
+    return total
+
+
+def first_half_kernel(pos, acts, mine, out):
+    out[...] = half_product(acts, mine, pos[3])
+
+
+def first_half(pos, acts, mine):
     tokens, depth = acts.shape
-    return call(
-        arrange_kernel,
-        jax.ShapeDtypeStruct((NC, tokens, depth // NC), BF16),
-        [],
-        0,
-        4 * tokens * depth,
-        1,
-    )(pos, acts)
-
-
-def first_half_kernel(pos, acts, mine, out):
-    core, width = pos[3], 256
-    for j in range(out.shape[1] // width):
-        cols = slice(j * width, (j + 1) * width)
-        out[:, cols] = jnp.dot(acts[core], mine[:, cols], preferred_element_type=F32)
-
-
-def first_half(pos, acts, mine):
-    _, tokens, depth = acts.shape
     width = mine.shape[1]
     return call(
         first_half_kernel,
         jax.ShapeDtypeStruct((tokens, width), F32),
         [],
-        2 * tokens * depth * width,
-        2 * (tokens * depth + depth * width) + 4 * tokens * width,
+        tokens * depth * width,
+        2 * (tokens * depth + depth * width // 2) + 4 * tokens * width,
         2,
     )(pos, acts, mine)
 
 
 def masked_kernel(pos, acts, other, first, mask, out):
-    core, width = pos[3], 256
-    for j in range(out.shape[1] // width):
-        cols = slice(j * width, (j + 1) * width)
-        total = first[:, cols] + jnp.dot(acts[1 - core], other[:, cols], preferred_element_type=F32)
-        out[:, cols] = (total.astype(BF16).astype(F32) * mask[...]).astype(BF16)
+    total = first[...] + half_product(acts, other, 1 - pos[3])
+    out[...] = (total.astype(BF16).astype(F32) * mask[...]).astype(BF16)
 
 
 def masked(pos, acts, other, first, mask):
-    _, tokens, depth = acts.shape
+    tokens, depth = acts.shape
     width = other.shape[1]
     return call(
         masked_kernel,
         jax.ShapeDtypeStruct((tokens, width), BF16),
         [],
-        2 * tokens * depth * width,
-        2 * (tokens * depth + depth * width) + 6 * tokens * width,
+        tokens * depth * width,
+        2 * (tokens * depth + depth * width // 2) + 6 * tokens * width,
         4,
     )(pos, acts, other, first, mask)
 
@@ -177,8 +162,8 @@
 
 def gather_in_basis(chunk):
     groups = [[z * NYH * NC + r for z in range(NZ)] for r in range(NYH * NC)]
-    copies = jnp.concatenate([chunk] * NZ, axis=0)
-    return lax.all_to_all(copies, "wide", 0, 0, tiled=True, axis_index_groups=groups)
+    copies = jnp.broadcast_to(chunk[None], (NZ, *chunk.shape))
+    return lax.all_to_all(copies, "wide", 0, 0, axis_index_groups=groups).reshape(-1, chunk.shape[1])
 
 
 def from_x(value):
@@ -232,20 +217,19 @@
     pos = jnp.stack([z, yl, x, core]).astype(jnp.int32)
     sequences = activations.shape[0] // SEQ * lax.axis_size("wide")
 
+    in_basis, picked = lax.optimization_barrier((in_basis, pick(out_basis, core)))
+    basis_own = jnp.concatenate(from_x(picked), axis=0)
+    chunk = place_in_basis(in_basis, yh)
+    activations, basis_own, chunk = lax.optimization_barrier((activations, basis_own, chunk))
     acts = lax.all_gather(activations, "narrow", axis=1, tiled=True)
-    chunk = place_in_basis(in_basis, yh)
     mine = gather_in_basis(chunk)
-    picked, _ = lax.optimization_barrier((pick(out_basis, core), chunk))
-    basis_own = jnp.concatenate(from_x(picked), axis=0)
     basis_flipped = other_yl(basis_own)
     basis = jnp.concatenate([basis_own, basis_flipped], axis=0)
     basis_other = other_core(basis)
     half = basis.shape[0] // 2
     out_mine = rotate_out(pos, out_grads, basis_own, basis_flipped)
     out_other = rotate_out(pos, out_grads, basis_other[:half], basis_other[half:])
-    acts = arrange(pos, acts)
     mask = valid.astype(F32)[:, None]
-    mine, acts, mask, out_mine, out_other = lax.optimization_barrier((mine, acts, mask, out_mine, out_other))
     other = other_core(mine)
     masked_in = masked(pos, acts, other, first_half(pos, acts, mine), mask)
     total = other_core(squares(pos, out_other, masked_in)) + squares(pos, out_mine, masked_in)

time: 193 us -> 182 us (0.943)
  the two profiles are of different devices: /device:TPU:32 before, /device:TPU:8 now
where the time goes in v5:
time: 182 us
  waiting for transfers between devices  49.5 us (27%)
  starting transfers between devices  47.6 us (26%)
  blocking collectives  42.3 us (23%)
  Pallas kernels  15.6 us (9%)
  between operations  14.6 us (8%)
  local copies, waits for them, and re-layouts  7 us (4%)
  other arithmetic  4.04 us (2%)
    all_to_all x1, blocking collectives, scatter_sum(): lax.all_to_all(jnp.concatenate([coded, label], axis=1), 'wide', 0, 0, til...  42.3 us
    ppermute x12, starting transfers between devices, send(): return lax.ppermute(value, BOTH, pairs)  37.3 us
    ppermute x12, waiting for transfers between devices, send(): return lax.ppermute(value, BOTH, pairs)  33.7 us
    all_to_all x1, waiting for transfers between devices, gather_in_basis(): lax.all_to_all(copies, 'wide', 0, 0, axis_index_groups=groups)  14 us
    all_to_all x1, starting transfers between devices, gather_in_basis(): lax.all_to_all(copies, 'wide', 0, 0, axis_index_groups=groups)  10.3 us
    pallas_call x1, Pallas kernels, masked(): call(masked_kernel, jax.ShapeDtypeStruct((tokens, width), BF16), [], toke...  4.2 us
    pallas_call x2, Pallas kernels, rotate_out(): call(rotate_out_kernel, jax.ShapeDtypeStruct((tokens, width), BF16), [plt...  4.18 us
    pallas_call x1, Pallas kernels, first_half(): call(first_half_kernel, jax.ShapeDtypeStruct((tokens, width), F32), [], t...  4.15 us
  transfers between devices with their start and end apart: 14, of which 6 were waited for; matrix products, arithmetic and copies ran while one was open for 4% of the time, Pallas kernels for 5%

profile of v5, /device:TPU:8, one launch (start us, length us, event | category | flops | bytes accessed | tf_op | source)
XLA Modules:
  0.0 181.8 jit_solution(3865501708950449517)
XLA Ops:
  6.5 0.0 copy-start
  6.5 0.0 all-gather.2.cloned.1.call-start
  6.6 1.0 copy-done
  7.6 1.1 fusion.11
  8.7 0.0 copy-done.10
  8.7 0.7 collective-permute-start.3
  9.4 4.7 %collective-permute-start.2 = (bf16[192,768]{1,0:T(8,128)(2,1)S(1)}, bf16[192,768]{1,0:T(8,128)(2,1)S(1)}, u32[]{:S(2)}, u32[]{:S(2)}) collective-permute-start(bf16[192,768]{1,0:T(8,128)(2,1)S(1)} %fusion.11), channel_id=1, source_target_pairs={{0,3},{1,0},{2,1},{3,2},{4,7},{5,4},{6,5},{7,6},{8,11},{9,8},{10,9... | collective-permute-start | bytes 884744 | tf_op jit(solution)/shard_map/ppermute | solution.py:27
  14.1 2.7 %collective-permute-start.1 = (bf16[192,768]{1,0:T(8,128)(2,1)S(1)}, bf16[192,768]{1,0:T(8,128)(2,1)S(1)}, u32[]{:S(2)}, u32[]{:S(2)}) collective-permute-start(bf16[192,768]{1,0:T(8,128)(2,1)S(1)} %fusion.11), channel_id=1, source_target_pairs={{0,2},{1,3},{2,0},{3,1},{4,6},{5,7},{6,4},{7,5},{8,10},{9,11},{10,... | collective-permute-start | bytes 884744 | tf_op jit(solution)/shard_map/ppermute | solution.py:27
  16.8 2.8 %collective-permute-start = (bf16[192,768]{1,0:T(8,128)(2,1)S(1)}, bf16[192,768]{1,0:T(8,128)(2,1)S(1)}, u32[]{:S(2)}, u32[]{:S(2)}) collective-permute-start(bf16[192,768]{1,0:T(8,128)(2,1)S(1)} %fusion.11), channel_id=1, source_target_pairs={{0,1},{1,2},{2,3},{3,0},{4,5},{5,6},{6,7},{7,4},{8,9},{9,10},{10,1... | collective-permute-start | bytes 884744 | tf_op jit(solution)/shard_map/ppermute | solution.py:27
  19.6 8.1 %collective-permute-start.4 = (bf16[64,512]{1,0:T(8,128)(2,1)S(1)}, bf16[64,512]{1,0:T(8,128)(2,1)S(1)}, u32[]{:S(2)}, u32[]{:S(2)}) collective-permute-start(bf16[64,512]{1,0:T(8,128)(2,1)S(1)} %copy-done.10), channel_id=1, source_target_pairs={{0,48},{1,49},{2,50},{3,51},{4,52},{5,53},{6,54},{7,55},{8,0},{9,1... | collective-permute-start | bytes 196616 | tf_op jit(solution)/shard_map/ppermute | solution.py:27
  27.7 0.0 collective-permute-done.3
  27.7 2.4 %collective-permute-start.5 = (bf16[64,512]{1,0:T(8,128)(2,1)S(1)}, bf16[64,512]{1,0:T(8,128)(2,1)S(1)}, u32[]{:S(2)}, u32[]{:S(2)}) collective-permute-start(bf16[64,512]{1,0:T(8,128)(2,1)S(1)} %copy-done.10), channel_id=1, source_target_pairs={{0,32},{1,33},{2,34},{3,35},{4,36},{5,37},{6,38},{7,39},{8,48},{9,... | collective-permute-start | bytes 196616 | tf_op jit(solution)/shard_map/ppermute | solution.py:27
  30.1 0.0 collective-permute-done.4
  30.1 4.4 %collective-permute-start.6 = (bf16[64,512]{1,0:T(8,128)(2,1)S(1)}, bf16[64,512]{1,0:T(8,128)(2,1)S(1)}, u32[]{:S(2)}, u32[]{:S(2)}) collective-permute-start(bf16[64,512]{1,0:T(8,128)(2,1)S(1)} %copy-done.10), channel_id=1, source_target_pairs={{0,16},{1,17},{2,18},{3,19},{4,20},{5,21},{6,22},{7,23},{8,32},{9,... | collective-permute-start | bytes 196616 | tf_op jit(solution)/shard_map/ppermute | solution.py:27
  34.5 0.4 collective-permute-done.5
  34.9 4.2 %collective-permute-done.6 = bf16[64,512]{1,0:T(8,128)(2,1)S(1)} collective-permute-done((bf16[64,512]{1,0:T(8,128)(2,1)S(1)}, bf16[64,512]{1,0:T(8,128)(2,1)S(1)}, u32[]{:S(2)}, u32[]{:S(2)}) %collective-permute-start.6) | collective-permute-done | bytes 65568 | tf_op jit(solution)/shard_map/ppermute | solution.py:27
  39.1 0.0 collective-permute-done.2
  39.2 0.0 collective-permute-done.1
  39.2 0.0 collective-permute-done
  39.2 0.1 pad_maximum_fusion.1.own
  39.3 0.0 all-gather.2.cloned.1.call-update
  39.3 1.6 broadcast_in_dim.4
  40.9 10.3 %all-to-all-start = ((bf16[8,256,512]{2,1,0:T(8,128)(2,1)}), bf16[8,256,512]{2,1,0:T(8,128)(2,1)}, u32[]{:S(2)}, u32[]{:S(2)}) async-start(bf16[8,256,512]{2,1,0:T(8,128)(2,1)} %broadcast_in_dim.4), calls=%async_computation | async-start | bytes 4194304 | tf_op jit(solution)/shard_map/all_to_all | solution.py:166
  51.2 0.1 fusion.22
  51.3 3.7 %collective-permute-start.8 = (bf16[384,768]{1,0:T(8,128)(2,1)S(1)}, bf16[384,768]{1,0:T(8,128)(2,1)S(1)}, u32[]{:S(2)}, u32[]{:S(2)}) collective-permute-start(bf16[384,768]{1,0:T(8,128)(2,1)S(1)} %get-tuple-element.20), channel_id=1, source_target_pairs={{0,52},{1,53},{2,54},{3,55},{4,0},{5,1},{6,2},{7,3},{8,60},{9,61},... | collective-permute-start | bytes 1769480 | tf_op jit(solution)/shard_map/ppermute | solution.py:27
  55.0 0.0 copy-start.9
  55.0 2.2 %collective-permute-start.7 = (bf16[384,768]{1,0:T(8,128)(2,1)S(1)}, bf16[384,768]{1,0:T(8,128)(2,1)S(1)}, u32[]{:S(2)}, u32[]{:S(2)}) collective-permute-start(bf16[384,768]{1,0:T(8,128)(2,1)S(1)} %get-tuple-element.19), channel_id=1, source_target_pairs={{0,4},{1,5},{2,6},{3,7},{4,16},{5,17},{6,18},{7,19},{8,12},{9,13},... | collective-permute-start | bytes 1769480 | tf_op jit(solution)/shard_map/ppermute | solution.py:27
  57.2 21.4 %collective-permute-done.8 = bf16[384,768]{1,0:T(8,128)(2,1)S(1)} collective-permute-done((bf16[384,768]{1,0:T(8,128)(2,1)S(1)}, bf16[384,768]{1,0:T(8,128)(2,1)S(1)}, u32[]{:S(2)}, u32[]{:S(2)}) %collective-permute-start.8) | collective-permute-done | bytes 589856 | tf_op jit(solution)/shard_map/ppermute | solution.py:27
  78.5 7.8 %collective-permute-done.7 = bf16[384,768]{1,0:T(8,128)(2,1)S(1)} collective-permute-done((bf16[384,768]{1,0:T(8,128)(2,1)S(1)}, bf16[384,768]{1,0:T(8,128)(2,1)S(1)}, u32[]{:S(2)}, u32[]{:S(2)}) %collective-permute-start.7) | collective-permute-done | bytes 589856 | tf_op jit(solution)/shard_map/ppermute | solution.py:27
  86.3 1.6 pad_maximum_fusion
  88.0 0.0 copy-done.5
  88.0 0.0 copy-done.7
  88.0 1.9 %collective-permute-start.9 = (bf16[1536,768]{1,0:T(8,128)(2,1)}, bf16[1536,768]{1,0:T(8,128)(2,1)}, u32[]{:S(2)}, u32[]{:S(2)}) collective-permute-start(bf16[1536,768]{1,0:T(8,128)(2,1)} %pad_maximum_fusion), channel_id=1, source_target_pairs={{0,8},{1,9},{2,10},{3,11},{4,12},{5,13},{6,14},{7,15},{8,0},{9,1},... | collective-permute-start | bytes 7077896 | tf_op jit(solution)/shard_map/ppermute | solution.py:27
  89.9 14.0 %all-to-all-done = bf16[8,256,512]{2,1,0:T(8,128)(2,1)} async-done(((bf16[8,256,512]{2,1,0:T(8,128)(2,1)}), bf16[8,256,512]{2,1,0:T(8,128)(2,1)}, u32[]{:S(2)}, u32[]{:S(2)}) %all-to-all-start) | async-done | bytes 2097184 | tf_op jit(solution)/shard_map/all_to_all | solution.py:166
  103.8 1.9 %collective-permute-start.10 = (bf16[2048,512]{1,0:T(8,128)(2,1)}, bf16[2048,512]{1,0:T(8,128)(2,1)}, u32[]{:S(2)}, u32[]{:S(2)}) collective-permute-start(bf16[2048,512]{1,0:T(8,128)(2,1)} %bitcast.5.mine), channel_id=1, source_target_pairs={{0,8},{1,9},{2,10},{3,11},{4,12},{5,13},{6,14},{7,15},{8,0},{9,1},... | collective-permute-start | bytes 6291464 | tf_op jit(solution)/shard_map/ppermute | solution.py:27
  105.8 0.9 copy.11.mask
  106.7 0.1 pad_add_fusion.pos
  106.8 0.0 collective-permute-done.9
  106.8 1.9 %fusion.21 = (bf16[768,768]{1,0:T(8,128)(2,1)S(1)}, bf16[768,768]{1,0:T(8,128)(2,1)S(1)}) fusion(bf16[1536,768]{1,0:T(8,128)(2,1)} %collective-permute-done.9), kind=kLoop, calls=%fused_computation.43 | loop fusion | bytes 4718592 | tf_op jit(solution)/shard_map/slice | solution.py:231
  108.7 0.2 copy-done.1
  109.0 2.1 %shard_map.55.outs = bf16[512,768]{1,0:T(8,128)(2,1)S(1)} custom-call(s32[4]{0:T(128)S(1)} %pad_add_fusion.pos, bf16[512,1536]{1,0:T(8,128)(2,1)S(1)} %copy-done.1, bf16[768,768]{1,0:T(8,128)(2,1)S(1)} %get-tuple-element.18.own, bf16[768,768]{1,0:T(8,128)(2,1)S(1)} %get-tuple-element.17.flipped), custom_call_target="tpu_custom_call" | custom-call | flops 1207959552 | bytes 4718592 | tf_op jit(solution)/shard_map/pallas_call | solution.py:65
  111.1 0.0 copy-start.2
  111.1 0.9 copy-done.2
  111.9 1.8 all-gather.2.cloned.1.call-done.acts
  113.7 4.2 %shard_map.56.first = f32[512,512]{1,0:T(8,128)S(1)} custom-call(s32[4]{0:T(128)S(1)} %pad_add_fusion.pos, bf16[512,4096]{1,0:T(8,128)(2,1)} %all-gather.2.cloned.1.call-done.acts, bf16[2048,512]{1,0:T(8,128)(2,1)} %bitcast.5.mine), custom_call_target="tpu_custom_call" | custom-call | flops 1073741824 | bytes 7340032 | tf_op jit(solution)/shard_map/pallas_call | solution.py:93
  117.9 0.0 collective-permute-done.10.other
  117.9 0.0 copy-done.4
  117.9 4.2 %shard_map.57.ins = bf16[512,512]{1,0:T(8,128)(2,1)S(1)} custom-call(s32[4]{0:T(128)S(1)} %pad_add_fusion.pos, bf16[512,4096]{1,0:T(8,128)(2,1)} %all-gather.2.cloned.1.call-done.acts, bf16[2048,512]{1,0:T(8,128)(2,1)} %collective-permute-done.10.other, f32[512,512]{1,0:T(8,128)S(1)} %shard_map.56.first, f32[512,1]{1,0:T(8,128)S(1)} %copy-done.4), custom_call_target="tpu_custom_call" | custom-call | flops 1073741824 | bytes 7864320 | tf_op jit(solution)/shard_map/pallas_call | solution.py:111
  122.1 0.0 copy-done.3
  122.1 0.0 copy-start.6
  122.1 0.0 copy-start.8
  122.2 1.5 shard_map.58
  123.7 1.9 %collective-permute-start.11 = (f32[768,512]{1,0:T(8,128)S(1)}, f32[768,512]{1,0:T(8,128)S(1)}, u32[]{:S(2)}, u32[]{:S(2)}) collective-permute-start(f32[768,512]{1,0:T(8,128)S(1)} %shard_map.58), channel_id=1, source_target_pairs={{0,8},{1,9},{2,10},{3,11},{4,12},{5,13},{6,14},{7,15},{8,0},{9,1},... | collective-permute-start | bytes 4718600 | tf_op jit(solution)/shard_map/ppermute | solution.py:27
  125.7 0.1 pad_maximum_fusion.2.flipped
  125.8 2.1 %shard_map.59.outs = bf16[512,768]{1,0:T(8,128)(2,1)S(1)} custom-call(s32[4]{0:T(128)S(1)} %pad_add_fusion.pos, bf16[512,1536]{1,0:T(8,128)(2,1)S(1)} %copy-done.1, bf16[768,768]{1,0:T(8,128)(2,1)S(1)} %pad_maximum_fusion.1.own, bf16[768,768]{1,0:T(8,128)(2,1)S(1)} %pad_maximum_fusion.2.flipped), custom_call_target="tpu_custom_call" | custom-call | flops 1207959552 | bytes 4718592 | tf_op jit(solution)/shard_map/pallas_call | solution.py:65
  127.9 1.5 shard_map.60
  129.4 0.0 collective-permute-done.11
  129.4 1.1 fusion.20
  131.2 0.2 multiply_convert_fusion
  131.5 0.2 concatenate.20
  131.6 42.3 %all_to_all.10 = f16[32,104,128]{2,1,0:T(8,128)(2,1)S(1)} all-to-all(f16[32,104,128]{2,1,0:T(8,128)(2,1)S(1)} %concatenate.20), channel_id=1, replica_groups={{0,16,32,48,64,80,96,112,128,144,160,176,192,208,224,240,256,272,288,30..., dimensions={0} | all-to-all | bytes 1703936 | tf_op jit(solution)/shard_map/all_to_all | solution.py:205
  174.0 0.1 copy.13
  174.1 0.2 multiply_reduce_fusion
  174.3 0.6 broadcast_multiply_fusion
  (24 shorter events, 0.1 us)
Async XLA Ops:
  6.5 1.1 copy-start
  6.5 107.2 %all-gather.2.cloned.1.call-start = ((), (), s32[]{:S(2)}) async-start(), calls=%async_computation.2 | async-start | bytes 4718592 | tf_op jit(solution)/shard_map/all_gather | solution.py:224
  7.6 1.1 copy-start.10
  8.7 19.0 %collective-permute-start.3 = (bf16[64,512]{1,0:T(8,128)(2,1)S(1)}, bf16[64,512]{1,0:T(8,128)(2,1)S(1)}, u32[]{:S(2)}, u32[]{:S(2)}) collective-permute-start(bf16[64,512]{1,0:T(8,128)(2,1)S(1)} %copy-done.10), channel_id=1, source_target_pairs={{0,0},{1,1},{2,2},{3,3},{4,4},{5,5},{6,6},{7,7},{8,16},{9,17},{10,... | collective-permute-start | bytes 196616 | tf_op jit(solution)/shard_map/ppermute | solution.py:27
  9.4 29.8 %collective-permute-start.2 = (bf16[192,768]{1,0:T(8,128)(2,1)S(1)}, bf16[192,768]{1,0:T(8,128)(2,1)S(1)}, u32[]{:S(2)}, u32[]{:S(2)}) collective-permute-start(bf16[192,768]{1,0:T(8,128)(2,1)S(1)} %fusion.11), channel_id=1, source_target_pairs={{0,3},{1,0},{2,1},{3,2},{4,7},{5,4},{6,5},{7,6},{8,11},{9,8},{10,9... | collective-permute-start | bytes 884744 | tf_op jit(solution)/shard_map/ppermute | solution.py:27
  14.1 25.1 %collective-permute-start.1 = (bf16[192,768]{1,0:T(8,128)(2,1)S(1)}, bf16[192,768]{1,0:T(8,128)(2,1)S(1)}, u32[]{:S(2)}, u32[]{:S(2)}) collective-permute-start(bf16[192,768]{1,0:T(8,128)(2,1)S(1)} %fusion.11), channel_id=1, source_target_pairs={{0,2},{1,3},{2,0},{3,1},{4,6},{5,7},{6,4},{7,5},{8,10},{9,11},{10,... | collective-permute-start | bytes 884744 | tf_op jit(solution)/shard_map/ppermute | solution.py:27
  16.8 22.4 %collective-permute-start = (bf16[192,768]{1,0:T(8,128)(2,1)S(1)}, bf16[192,768]{1,0:T(8,128)(2,1)S(1)}, u32[]{:S(2)}, u32[]{:S(2)}) collective-permute-start(bf16[192,768]{1,0:T(8,128)(2,1)S(1)} %fusion.11), channel_id=1, source_target_pairs={{0,1},{1,2},{2,3},{3,0},{4,5},{5,6},{6,7},{7,4},{8,9},{9,10},{10,1... | collective-permute-start | bytes 884744 | tf_op jit(solution)/shard_map/ppermute | solution.py:27
  19.6 10.5 %collective-permute-start.4 = (bf16[64,512]{1,0:T(8,128)(2,1)S(1)}, bf16[64,512]{1,0:T(8,128)(2,1)S(1)}, u32[]{:S(2)}, u32[]{:S(2)}) collective-permute-start(bf16[64,512]{1,0:T(8,128)(2,1)S(1)} %copy-done.10), channel_id=1, source_target_pairs={{0,48},{1,49},{2,50},{3,51},{4,52},{5,53},{6,54},{7,55},{8,0},{9,1... | collective-permute-start | bytes 196616 | tf_op jit(solution)/shard_map/ppermute | solution.py:27
  27.7 7.2 %collective-permute-start.5 = (bf16[64,512]{1,0:T(8,128)(2,1)S(1)}, bf16[64,512]{1,0:T(8,128)(2,1)S(1)}, u32[]{:S(2)}, u32[]{:S(2)}) collective-permute-start(bf16[64,512]{1,0:T(8,128)(2,1)S(1)} %copy-done.10), channel_id=1, source_target_pairs={{0,32},{1,33},{2,34},{3,35},{4,36},{5,37},{6,38},{7,39},{8,48},{9,... | collective-permute-start | bytes 196616 | tf_op jit(solution)/shard_map/ppermute | solution.py:27
  30.1 8.9 %collective-permute-start.6 = (bf16[64,512]{1,0:T(8,128)(2,1)S(1)}, bf16[64,512]{1,0:T(8,128)(2,1)S(1)}, u32[]{:S(2)}, u32[]{:S(2)}) collective-permute-start(bf16[64,512]{1,0:T(8,128)(2,1)S(1)} %copy-done.10), channel_id=1, source_target_pairs={{0,16},{1,17},{2,18},{3,19},{4,20},{5,21},{6,22},{7,23},{8,32},{9,... | collective-permute-start | bytes 196616 | tf_op jit(solution)/shard_map/ppermute | solution.py:27
  40.9 63.0 %all-to-all-start = ((bf16[8,256,512]{2,1,0:T(8,128)(2,1)}), bf16[8,256,512]{2,1,0:T(8,128)(2,1)}, u32[]{:S(2)}, u32[]{:S(2)}) async-start(bf16[8,256,512]{2,1,0:T(8,128)(2,1)} %broadcast_in_dim.4), calls=%async_computation | async-start | bytes 4194304 | tf_op jit(solution)/shard_map/all_to_all | solution.py:166
  51.3 27.2 %collective-permute-start.8 = (bf16[384,768]{1,0:T(8,128)(2,1)S(1)}, bf16[384,768]{1,0:T(8,128)(2,1)S(1)}, u32[]{:S(2)}, u32[]{:S(2)}) collective-permute-start(bf16[384,768]{1,0:T(8,128)(2,1)S(1)} %get-tuple-element.20), channel_id=1, source_target_pairs={{0,52},{1,53},{2,54},{3,55},{4,0},{5,1},{6,2},{7,3},{8,60},{9,61},... | collective-permute-start | bytes 1769480 | tf_op jit(solution)/shard_map/ppermute | solution.py:27
  55.0 50.8 %copy-start.9 = (s32[512]{0:T(512)S(1)}, s32[512]{0:T(512)}, u32[]{:S(2)}) copy-start(s32[512]{0:T(512)} %param.9) | copy-start | bytes 6148
  55.0 31.3 %collective-permute-start.7 = (bf16[384,768]{1,0:T(8,128)(2,1)S(1)}, bf16[384,768]{1,0:T(8,128)(2,1)S(1)}, u32[]{:S(2)}, u32[]{:S(2)}) collective-permute-start(bf16[384,768]{1,0:T(8,128)(2,1)S(1)} %get-tuple-element.19), channel_id=1, source_target_pairs={{0,4},{1,5},{2,6},{3,7},{4,16},{5,17},{6,18},{7,19},{8,12},{9,13},... | collective-permute-start | bytes 1769480 | tf_op jit(solution)/shard_map/ppermute | solution.py:27
  78.5 9.4 %copy-start.5 = (bf16[384,768]{1,0:T(8,128)(2,1)}, bf16[384,768]{1,0:T(8,128)(2,1)S(1)}, u32[]{:S(2)}) copy-start(bf16[384,768]{1,0:T(8,128)(2,1)S(1)} %collective-permute-done.8) | copy-start | bytes 1769476
  86.3 1.7 copy-start.7
  88.0 18.8 %collective-permute-start.9 = (bf16[1536,768]{1,0:T(8,128)(2,1)}, bf16[1536,768]{1,0:T(8,128)(2,1)}, u32[]{:S(2)}, u32[]{:S(2)}) collective-permute-start(bf16[1536,768]{1,0:T(8,128)(2,1)} %pad_maximum_fusion), channel_id=1, source_target_pairs={{0,8},{1,9},{2,10},{3,11},{4,12},{5,13},{6,14},{7,15},{8,0},{9,1},... | collective-permute-start | bytes 7077896 | tf_op jit(solution)/shard_map/ppermute | solution.py:27
  103.8 14.1 %collective-permute-start.10 = (bf16[2048,512]{1,0:T(8,128)(2,1)}, bf16[2048,512]{1,0:T(8,128)(2,1)}, u32[]{:S(2)}, u32[]{:S(2)}) collective-permute-start(bf16[2048,512]{1,0:T(8,128)(2,1)} %bitcast.5.mine), channel_id=1, source_target_pairs={{0,8},{1,9},{2,10},{3,11},{4,12},{5,13},{6,14},{7,15},{8,0},{9,1},... | collective-permute-start | bytes 6291464 | tf_op jit(solution)/shard_map/ppermute | solution.py:27
  106.8 2.2 %copy-start.1 = (bf16[512,1536]{1,0:T(8,128)(2,1)S(1)}, bf16[512,1536]{1,0:T(8,128)(2,1)}, u32[]{:S(2)}) copy-start(bf16[512,1536]{1,0:T(8,128)(2,1)} %grads.3) | copy-start | bytes 4718596
  111.1 0.9 copy-start.2
  113.7 4.2 %copy-start.4 = (f32[512,1]{1,0:T(8,128)S(1)}, f32[512,1]{1,0:T(8,128)}, u32[]{:S(2)}) copy-start(f32[512,1]{1,0:T(8,128)} %copy.11.mask) | copy-start | bytes 6148
  117.9 4.2 %copy-start.3 = (bf16[512,768]{1,0:T(8,128)(2,1)S(1)}, bf16[512,768]{1,0:T(8,128)(2,1)}, u32[]{:S(2)}) copy-start(bf16[512,768]{1,0:T(8,128)(2,1)} %copy-done.2) | copy-start | bytes 2359300
  122.1 3.5 %copy-start.6 = (bf16[384,768]{1,0:T(8,128)(2,1)S(1)}, bf16[384,768]{1,0:T(8,128)(2,1)}, u32[]{:S(2)}) copy-start(bf16[384,768]{1,0:T(8,128)(2,1)} %copy-done.5) | copy-start | bytes 1769476
  122.1 3.5 %copy-start.8 = (bf16[384,768]{1,0:T(8,128)(2,1)S(1)}, bf16[384,768]{1,0:T(8,128)(2,1)}, u32[]{:S(2)}) copy-start(bf16[384,768]{1,0:T(8,128)(2,1)} %copy-done.7) | copy-start | bytes 1769476
  123.7 5.7 %collective-permute-start.11 = (f32[768,512]{1,0:T(8,128)S(1)}, f32[768,512]{1,0:T(8,128)S(1)}, u32[]{:S(2)}, u32[]{:S(2)}) collective-permute-start(f32[768,512]{1,0:T(8,128)S(1)} %shard_map.58), channel_id=1, source_target_pairs={{0,8},{1,9},{2,10},{3,11},{4,12},{5,13},{6,14},{7,15},{8,0},{9,1},... | collective-permute-start | bytes 4718600 | tf_op jit(solution)/shard_map/ppermute | solution.py:27
Sparse Core Ops, SparseCore 0:
  39.4 74.2 all-gather.1

commit v6 on v4

--- a/solution.py
+++ b/solution.py
@@ -222,33 +222,32 @@
     sequences = activations.shape[0] // SEQ * lax.axis_size("wide")
 
     chunk = place_in_basis(in_basis, yh)
-    activations, chunk, picked = lax.optimization_barrier((activations, chunk, pick(out_basis, core)))
+    picked, chunk = lax.optimization_barrier((pick(out_basis, core), chunk))
     mine = gather_in_basis(chunk)
     basis_own = jnp.concatenate(from_x(picked), axis=0)
+    activations, basis_own = lax.optimization_barrier((activations, basis_own))
+    acts_pieces = from_x(activations)
     basis_flipped = other_yl(basis_own)
-    acts_pieces = from_x(activations)
-
-    top = jnp.max(jnp.abs(jnp.stack([jnp.max(jnp.abs(piece)) for piece in acts_pieces])))
-    depth = NX * activations.shape[1]
-    power = power_of(top.astype(F32) * (8.0 * depth))
-    power_theirs = flip_yl(jnp.broadcast_to(power, (8, 128)))[0, 0]
-    acts = arrange(pos, acts_pieces)
-    mine, acts, basis_flipped, power_theirs = lax.optimization_barrier((mine, acts, basis_flipped, power_theirs))
-
-    other = other_core(mine)
     basis = jnp.concatenate([basis_own, basis_flipped], axis=0)
     basis_other = other_core(basis)
     half = basis.shape[0] // 2
     out_mine = rotate_out(pos, out_grads, basis_own, basis_flipped)
     out_other = rotate_out(pos, out_grads, basis_other[:half], basis_other[half:])
-
+    acts = arrange(pos, acts_pieces)
+    top = jnp.max(jnp.abs(acts)).astype(F32)
+    power = power_of(top * (8.0 * NX * activations.shape[1]))
+    scale = jnp.exp2(14.0 - power)
+    mine, acts, scale = lax.optimization_barrier((mine, acts, scale))
+
+    other = other_core(mine)
     columns = mine.shape[1]
     width = columns // 2
+    label = jnp.broadcast_to(power, (8, width)).astype(F16)
     theirs = []
     for start in range(0, columns, width):
         given = partial(1, start, width, pos, acts, mine, other)
-        got = flip_yl((given * jnp.exp2(14.0 - power)).astype(F16))
-        theirs.append(got.astype(F32) * jnp.exp2(power_theirs - 14.0))
+        got = flip_yl(jnp.concatenate([(given * scale).astype(F16), label], axis=0))
+        theirs.append(got[:-8].astype(F32) * jnp.exp2(got[-8:-7, :1].astype(F32) - 14.0))
     rotated_in = partial(0, 0, columns, pos, acts, mine, other) + jnp.concatenate(theirs, axis=1)
     masked_in = rotated_in.astype(BF16) * valid.astype(BF16)[:, None]
     total = other_core(squares(pos, out_other, masked_in)) + squares(pos, out_mine, masked_in)

time: 189 us -> 191 us (1.011)
  the two profiles are of different devices: /device:TPU:48 before, /device:TPU:10 now
where the time goes in v6:
time: 191 us; the launch traced here: 190 us
  starting transfers between devices  65.9 us (35%)
  blocking collectives  37.8 us (20%)
  waiting for transfers between devices  31.7 us (17%)
  between operations  17 us (9%)
  Pallas kernels  15.7 us (8%)
  local copies, waits for them, and re-layouts  12.3 us (6%)
  other arithmetic  8.26 us (4%)
    ppermute x17, starting transfers between devices, send(): return lax.ppermute(value, BOTH, pairs)  65.9 us
    all_to_all x1, blocking collectives, scatter_sum(): lax.all_to_all(jnp.concatenate([coded, label], axis=1), 'wide', 0, 0, til...  37.8 us
    ppermute x17, waiting for transfers between devices, send(): return lax.ppermute(value, BOTH, pairs)  31.7 us
    pallas_call x3, Pallas kernels, partial(): call(functools.partial(partial_kernel, flip, start), jax.ShapeDtypeStruct...  7.49 us
    unnamed x36, local copies, waits for them, and re-layouts  7.33 us
    pallas_call x2, Pallas kernels, rotate_out(): call(rotate_out_kernel, jax.ShapeDtypeStruct((tokens, width), BF16), [plt...  4.18 us
  transfers between devices with their start and end apart: 18, of which 5 were waited for; matrix products, arithmetic and copies ran while one was open for 6% of the time, Pallas kernels for 7%

profile of v6, /device:TPU:10, one launch (start us, length us, event | category | flops | bytes accessed | tf_op | source)
XLA Modules:
  0.0 189.7 jit_solution(894859321730744514)
XLA Ops:
  6.5 10.9 %collective-permute-start = (bf16[64,512]{1,0:T(8,128)(2,1)}, bf16[64,512]{1,0:T(8,128)(2,1)S(1)}, u32[]{:S(2)}, u32[]{:S(2)}) collective-permute-start(bf16[64,512]{1,0:T(8,128)(2,1)} %param.7), channel_id=1, source_target_pairs={{0,0},{1,1},{2,2},{3,3},{4,256},{5,257},{6,258},{7,259},{8,16},{9,... | collective-permute-start | bytes 196616 | tf_op jit(solution)/shard_map/ppermute | solution.py:27
  17.5 5.6 %collective-permute-start.1 = (bf16[64,512]{1,0:T(8,128)(2,1)}, bf16[64,512]{1,0:T(8,128)(2,1)S(1)}, u32[]{:S(2)}, u32[]{:S(2)}) collective-permute-start(bf16[64,512]{1,0:T(8,128)(2,1)} %param.7), channel_id=1, source_target_pairs={{0,48},{1,49},{2,50},{3,51},{4,304},{5,305},{6,306},{7,307},{8,0},... | collective-permute-start | bytes 196616 | tf_op jit(solution)/shard_map/ppermute | solution.py:27
  23.1 8.8 %collective-permute-start.2 = (bf16[64,512]{1,0:T(8,128)(2,1)}, bf16[64,512]{1,0:T(8,128)(2,1)S(1)}, u32[]{:S(2)}, u32[]{:S(2)}) collective-permute-start(bf16[64,512]{1,0:T(8,128)(2,1)} %param.7), channel_id=1, source_target_pairs={{0,32},{1,33},{2,34},{3,35},{4,288},{5,289},{6,290},{7,291},{8,48}... | collective-permute-start | bytes 196616 | tf_op jit(solution)/shard_map/ppermute | solution.py:27
  31.9 1.9 %collective-permute-start.3 = (bf16[64,512]{1,0:T(8,128)(2,1)}, bf16[64,512]{1,0:T(8,128)(2,1)S(1)}, u32[]{:S(2)}, u32[]{:S(2)}) collective-permute-start(bf16[64,512]{1,0:T(8,128)(2,1)} %param.7), channel_id=1, source_target_pairs={{0,16},{1,17},{2,18},{3,19},{4,272},{5,273},{6,274},{7,275},{8,32}... | collective-permute-start | bytes 196616 | tf_op jit(solution)/shard_map/ppermute | solution.py:27
  33.9 1.1 fusion.11
  35.0 0.0 copy-start.6
  35.1 8.1 %collective-permute-done.3 = bf16[64,512]{1,0:T(8,128)(2,1)S(1)} collective-permute-done((bf16[64,512]{1,0:T(8,128)(2,1)}, bf16[64,512]{1,0:T(8,128)(2,1)S(1)}, u32[]{:S(2)}, u32[]{:S(2)}) %collective-permute-start.3) | collective-permute-done | bytes 65568 | tf_op jit(solution)/shard_map/ppermute | solution.py:27
  43.2 0.8 constant_dynamic-slice_fusion
  44.0 0.0 all-gather.2.cloned.1.call-update
  44.0 3.4 %collective-permute-start.4 = (bf16[192,768]{1,0:T(8,128)(2,1)S(1)}, bf16[192,768]{1,0:T(8,128)(2,1)S(1)}, u32[]{:S(2)}, u32[]{:S(2)}) collective-permute-start(bf16[192,768]{1,0:T(8,128)(2,1)S(1)} %fusion.11), channel_id=1, source_target_pairs={{0,1},{1,2},{2,3},{3,0},{4,5},{5,6},{6,7},{7,4},{8,9},{9,10},{10,1... | collective-permute-start | bytes 884744 | tf_op jit(solution)/shard_map/ppermute | solution.py:27
  47.4 3.0 %collective-permute-start.5 = (bf16[192,768]{1,0:T(8,128)(2,1)S(1)}, bf16[192,768]{1,0:T(8,128)(2,1)S(1)}, u32[]{:S(2)}, u32[]{:S(2)}) collective-permute-start(bf16[192,768]{1,0:T(8,128)(2,1)S(1)} %fusion.11), channel_id=1, source_target_pairs={{0,2},{1,3},{2,0},{3,1},{4,6},{5,7},{6,4},{7,5},{8,10},{9,11},{10,... | collective-permute-start | bytes 884744 | tf_op jit(solution)/shard_map/ppermute | solution.py:27
  50.4 4.1 %collective-permute-start.6 = (bf16[192,768]{1,0:T(8,128)(2,1)S(1)}, bf16[192,768]{1,0:T(8,128)(2,1)S(1)}, u32[]{:S(2)}, u32[]{:S(2)}) collective-permute-start(bf16[192,768]{1,0:T(8,128)(2,1)S(1)} %fusion.11), channel_id=1, source_target_pairs={{0,3},{1,0},{2,1},{3,2},{4,7},{5,4},{6,5},{7,6},{8,11},{9,8},{10,9... | collective-permute-start | bytes 884744 | tf_op jit(solution)/shard_map/ppermute | solution.py:27
  54.5 3.1 %collective-permute-done.5 = bf16[192,768]{1,0:T(8,128)(2,1)S(1)} collective-permute-done((bf16[192,768]{1,0:T(8,128)(2,1)S(1)}, bf16[192,768]{1,0:T(8,128)(2,1)S(1)}, u32[]{:S(2)}, u32[]{:S(2)}) %collective-permute-start.5) | collective-permute-done | bytes 294944 | tf_op jit(solution)/shard_map/ppermute | solution.py:27
  57.6 7.8 %collective-permute-done.6 = bf16[192,768]{1,0:T(8,128)(2,1)S(1)} collective-permute-done((bf16[192,768]{1,0:T(8,128)(2,1)S(1)}, bf16[192,768]{1,0:T(8,128)(2,1)S(1)}, u32[]{:S(2)}, u32[]{:S(2)}) %collective-permute-start.6) | collective-permute-done | bytes 294944 | tf_op jit(solution)/shard_map/ppermute | solution.py:27
  65.5 0.1 pad_maximum_fusion.1.own
  65.6 1.9 %collective-permute-start.10 = (bf16[512,512]{1,0:T(8,128)(2,1)S(1)}, bf16[512,512]{1,0:T(8,128)(2,1)S(1)}, u32[]{:S(2)}, u32[]{:S(2)}) collective-permute-start(bf16[512,512]{1,0:T(8,128)(2,1)S(1)} %copy-done.6), channel_id=1, source_target_pairs={{0,1},{1,2},{2,3},{3,0},{4,5},{5,6},{6,7},{7,4},{8,9},{9,10},{10,1... | collective-permute-start | bytes 1572872 | tf_op jit(solution)/shard_map/ppermute | solution.py:27
  67.5 3.5 %collective-permute-start.11 = (bf16[512,512]{1,0:T(8,128)(2,1)S(1)}, bf16[512,512]{1,0:T(8,128)(2,1)S(1)}, u32[]{:S(2)}, u32[]{:S(2)}) collective-permute-start(bf16[512,512]{1,0:T(8,128)(2,1)S(1)} %copy-done.6), channel_id=1, source_target_pairs={{0,2},{1,3},{2,0},{3,1},{4,6},{5,7},{6,4},{7,5},{8,10},{9,11},{10,... | collective-permute-start | bytes 1572872 | tf_op jit(solution)/shard_map/ppermute | solution.py:27
  71.0 4.5 %collective-permute-start.12 = (bf16[512,512]{1,0:T(8,128)(2,1)S(1)}, bf16[512,512]{1,0:T(8,128)(2,1)S(1)}, u32[]{:S(2)}, u32[]{:S(2)}) collective-permute-start(bf16[512,512]{1,0:T(8,128)(2,1)S(1)} %copy-done.6), channel_id=1, source_target_pairs={{0,3},{1,0},{2,1},{3,2},{4,7},{5,4},{6,5},{7,6},{8,11},{9,8},{10,9... | collective-permute-start | bytes 1572872 | tf_op jit(solution)/shard_map/ppermute | solution.py:27
  75.5 1.1 fusion.24
  76.6 1.9 %collective-permute-start.7 = (bf16[384,768]{1,0:T(8,128)(2,1)}, bf16[384,768]{1,0:T(8,128)(2,1)}, u32[]{:S(2)}, u32[]{:S(2)}) collective-permute-start(bf16[384,768]{1,0:T(8,128)(2,1)} %get-tuple-element.23), channel_id=1, source_target_pairs={{0,4},{1,5},{2,6},{3,7},{4,16},{5,17},{6,18},{7,19},{8,12},{9,13},... | collective-permute-start | bytes 1769480 | tf_op jit(solution)/shard_map/ppermute | solution.py:27
  78.5 3.9 %collective-permute-start.8 = (bf16[384,768]{1,0:T(8,128)(2,1)}, bf16[384,768]{1,0:T(8,128)(2,1)}, u32[]{:S(2)}, u32[]{:S(2)}) collective-permute-start(bf16[384,768]{1,0:T(8,128)(2,1)} %get-tuple-element.24), channel_id=1, source_target_pairs={{0,52},{1,53},{2,54},{3,55},{4,0},{5,1},{6,2},{7,3},{8,60},{9,61},... | collective-permute-start | bytes 1769480 | tf_op jit(solution)/shard_map/ppermute | solution.py:27
  82.5 0.1 pad_add_fusion.pos
  82.6 0.8 copy-done.7
  83.4 1.4 collective-permute-done.11.refs_2_
  84.7 0.8 copy-done.9
  85.5 11.3 %collective-permute-done.12.refs_3_ = bf16[512,512]{1,0:T(8,128)(2,1)S(1)} collective-permute-done((bf16[512,512]{1,0:T(8,128)(2,1)S(1)}, bf16[512,512]{1,0:T(8,128)(2,1)S(1)}, u32[]{:S(2)}, u32[]{:S(2)}) %collective-permute-start.12) | collective-permute-done | bytes 524320 | tf_op jit(solution)/shard_map/ppermute | solution.py:27
  96.8 0.8 copy-done.11
  97.7 1.0 copy-done.8
  98.7 1.0 copy-done.10
  99.8 1.0 copy-done.12
  100.8 0.8 shard_map.56.acts
  101.6 1.0 abs_reduce_fusion
  103.4 0.0 all-gather.2.cloned.1.call-done.mine
  103.4 2.2 %collective-permute-start.13 = (bf16[2048,512]{1,0:T(8,128)(2,1)}, bf16[2048,512]{1,0:T(8,128)(2,1)}, u32[]{:S(2)}, u32[]{:S(2)}) collective-permute-start(bf16[2048,512]{1,0:T(8,128)(2,1)} %all-gather.2.cloned.1.call-done.mine), channel_id=1, source_target_pairs={{0,8},{1,9},{2,10},{3,11},{4,12},{5,13},{6,14},{7,15},{8,0},{9,1},... | collective-permute-start | bytes 6291464 | tf_op jit(solution)/shard_map/ppermute | solution.py:27
  105.7 3.2 %pad_maximum_fusion = bf16[1536,768]{1,0:T(8,128)(2,1)} fusion(bf16[384,768]{1,0:T(8,128)(2,1)} %collective-permute-done.8, bf16[384,768]{1,0:T(8,128)(2,1)} %collective-permute-done.7, bf16[768,768]{1,0:T(8,128)(2,1)} %copy-done.1), kind=kLoop, calls=%fused_computation.2 | loop fusion | flops 7077888 | bytes 4718592 | tf_op jit(solution)/shard_map/concatenate | solution.py:231
  108.9 2.1 %collective-permute-start.9 = (bf16[1536,768]{1,0:T(8,128)(2,1)}, bf16[1536,768]{1,0:T(8,128)(2,1)}, u32[]{:S(2)}, u32[]{:S(2)}) collective-permute-start(bf16[1536,768]{1,0:T(8,128)(2,1)} %pad_maximum_fusion), channel_id=1, source_target_pairs={{0,8},{1,9},{2,10},{3,11},{4,12},{5,13},{6,14},{7,15},{8,0},{9,1},... | collective-permute-start | bytes 7077896 | tf_op jit(solution)/shard_map/ppermute | solution.py:27
  111.1 1.6 copy-done.3
  112.6 2.3 %shard_map.58 = f32[512,256]{1,0:T(8,128)S(1)} custom-call(s32[4]{0:T(128)S(1)} %pad_add_fusion.pos, bf16[2,512,1024]{2,1,0:T(8,128)(2,1)S(1)} %shard_map.56.acts, bf16[2048,512]{1,0:T(8,128)(2,1)S(1)} %copy-done.3, bf16[2048,512]{1,0:T(8,128)(2,1)} %collective-permute-done.13.other), custom_call_target="tpu_custom_call" | custom-call | flops 536870912 | bytes 3670016 | tf_op jit(solution)/shard_map/pallas_call | solution.py:112
  115.0 0.1 multiply_convert_fusion.2
  115.0 0.1 concatenate.28
  115.1 1.9 %collective-permute-start.14 = (f16[520,256]{1,0:T(8,128)(2,1)S(1)}, f16[520,256]{1,0:T(8,128)(2,1)S(1)}, u32[]{:S(2)}, u32[]{:S(2)}) collective-permute-start(f16[520,256]{1,0:T(8,128)(2,1)S(1)} %concatenate.28), channel_id=1, source_target_pairs={{0,4},{1,5},{2,6},{3,7},{4,0},{5,1},{6,2},{7,3},{8,12},{9,13},{10,... | collective-permute-start | bytes 798728 | tf_op jit(solution)/shard_map/ppermute | solution.py:27
  117.0 2.3 %shard_map.59 = f32[512,256]{1,0:T(8,128)S(1)} custom-call(s32[4]{0:T(128)S(1)} %pad_add_fusion.pos, bf16[2,512,1024]{2,1,0:T(8,128)(2,1)S(1)} %shard_map.56.acts, bf16[2048,512]{1,0:T(8,128)(2,1)S(1)} %copy-done.3, bf16[2048,512]{1,0:T(8,128)(2,1)} %collective-permute-done.13.other), custom_call_target="tpu_custom_call" | custom-call | flops 536870912 | bytes 3670016 | tf_op jit(solution)/shard_map/pallas_call | solution.py:112
  119.3 0.1 multiply_convert_fusion.1
  119.4 0.1 concatenate.29
  119.5 0.0 copy-start.5
  119.5 4.1 %collective-permute-start.15 = (f16[520,256]{1,0:T(8,128)(2,1)S(1)}, f16[520,256]{1,0:T(8,128)(2,1)S(1)}, u32[]{:S(2)}, u32[]{:S(2)}) collective-permute-start(f16[520,256]{1,0:T(8,128)(2,1)S(1)} %concatenate.29), channel_id=1, source_target_pairs={{0,4},{1,5},{2,6},{3,7},{4,0},{5,1},{6,2},{7,3},{8,12},{9,13},{10,... | collective-permute-start | bytes 798728 | tf_op jit(solution)/shard_map/ppermute | solution.py:27
  123.5 1.8 fusion.23
  125.3 2.1 %shard_map.55.outs = bf16[512,768]{1,0:T(8,128)(2,1)S(1)} custom-call(s32[4]{0:T(128)S(1)} %pad_add_fusion.pos, bf16[512,1536]{1,0:T(8,128)(2,1)S(1)} %copy-done.5, bf16[768,768]{1,0:T(8,128)(2,1)S(1)} %get-tuple-element.22.own, bf16[768,768]{1,0:T(8,128)(2,1)S(1)} %get-tuple-element.21.flipped), custom_call_target="tpu_custom_call" | custom-call | flops 1207959552 | bytes 4718592 | tf_op jit(solution)/shard_map/pallas_call | solution.py:65
  127.5 2.9 %shard_map.57 = f32[512,512]{1,0:T(8,128)S(1)} custom-call(s32[4]{0:T(128)S(1)} %pad_add_fusion.pos, bf16[2,512,1024]{2,1,0:T(8,128)(2,1)S(1)} %shard_map.56.acts, bf16[2048,512]{1,0:T(8,128)(2,1)S(1)} %copy-done.4, bf16[2048,512]{1,0:T(8,128)(2,1)} %collective-permute-done.13.other), custom_call_target="tpu_custom_call" | custom-call | flops 1073741824 | bytes 5242880 | tf_op jit(solution)/shard_map/pallas_call | solution.py:112
  130.3 0.5 slice.43
  131.6 0.5 slice.45
  132.9 0.2 fusion.13.ins
  133.1 1.6 shard_map.60
  134.7 2.1 %collective-permute-start.16 = (f32[768,512]{1,0:T(8,128)S(1)}, f32[768,512]{1,0:T(8,128)S(1)}, u32[]{:S(2)}, u32[]{:S(2)}) collective-permute-start(f32[768,512]{1,0:T(8,128)S(1)} %shard_map.60), channel_id=1, source_target_pairs={{0,8},{1,9},{2,10},{3,11},{4,12},{5,13},{6,14},{7,15},{8,0},{9,1},... | collective-permute-start | bytes 4718600 | tf_op jit(solution)/shard_map/ppermute | solution.py:27
  136.8 1.3 pad_maximum_fusion.2.flipped
  138.1 2.1 %shard_map.61.outs = bf16[512,768]{1,0:T(8,128)(2,1)S(1)} custom-call(s32[4]{0:T(128)S(1)} %pad_add_fusion.pos, bf16[512,1536]{1,0:T(8,128)(2,1)S(1)} %copy-done.5, bf16[768,768]{1,0:T(8,128)(2,1)S(1)} %copy-done.2, bf16[768,768]{1,0:T(8,128)(2,1)S(1)} %pad_maximum_fusion.2.flipped), custom_call_target="tpu_custom_call" | custom-call | flops 1207959552 | bytes 4718592 | tf_op jit(solution)/shard_map/pallas_call | solution.py:65
  140.2 1.6 shard_map.62
  141.8 1.1 fusion.22
  143.6 0.2 multiply_convert_fusion
  143.9 0.2 concatenate.32
  144.0 37.8 %all_to_all.5 = f16[32,104,128]{2,1,0:T(8,128)(2,1)S(1)} all-to-all(f16[32,104,128]{2,1,0:T(8,128)(2,1)S(1)} %concatenate.32), channel_id=1, replica_groups={{0,16,32,48,64,80,96,112,128,144,160,176,192,208,224,240,256,272,288,30..., dimensions={0} | all-to-all | bytes 1703936 | tf_op jit(solution)/shard_map/all_to_all | solution.py:209
  181.9 0.1 copy.8
  182.0 0.2 multiply_reduce_fusion
  182.2 0.6 broadcast_multiply_fusion
  (48 shorter events, 0.3 us)
Async XLA Ops:
  6.5 27.3 %copy-start = (bf16[192,1536]{1,0:T(8,128)(2,1)S(1)}, bf16[192,1536]{1,0:T(8,128)(2,1)}, u32[]{:S(2)}) copy-start(bf16[192,1536]{1,0:T(8,128)(2,1)} %param.8) | copy-start | bytes 1769476
  6.5 96.9 %all-gather.2.cloned.1.call-start = ((), (), s32[]{:S(2)}) async-start(), calls=%async_computation.1 | async-start | bytes 2359296 | tf_op jit(solution)/shard_map/all_gather | solution.py:166
  6.5 28.5 %collective-permute-start = (bf16[64,512]{1,0:T(8,128)(2,1)}, bf16[64,512]{1,0:T(8,128)(2,1)S(1)}, u32[]{:S(2)}, u32[]{:S(2)}) collective-permute-start(bf16[64,512]{1,0:T(8,128)(2,1)} %param.7), channel_id=1, source_target_pairs={{0,0},{1,1},{2,2},{3,3},{4,256},{5,257},{6,258},{7,259},{8,16},{9,... | collective-permute-start | bytes 196616 | tf_op jit(solution)/shard_map/ppermute | solution.py:27
  17.5 17.6 %collective-permute-start.1 = (bf16[64,512]{1,0:T(8,128)(2,1)}, bf16[64,512]{1,0:T(8,128)(2,1)S(1)}, u32[]{:S(2)}, u32[]{:S(2)}) collective-permute-start(bf16[64,512]{1,0:T(8,128)(2,1)} %param.7), channel_id=1, source_target_pairs={{0,48},{1,49},{2,50},{3,51},{4,304},{5,305},{6,306},{7,307},{8,0},... | collective-permute-start | bytes 196616 | tf_op jit(solution)/shard_map/ppermute | solution.py:27
  23.1 12.0 %collective-permute-start.2 = (bf16[64,512]{1,0:T(8,128)(2,1)}, bf16[64,512]{1,0:T(8,128)(2,1)S(1)}, u32[]{:S(2)}, u32[]{:S(2)}) collective-permute-start(bf16[64,512]{1,0:T(8,128)(2,1)} %param.7), channel_id=1, source_target_pairs={{0,32},{1,33},{2,34},{3,35},{4,288},{5,289},{6,290},{7,291},{8,48}... | collective-permute-start | bytes 196616 | tf_op jit(solution)/shard_map/ppermute | solution.py:27
  31.9 11.3 %collective-permute-start.3 = (bf16[64,512]{1,0:T(8,128)(2,1)}, bf16[64,512]{1,0:T(8,128)(2,1)S(1)}, u32[]{:S(2)}, u32[]{:S(2)}) collective-permute-start(bf16[64,512]{1,0:T(8,128)(2,1)} %param.7), channel_id=1, source_target_pairs={{0,16},{1,17},{2,18},{3,19},{4,272},{5,273},{6,274},{7,275},{8,32}... | collective-permute-start | bytes 196616 | tf_op jit(solution)/shard_map/ppermute | solution.py:27
  35.0 30.5 %copy-start.6 = (bf16[512,512]{1,0:T(8,128)(2,1)S(1)}, bf16[512,512]{1,0:T(8,128)(2,1)}, u32[]{:S(2)}) copy-start(bf16[512,512]{1,0:T(8,128)(2,1)} %refs_0_) | copy-start | bytes 1572868
  44.0 10.5 %collective-permute-start.4 = (bf16[192,768]{1,0:T(8,128)(2,1)S(1)}, bf16[192,768]{1,0:T(8,128)(2,1)S(1)}, u32[]{:S(2)}, u32[]{:S(2)}) collective-permute-start(bf16[192,768]{1,0:T(8,128)(2,1)S(1)} %fusion.11), channel_id=1, source_target_pairs={{0,1},{1,2},{2,3},{3,0},{4,5},{5,6},{6,7},{7,4},{8,9},{9,10},{10,1... | collective-permute-start | bytes 884744 | tf_op jit(solution)/shard_map/ppermute | solution.py:27
  47.4 10.2 %collective-permute-start.5 = (bf16[192,768]{1,0:T(8,128)(2,1)S(1)}, bf16[192,768]{1,0:T(8,128)(2,1)S(1)}, u32[]{:S(2)}, u32[]{:S(2)}) collective-permute-start(bf16[192,768]{1,0:T(8,128)(2,1)S(1)} %fusion.11), channel_id=1, source_target_pairs={{0,2},{1,3},{2,0},{3,1},{4,6},{5,7},{6,4},{7,5},{8,10},{9,11},{10,... | collective-permute-start | bytes 884744 | tf_op jit(solution)/shard_map/ppermute | solution.py:27
  50.4 15.0 %collective-permute-start.6 = (bf16[192,768]{1,0:T(8,128)(2,1)S(1)}, bf16[192,768]{1,0:T(8,128)(2,1)S(1)}, u32[]{:S(2)}, u32[]{:S(2)}) collective-permute-start(bf16[192,768]{1,0:T(8,128)(2,1)S(1)} %fusion.11), channel_id=1, source_target_pairs={{0,3},{1,0},{2,1},{3,2},{4,7},{5,4},{6,5},{7,6},{8,11},{9,8},{10,9... | collective-permute-start | bytes 884744 | tf_op jit(solution)/shard_map/ppermute | solution.py:27
  65.6 9.9 %copy-start.1 = (bf16[768,768]{1,0:T(8,128)(2,1)}, bf16[768,768]{1,0:T(8,128)(2,1)S(1)}, u32[]{:S(2)}) copy-start(bf16[768,768]{1,0:T(8,128)(2,1)S(1)} %pad_maximum_fusion.1.own) | copy-start | bytes 3538948
  65.6 17.0 %collective-permute-start.10 = (bf16[512,512]{1,0:T(8,128)(2,1)S(1)}, bf16[512,512]{1,0:T(8,128)(2,1)S(1)}, u32[]{:S(2)}, u32[]{:S(2)}) collective-permute-start(bf16[512,512]{1,0:T(8,128)(2,1)S(1)} %copy-done.6), channel_id=1, source_target_pairs={{0,1},{1,2},{2,3},{3,0},{4,5},{5,6},{6,7},{7,4},{8,9},{9,10},{10,1... | collective-permute-start | bytes 1572872 | tf_op jit(solution)/shard_map/ppermute | solution.py:27
  67.5 17.2 %collective-permute-start.11 = (bf16[512,512]{1,0:T(8,128)(2,1)S(1)}, bf16[512,512]{1,0:T(8,128)(2,1)S(1)}, u32[]{:S(2)}, u32[]{:S(2)}) collective-permute-start(bf16[512,512]{1,0:T(8,128)(2,1)S(1)} %copy-done.6), channel_id=1, source_target_pairs={{0,2},{1,3},{2,0},{3,1},{4,6},{5,7},{6,4},{7,5},{8,10},{9,11},{10,... | collective-permute-start | bytes 1572872 | tf_op jit(solution)/shard_map/ppermute | solution.py:27
  71.0 25.9 %collective-permute-start.12 = (bf16[512,512]{1,0:T(8,128)(2,1)S(1)}, bf16[512,512]{1,0:T(8,128)(2,1)S(1)}, u32[]{:S(2)}, u32[]{:S(2)}) collective-permute-start(bf16[512,512]{1,0:T(8,128)(2,1)S(1)} %copy-done.6), channel_id=1, source_target_pairs={{0,3},{1,0},{2,1},{3,2},{4,7},{5,4},{6,5},{7,6},{8,11},{9,8},{10,9... | collective-permute-start | bytes 1572872 | tf_op jit(solution)/shard_map/ppermute | solution.py:27
  76.6 29.1 %collective-permute-start.7 = (bf16[384,768]{1,0:T(8,128)(2,1)}, bf16[384,768]{1,0:T(8,128)(2,1)}, u32[]{:S(2)}, u32[]{:S(2)}) collective-permute-start(bf16[384,768]{1,0:T(8,128)(2,1)} %get-tuple-element.23), channel_id=1, source_target_pairs={{0,4},{1,5},{2,6},{3,7},{4,16},{5,17},{6,18},{7,19},{8,12},{9,13},... | collective-permute-start | bytes 1769480 | tf_op jit(solution)/shard_map/ppermute | solution.py:27
  78.5 27.2 %collective-permute-start.8 = (bf16[384,768]{1,0:T(8,128)(2,1)}, bf16[384,768]{1,0:T(8,128)(2,1)}, u32[]{:S(2)}, u32[]{:S(2)}) collective-permute-start(bf16[384,768]{1,0:T(8,128)(2,1)} %get-tuple-element.24), channel_id=1, source_target_pairs={{0,52},{1,53},{2,54},{3,55},{4,0},{5,1},{6,2},{7,3},{8,60},{9,61},... | collective-permute-start | bytes 1769480 | tf_op jit(solution)/shard_map/ppermute | solution.py:27
  82.6 0.8 copy-start.7
  84.7 0.8 copy-start.9
  96.8 0.8 copy-start.11
  97.7 1.0 copy-start.8
  98.7 1.0 copy-start.10
  99.8 1.0 copy-start.12
  103.4 7.6 %copy-start.13 = (s32[512]{0:T(512)S(1)}, s32[512]{0:T(512)}, u32[]{:S(2)}) copy-start(s32[512]{0:T(512)} %param.9) | copy-start | bytes 6148
  103.4 7.6 %collective-permute-start.13 = (bf16[2048,512]{1,0:T(8,128)(2,1)}, bf16[2048,512]{1,0:T(8,128)(2,1)}, u32[]{:S(2)}, u32[]{:S(2)}) collective-permute-start(bf16[2048,512]{1,0:T(8,128)(2,1)} %all-gather.2.cloned.1.call-done.mine), channel_id=1, source_target_pairs={{0,8},{1,9},{2,10},{3,11},{4,12},{5,13},{6,14},{7,15},{8,0},{9,1},... | collective-permute-start | bytes 6291464 | tf_op jit(solution)/shard_map/ppermute | solution.py:27
  108.9 14.6 %collective-permute-start.9 = (bf16[1536,768]{1,0:T(8,128)(2,1)}, bf16[1536,768]{1,0:T(8,128)(2,1)}, u32[]{:S(2)}, u32[]{:S(2)}) collective-permute-start(bf16[1536,768]{1,0:T(8,128)(2,1)} %pad_maximum_fusion), channel_id=1, source_target_pairs={{0,8},{1,9},{2,10},{3,11},{4,12},{5,13},{6,14},{7,15},{8,0},{9,1},... | collective-permute-start | bytes 7077896 | tf_op jit(solution)/shard_map/ppermute | solution.py:27
  111.0 1.6 copy-start.3
  115.1 15.2 %collective-permute-start.14 = (f16[520,256]{1,0:T(8,128)(2,1)S(1)}, f16[520,256]{1,0:T(8,128)(2,1)S(1)}, u32[]{:S(2)}, u32[]{:S(2)}) collective-permute-start(f16[520,256]{1,0:T(8,128)(2,1)S(1)} %concatenate.28), channel_id=1, source_target_pairs={{0,4},{1,5},{2,6},{3,7},{4,0},{5,1},{6,2},{7,3},{8,12},{9,13},{10,... | collective-permute-start | bytes 798728 | tf_op jit(solution)/shard_map/ppermute | solution.py:27
  119.5 5.9 %copy-start.5 = (bf16[512,1536]{1,0:T(8,128)(2,1)S(1)}, bf16[512,1536]{1,0:T(8,128)(2,1)}, u32[]{:S(2)}) copy-start(bf16[512,1536]{1,0:T(8,128)(2,1)} %grads.3) | copy-start | bytes 4718596
  119.5 12.1 %collective-permute-start.15 = (f16[520,256]{1,0:T(8,128)(2,1)S(1)}, f16[520,256]{1,0:T(8,128)(2,1)S(1)}, u32[]{:S(2)}, u32[]{:S(2)}) collective-permute-start(f16[520,256]{1,0:T(8,128)(2,1)S(1)} %concatenate.29), channel_id=1, source_target_pairs={{0,4},{1,5},{2,6},{3,7},{4,0},{5,1},{6,2},{7,3},{8,12},{9,13},{10,... | collective-permute-start | bytes 798728 | tf_op jit(solution)/shard_map/ppermute | solution.py:27
  125.3 2.1 %copy-start.4 = (bf16[2048,512]{1,0:T(8,128)(2,1)S(1)}, bf16[2048,512]{1,0:T(8,128)(2,1)}, u32[]{:S(2)}) copy-start(bf16[2048,512]{1,0:T(8,128)(2,1)} %all-gather.2.cloned.1.call-done.mine) | copy-start | bytes 6291460
  133.1 5.0 %copy-start.2 = (bf16[768,768]{1,0:T(8,128)(2,1)S(1)}, bf16[768,768]{1,0:T(8,128)(2,1)}, u32[]{:S(2)}) copy-start(bf16[768,768]{1,0:T(8,128)(2,1)} %copy-done.1) | copy-start | bytes 3538948
  134.7 7.1 %collective-permute-start.16 = (f32[768,512]{1,0:T(8,128)S(1)}, f32[768,512]{1,0:T(8,128)S(1)}, u32[]{:S(2)}, u32[]{:S(2)}) collective-permute-start(f32[768,512]{1,0:T(8,128)S(1)} %shard_map.60), channel_id=1, source_target_pairs={{0,8},{1,9},{2,10},{3,11},{4,12},{5,13},{6,14},{7,15},{8,0},{9,1},... | collective-permute-start | bytes 4718600 | tf_op jit(solution)/shard_map/ppermute | solution.py:27
Sparse Core Ops, SparseCore 0:
  44.1 43.3 all-gather.1

commit v7 on v1

v7 whole, which is shorter than its diff:
```python
import functools

import jax
import jax.numpy as jnp
import numpy as np
from jax import lax
from jax.experimental import pallas as pl
from jax.experimental.pallas import tpu as pltpu
from jax.sharding import PartitionSpec as P

SEQ = 128
NZ, NYH, NC, NYL, NX = 8, 4, 2, 2, 4
BOTH = ("wide", "narrow")
F32, BF16, F16 = jnp.float32, jnp.bfloat16, jnp.float16
VMEM = pl.BlockSpec(memory_space=pltpu.VMEM)
SMEM = pl.BlockSpec(memory_space=pltpu.SMEM)
LIMIT = 48 * 1024 * 1024


def send(value, target):
    pairs = []
    for z, yh, c, yl, x in np.ndindex(NZ, NYH, NC, NYL, NX):
        z2, yh2, c2, yl2, x2 = target(z, yh, c, yl, x)
        z2, yh2, c2, yl2, x2 = z2 % NZ, yh2 % NYH, c2 % NC, yl2 % NYL, x2 % NX
        source = (((z * NYH + yh) * NC + c) * NYL + yl) * NX + x
        pairs.append((source, (((z2 * NYH + yh2) * NC + c2) * NYL + yl2) * NX + x2))
    return lax.ppermute(value, BOTH, pairs)


def other_core(value):
    return send(value, lambda z, yh, c, yl, x: (z, yh, c + 1, yl, x))


def cost(flops, nbytes):
    return pl.CostEstimate(flops=flops, bytes_accessed=nbytes, transcendentals=0)


def call(kernel, out, scratch, flops, nbytes, n_vmem):
    return pl.pallas_call(
        kernel,
        out_shape=out,
        in_specs=[SMEM] + [VMEM] * n_vmem,
        out_specs=VMEM,
        scratch_shapes=scratch,
        compiler_params=pltpu.CompilerParams(vmem_limit_bytes=LIMIT),
        cost_estimate=cost(flops, nbytes),
    )


def rotate_out_kernel(pos, grads, packed, out, basis):
    parts = NYL * NX
    rows, stride = basis.shape[0] // parts, packed.shape[0] // parts
    wide = packed.shape[1]
    for n in range(parts):
        at, half = n * stride, rows // 2
        basis[n * rows : (n + 1) * rows, :wide] = packed[at : at + rows, :]
        for h in range(2):
            basis[n * rows + h * half : n * rows + (h + 1) * half, wide:] = packed[
                at + rows : at + stride, h * wide // 2 : (h + 1) * wide // 2
            ]
    width = 256
    for j in range(out.shape[1] // width):
        cols = slice(j * width, (j + 1) * width)
        out[:, cols] = jnp.dot(grads[...], basis[:, cols], preferred_element_type=F32).astype(out.dtype)


def rotate_out(pos, grads, packed):
    tokens, depth = grads.shape
    width = depth // NC
    return call(
        rotate_out_kernel,
        jax.ShapeDtypeStruct((tokens, width), BF16),
        [pltpu.VMEM((depth, width), BF16)],
        2 * tokens * depth * width,
        2 * (tokens * depth + depth * width + tokens * width),
        2,
    )(pos, grads, packed)


def rotate_in_kernel(pos, gathered, mine, other, mask, out, basis):
    core = pos[3]
    blocks = NZ * NYH
    rows = mine.shape[0] // blocks
    for i in range(blocks):
        for ref, c in ((mine, core), (other, 1 - core)):
            at = pl.multiple_of((i * NC + c) * rows, rows)
            basis[pl.ds(at, rows), :] = ref[i * rows : (i + 1) * rows, :]
    parts = NYL * NX
    stride, depth = gathered.shape[0] // parts, gathered.shape[1]
    half = out.shape[0] // 2
    for part in range(2):
        total = jnp.zeros((half, out.shape[1]), F32)
        for n in range(parts):
            at = n * stride + part * half
            total += jnp.dot(
                gathered[at : at + half, :], basis[n * depth : (n + 1) * depth, :], preferred_element_type=F32
            )
        here = slice(part * half, (part + 1) * half)
        out[here, :] = (total.astype(BF16).astype(F32) * mask[here, :]).astype(BF16)


def rotate_in(pos, gathered, mine, other, mask):
    tokens = mask.shape[0]
    depth, width = 2 * mine.shape[0], mine.shape[1]
    return call(
        rotate_in_kernel,
        jax.ShapeDtypeStruct((tokens, width), BF16),
        [pltpu.VMEM((depth, width), BF16)],
        2 * tokens * depth * width,
        2 * (tokens * depth + depth * width + tokens * width),
        4,
    )(pos, gathered, mine, other, mask)


def squares_kernel(pos, outs, ins, out):
    width = 256
    for j in range(out.shape[0] // width):
        cols = slice(j * width, (j + 1) * width)
        total = None
        for s in range(outs.shape[0] // SEQ):
            rows = slice(s * SEQ, (s + 1) * SEQ)
            grad = lax.dot_general(
                outs[rows, cols], ins[rows, :], (((0,), (0,)), ((), ())), preferred_element_type=F32
            )
            total = grad * grad if total is None else total + grad * grad
        out[cols, :] = total


def squares(pos, outs, ins):
    tokens, width = outs.shape
    return call(
        squares_kernel,
        jax.ShapeDtypeStruct((width, ins.shape[1]), F32),
        [],
        2 * tokens * width * ins.shape[1],
        2 * tokens * (width + ins.shape[1]) + 4 * width * ins.shape[1],
        2,
    )(pos, outs, ins)


def gather_in_basis(in_basis):
    along_yh = [[(z * NYH + yh) * NC + c for yh in range(NYH)] for z in range(NZ) for c in range(NC)]
    along_z = [[z * NYH * NC + r for z in range(NZ)] for r in range(NYH * NC)]
    chunk = lax.all_gather(in_basis, "wide", axis=0, tiled=True, axis_index_groups=along_yh)
    copies = jnp.broadcast_to(chunk[None], (NZ, *chunk.shape))
    return lax.all_to_all(copies, "wide", 0, 0, axis_index_groups=along_z).reshape(-1, chunk.shape[1])


def gather_packed(activations, picked):
    width = activations.shape[1]
    half = picked.shape[0] // 2
    rest = jnp.concatenate([picked[:half, width:], picked[half:, width:]], axis=1)
    packed = jnp.concatenate([activations, picked[:, :width], rest], axis=0)
    return lax.all_gather(packed, "narrow", axis=0, tiled=True)


def power_of(top):
    return jnp.maximum(jnp.floor(jnp.log2(jnp.maximum(top, 1e-30))), -100.0)


def pick(out_basis, core):
    width = out_basis.shape[1]
    own = width // (NZ * NYH * NC)
    source = lax.broadcasted_iota(jnp.int32, (width, width // NC), 0)
    place = lax.broadcasted_iota(jnp.int32, (width, width // NC), 1)
    wanted = ((place // own) * NC + core) * own + place % own
    return jnp.dot(out_basis, (source == wanted).astype(BF16), preferred_element_type=F32).astype(BF16)


def scatter_sum(total):
    blocks = NZ * NYH
    groups = [[zy * NC + c for zy in range(blocks)] for c in range(NC)]
    rows, columns = total.shape[0] // blocks, total.shape[1]
    tiles = (rows // 8, columns // 128)
    power = power_of(jnp.max(total))
    coded = (total * jnp.exp2(14.0 - power)).astype(F16)
    coded = coded.reshape(blocks, tiles[0], 8, tiles[1], 128).transpose(0, 1, 3, 2, 4).reshape(blocks, -1, 128)
    label = jnp.broadcast_to(power.astype(F16), (blocks, 8, 128))
    got = lax.all_to_all(
        jnp.concatenate([coded, label], axis=1), "wide", 0, 0, tiled=True, axis_index_groups=groups
    )
    scale = jnp.exp2(got[:, -8:-7, :1].astype(F32) - 14.0)
    summed = jnp.sum(got[:, :-8, :].astype(F32) * scale, axis=0)
    return summed.reshape(tiles[0], tiles[1], 8, 128).transpose(0, 2, 1, 3).reshape(rows, columns)


def shards(activations, out_grads, in_basis, out_basis, valid):
    wide, narrow = lax.axis_index("wide"), lax.axis_index("narrow")
    z, yh, core = wide // (NYH * NC), (wide // NC) % NYH, wide % NC
    yl, x = narrow // NX, narrow % NX
    pos = jnp.stack([z, yl, x, core]).astype(jnp.int32)
    sequences = activations.shape[0] // SEQ * lax.axis_size("wide")

    gathered = gather_packed(activations, pick(out_basis, core))
    mine = gather_in_basis(in_basis)
    other = other_core(mine)
    parts = NYL * NX
    basis = gathered.reshape(parts, -1, gathered.shape[1])[:, activations.shape[0] :]
    basis = basis.reshape(-1, gathered.shape[1])
    basis_other = other_core(basis)
    mask = valid.astype(F32)[:, None]
    out_mine = rotate_out(pos, out_grads, basis)
    masked_in = rotate_in(pos, gathered, mine, other, mask)
    out_other = rotate_out(pos, out_grads, basis_other)
    total = other_core(squares(pos, out_other, masked_in)) + squares(pos, out_mine, masked_in)
    return scatter_sum(total) / sequences


def solution(mesh):
    in_specs = (
        P("wide", "narrow"),
        P("wide", None),
        P("wide", "narrow"),
        P("narrow", None),
        P("wide"),
    )
    out_specs = P("wide", "narrow")
    return jax.shard_map(shards, mesh=mesh, in_specs=in_specs, out_specs=out_specs, check_vma=False)
```

time: 183 us -> 173 us (0.945)
  the two profiles are of different devices: /device:TPU:8 before, /device:TPU:50 now
where the time goes in v7:
time: 173 us
  waiting for transfers between devices  60.9 us (35%)
  blocking collectives  56.9 us (33%)
  starting transfers between devices  16.7 us (10%)
  Pallas kernels  14.9 us (9%)
  between operations  14.4 us (8%)
  local copies, waits for them, and re-layouts  4.97 us (3%)
  other arithmetic  3.2 us (2%)
    all_gather x1, waiting for transfers between devices, gather_packed(): return lax.all_gather(packed, 'narrow', axis=0, tiled=True)  55.8 us
    all_to_all x1, blocking collectives, scatter_sum(): lax.all_to_all(jnp.concatenate([coded, label], axis=1), 'wide', 0, 0, til...  42.4 us
    all_gather x1, blocking collectives, gather_in_basis(): lax.all_gather(in_basis, 'wide', axis=0, tiled=True, axis_index_groups=al...  14.4 us
    all_to_all x1, starting transfers between devices, gather_in_basis(): lax.all_to_all(copies, 'wide', 0, 0, axis_index_groups=along_z)  10.3 us
    pallas_call x1, Pallas kernels, rotate_in(): call(rotate_in_kernel, jax.ShapeDtypeStruct((tokens, width), BF16), [pltp...  6.7 us
    ppermute x3, starting transfers between devices, send(): return lax.ppermute(value, BOTH, pairs)  6.37 us
    ppermute x3, waiting for transfers between devices, send(): return lax.ppermute(value, BOTH, pairs)  5.11 us
    pallas_call x2, Pallas kernels, rotate_out(): call(rotate_out_kernel, jax.ShapeDtypeStruct((tokens, width), BF16), [plt...  5.01 us
  transfers between devices with their start and end apart: 5, of which 2 were waited for; matrix products, arithmetic and copies ran while one was open for 2% of the time, Pallas kernels for 6%

profile of v7, /device:TPU:50, one launch (start us, length us, event | category | flops | bytes accessed | tf_op | source)
XLA Modules:
  0.0 173.0 jit_solution(12896177629786630814)
XLA Ops:
  6.5 0.0 copy-start
  6.5 0.0 all-gather.2.cloned.1.call-start
  6.6 1.0 copy-done
  7.6 0.0 copy-start.2
  7.6 1.1 fusion.11
  8.7 0.0 copy-start.3
  8.7 0.0 copy-done.2
  8.8 1.0 maximum_maximum_fusion
  9.7 0.0 all-gather.2.cloned.1.call-update
  9.7 0.0 copy-done.3
  9.7 14.4 %all_gather.7 = bf16[256,512]{1,0:T(8,128)(2,1)S(1)} all-gather(bf16[64,512]{1,0:T(8,128)(2,1)S(1)} %copy-done.3), channel_id=1, replica_groups={{0,16,32,48},{8,24,40,56},{64,80,96,112},{72,88,104,120},{128,144,160,1..., dimensions={0}, use_global_device_ids=true | all-gather | bytes 327680 | tf_op jit(solution)/shard_map/all_gather | solution.py:144
  24.2 1.6 broadcast_in_dim.4
  25.7 10.3 %all-to-all-start = ((bf16[8,256,512]{2,1,0:T(8,128)(2,1)}), bf16[8,256,512]{2,1,0:T(8,128)(2,1)}, u32[]{:S(2)}, u32[]{:S(2)}) async-start(bf16[8,256,512]{2,1,0:T(8,128)(2,1)} %broadcast_in_dim.4), calls=%async_computation | async-start | bytes 4194304 | tf_op jit(solution)/shard_map/all_to_all | solution.py:146
  36.1 55.8 %all-gather.2.cloned.1.call-done.gathered = bf16[6400,512]{1,0:T(8,128)(2,1)} async-done(((bf16[800,512]{1,0:T(8,128)(2,1)}), bf16[6400,512]{1,0:T(8,128)(2,1)}) %all-gather.2.cloned.1.call-update) | async-done | bytes 6553616 | tf_op jit(solution)/shard_map/all_gather | solution.py:154
  91.8 0.0 copy-start.4
  91.8 1.9 %slice.27 = bf16[8,288,512]{2,1,0:T(8,128)(2,1)S(1)} slice(bf16[8,800,512]{2,1,0:T(8,128)(2,1)} %bitcast.25), slice={[0:8], [512:800], [0:512]} | slice | bytes 4718592 | tf_op jit(solution)/shard_map/slice | solution.py:198
  93.8 1.9 %collective-permute-start = (bf16[2304,512]{1,0:T(8,128)(2,1)S(1)}, bf16[2304,512]{1,0:T(8,128)(2,1)}, u32[]{:S(2)}, u32[]{:S(2)}) collective-permute-start(bf16[2304,512]{1,0:T(8,128)(2,1)S(1)} %bitcast.23), channel_id=1, source_target_pairs={{0,8},{1,9},{2,10},{3,11},{4,12},{5,13},{6,14},{7,15},{8,0},{9,1},... | collective-permute-start | bytes 7077896 | tf_op jit(solution)/shard_map/ppermute | solution.py:27
  95.7 0.0 all-to-all-done
  95.7 2.4 %collective-permute-start.1 = (bf16[2048,512]{1,0:T(8,128)(2,1)}, bf16[2048,512]{1,0:T(8,128)(2,1)}, u32[]{:S(2)}, u32[]{:S(2)}) collective-permute-start(bf16[2048,512]{1,0:T(8,128)(2,1)} %bitcast.7.mine), channel_id=1, source_target_pairs={{0,8},{1,9},{2,10},{3,11},{4,12},{5,13},{6,14},{7,15},{8,0},{9,1},... | collective-permute-start | bytes 6291464 | tf_op jit(solution)/shard_map/ppermute | solution.py:27
  98.2 0.0 copy-done.4
  98.2 0.1 copy.11.mask
  98.4 0.1 pad_add_fusion.pos
  98.4 0.0 copy-start.1
  98.4 5.1 %collective-permute-done.1.other = bf16[2048,512]{1,0:T(8,128)(2,1)} collective-permute-done((bf16[2048,512]{1,0:T(8,128)(2,1)}, bf16[2048,512]{1,0:T(8,128)(2,1)}, u32[]{:S(2)}, u32[]{:S(2)}) %collective-permute-start.1) | collective-permute-done | bytes 2097184 | tf_op jit(solution)/shard_map/ppermute | solution.py:27
  103.5 6.7 %shard_map.56.ins = bf16[512,512]{1,0:T(8,128)(2,1)S(1)} custom-call(s32[4]{0:T(128)S(1)} %pad_add_fusion.pos, bf16[6400,512]{1,0:T(8,128)(2,1)} %all-gather.2.cloned.1.call-done.gathered, bf16[2048,512]{1,0:T(8,128)(2,1)} %bitcast.7.mine, bf16[2048,512]{1,0:T(8,128)(2,1)} %collective-permute-done.1.other, f32[512,1]{1,0:T(8,128)S(1)} %copy.11.mask), custom_call_target="tpu_custom_call" | custom-call | flops 2147483648 | bytes 8912896 | tf_op jit(solution)/shard_map/pallas_call | solution.py:105
  110.3 0.0 collective-permute-done.packed
  110.3 0.0 copy-done.1
  110.3 3.1 %shard_map.55.outs = bf16[512,768]{1,0:T(8,128)(2,1)S(1)} custom-call(s32[4]{0:T(128)S(1)} %pad_add_fusion.pos, bf16[512,1536]{1,0:T(8,128)(2,1)S(1)} %copy-done.1, bf16[2304,512]{1,0:T(8,128)(2,1)} %collective-permute-done.packed), custom_call_target="tpu_custom_call" | custom-call | flops 1207959552 | bytes 4718592 | tf_op jit(solution)/shard_map/pallas_call | solution.py:70
  113.3 1.6 shard_map.57
  114.9 2.0 %collective-permute-start.2 = (f32[768,512]{1,0:T(8,128)S(1)}, f32[768,512]{1,0:T(8,128)S(1)}, u32[]{:S(2)}, u32[]{:S(2)}) collective-permute-start(f32[768,512]{1,0:T(8,128)S(1)} %shard_map.57), channel_id=1, source_target_pairs={{0,8},{1,9},{2,10},{3,11},{4,12},{5,13},{6,14},{7,15},{8,0},{9,1},... | collective-permute-start | bytes 4718600 | tf_op jit(solution)/shard_map/ppermute | solution.py:27
  117.0 1.9 %shard_map.58.outs = bf16[512,768]{1,0:T(8,128)(2,1)S(1)} custom-call(s32[4]{0:T(128)S(1)} %pad_add_fusion.pos, bf16[512,1536]{1,0:T(8,128)(2,1)S(1)} %copy-done.1, bf16[2304,512]{1,0:T(8,128)(2,1)S(1)} %bitcast.24), custom_call_target="tpu_custom_call" | custom-call | flops 1207959552 | bytes 4718592 | tf_op jit(solution)/shard_map/pallas_call | solution.py:70
  118.9 1.6 shard_map.59
  120.5 0.0 collective-permute-done.2
  120.6 1.1 fusion.20
  122.4 0.2 multiply_convert_fusion
  122.6 0.2 concatenate.11
  122.8 42.4 %all_to_all.10 = f16[32,104,128]{2,1,0:T(8,128)(2,1)S(1)} all-to-all(f16[32,104,128]{2,1,0:T(8,128)(2,1)S(1)} %concatenate.11), channel_id=1, replica_groups={{0,16,32,48,64,80,96,112,128,144,160,176,192,208,224,240,256,272,288,30..., dimensions={0} | all-to-all | bytes 1703936 | tf_op jit(solution)/shard_map/all_to_all | solution.py:179
  165.2 0.1 copy.13
  165.3 0.2 multiply_reduce_fusion
  165.5 0.6 broadcast_multiply_fusion
  (8 shorter events, 0.1 us)
Async XLA Ops:
  6.5 1.1 copy-start
  6.5 85.3 %all-gather.2.cloned.1.call-start = ((), (), s32[]{:S(2)}) async-start(), calls=%async_computation.2 | async-start | bytes 7372800 | tf_op jit(solution)/shard_map/all_gather | solution.py:154
  7.6 1.1 copy-start.2
  8.7 1.0 copy-start.3
  25.7 70.0 %all-to-all-start = ((bf16[8,256,512]{2,1,0:T(8,128)(2,1)}), bf16[8,256,512]{2,1,0:T(8,128)(2,1)}, u32[]{:S(2)}, u32[]{:S(2)}) async-start(bf16[8,256,512]{2,1,0:T(8,128)(2,1)} %broadcast_in_dim.4), calls=%async_computation | async-start | bytes 4194304 | tf_op jit(solution)/shard_map/all_to_all | solution.py:146
  91.8 6.3 %copy-start.4 = (s32[512]{0:T(512)S(1)}, s32[512]{0:T(512)}, u32[]{:S(2)}) copy-start(s32[512]{0:T(512)} %param.9) | copy-start | bytes 6148
  93.8 16.5 %collective-permute-start = (bf16[2304,512]{1,0:T(8,128)(2,1)S(1)}, bf16[2304,512]{1,0:T(8,128)(2,1)}, u32[]{:S(2)}, u32[]{:S(2)}) collective-permute-start(bf16[2304,512]{1,0:T(8,128)(2,1)S(1)} %bitcast.23), channel_id=1, source_target_pairs={{0,8},{1,9},{2,10},{3,11},{4,12},{5,13},{6,14},{7,15},{8,0},{9,1},... | collective-permute-start | bytes 7077896 | tf_op jit(solution)/shard_map/ppermute | solution.py:27
  95.7 7.8 %collective-permute-start.1 = (bf16[2048,512]{1,0:T(8,128)(2,1)}, bf16[2048,512]{1,0:T(8,128)(2,1)}, u32[]{:S(2)}, u32[]{:S(2)}) collective-permute-start(bf16[2048,512]{1,0:T(8,128)(2,1)} %bitcast.7.mine), channel_id=1, source_target_pairs={{0,8},{1,9},{2,10},{3,11},{4,12},{5,13},{6,14},{7,15},{8,0},{9,1},... | collective-permute-start | bytes 6291464 | tf_op jit(solution)/shard_map/ppermute | solution.py:27
  98.4 11.8 %copy-start.1 = (bf16[512,1536]{1,0:T(8,128)(2,1)S(1)}, bf16[512,1536]{1,0:T(8,128)(2,1)}, u32[]{:S(2)}) copy-start(bf16[512,1536]{1,0:T(8,128)(2,1)} %grads.3) | copy-start | bytes 4718596
  114.9 5.6 %collective-permute-start.2 = (f32[768,512]{1,0:T(8,128)S(1)}, f32[768,512]{1,0:T(8,128)S(1)}, u32[]{:S(2)}, u32[]{:S(2)}) collective-permute-start(f32[768,512]{1,0:T(8,128)S(1)} %shard_map.57), channel_id=1, source_target_pairs={{0,8},{1,9},{2,10},{3,11},{4,12},{5,13},{6,14},{7,15},{8,0},{9,1},... | collective-permute-start | bytes 4718600 | tf_op jit(solution)/shard_map/ppermute | solution.py:27
Sparse Core Ops, SparseCore 0:
  9.9 81.9 all-gather.1

commit v8 on v7

--- a/solution.py
+++ b/solution.py
@@ -50,13 +50,14 @@
 def rotate_out_kernel(pos, grads, packed, out, basis):
     parts = NYL * NX
     rows, stride = basis.shape[0] // parts, packed.shape[0] // parts
-    wide = packed.shape[1]
+    wide, half = packed.shape[1], rows // 2
+    skip = stride - rows - half
     for n in range(parts):
-        at, half = n * stride, rows // 2
+        at = n * stride + skip
         basis[n * rows : (n + 1) * rows, :wide] = packed[at : at + rows, :]
         for h in range(2):
             basis[n * rows + h * half : n * rows + (h + 1) * half, wide:] = packed[
-                at + rows : at + stride, h * wide // 2 : (h + 1) * wide // 2
+                at + rows : at + rows + half, h * wide // 2 : (h + 1) * wide // 2
             ]
     width = 256
     for j in range(out.shape[1] // width):
@@ -112,11 +113,12 @@
     )(pos, gathered, mine, other, mask)
 
 
-def squares_kernel(pos, outs, ins, out):
+def squares_kernel(pos, outs, ins, *refs):
+    before, out = refs[:-1], refs[-1]
     width = 256
     for j in range(out.shape[0] // width):
         cols = slice(j * width, (j + 1) * width)
-        total = None
+        total = before[0][cols, :] if before else None
         for s in range(outs.shape[0] // SEQ):
             rows = slice(s * SEQ, (s + 1) * SEQ)
             grad = lax.dot_general(
@@ -126,7 +128,7 @@
         out[cols, :] = total
 
 
-def squares(pos, outs, ins):
+def squares(pos, outs, ins, *before):
     tokens, width = outs.shape
     return call(
         squares_kernel,
@@ -134,8 +136,8 @@
         [],
         2 * tokens * width * ins.shape[1],
         2 * tokens * (width + ins.shape[1]) + 4 * width * ins.shape[1],
-        2,
-    )(pos, outs, ins)
+        2 + len(before),
+    )(pos, outs, ins, *before)
 
 
 def gather_in_basis(in_basis):
@@ -193,16 +195,15 @@
 
     gathered = gather_packed(activations, pick(out_basis, core))
     mine = gather_in_basis(in_basis)
+    grads_other = other_core(out_grads)
     other = other_core(mine)
-    parts = NYL * NX
-    basis = gathered.reshape(parts, -1, gathered.shape[1])[:, activations.shape[0] :]
-    basis = basis.reshape(-1, gathered.shape[1])
-    basis_other = other_core(basis)
+    gathered, other, grads_other = lax.optimization_barrier((gathered, other, grads_other))
     mask = valid.astype(F32)[:, None]
-    out_mine = rotate_out(pos, out_grads, basis)
     masked_in = rotate_in(pos, gathered, mine, other, mask)
-    out_other = rotate_out(pos, out_grads, basis_other)
-    total = other_core(squares(pos, out_other, masked_in)) + squares(pos, out_mine, masked_in)
+    masked_other = other_core(masked_in)
+    out_mine = rotate_out(pos, out_grads, gathered)
+    out_theirs = rotate_out(pos, grads_other, gathered)
+    total = squares(pos, out_theirs, masked_other, squares(pos, out_mine, masked_in))
     return scatter_sum(total) / sequences
 
 

time: 173 us -> 166 us (0.960)
  blocking collectives: 56.9 us -> 116 us
  waiting for transfers between devices: 60.9 us -> 4.16 us
  starting transfers between devices: 16.7 us -> 6.24 us
  Pallas kernels: 14.9 us -> 18.8 us
  local copies, waits for them, and re-layouts: 4.97 us -> 1.66 us
    all_to_all x0 -> x1, blocking collectives: none -> 58.7 us  [gather_in_basis(): lax.all_to_all(copies, 'wide', 0, 0, axis_index_groups=along_z)]
    all_gather x1, waiting for transfers between devices: 55.8 us -> 0.15 us  [gather_packed(): return lax.all_gather(packed, 'narrow', axis=0, tiled=True)]
    all_to_all x1 -> x0, starting transfers between devices: 10.3 us -> none  [gather_in_basis(): lax.all_to_all(copies, 'wide', 0, 0, axis_index_groups=along_z)]
    pallas_call x2, Pallas kernels: 5.01 us -> 9.48 us  [rotate_out(): call(rotate_out_kernel, jax.ShapeDtypeStruct((tokens, width), BF16), [plt...]
    slice x1 -> x0, local copies, waits for them, and re-layouts: 1.93 us -> none  [shards(): gathered.reshape(parts, -1, gathered.shape[1])[:, activations.shape[0]:]]
  transfers between devices with their start and end apart: 5 -> 4, of which waited for: 2 -> 2; matrix products, arithmetic and copies ran while one was open for 2% -> 0% of each run, Pallas kernels for 6% -> 7%
where the time goes in v8:
time: 166 us; the launch traced here: 165 us
  blocking collectives  116 us (70%)
  Pallas kernels  18.8 us (11%)
  between operations  14.4 us (9%)
  starting transfers between devices  6.24 us (4%)
  waiting for transfers between devices  4.16 us (3%)
  other arithmetic  3.14 us (2%)
    all_to_all x1, blocking collectives, gather_in_basis(): lax.all_to_all(copies, 'wide', 0, 0, axis_index_groups=along_z)  58.7 us
    all_to_all x1, blocking collectives, scatter_sum(): lax.all_to_all(jnp.concatenate([coded, label], axis=1), 'wide', 0, 0, til...  42.8 us
    all_gather x1, blocking collectives, gather_in_basis(): lax.all_gather(in_basis, 'wide', axis=0, tiled=True, axis_index_groups=al...  14.4 us
    pallas_call x2, Pallas kernels, rotate_out(): call(rotate_out_kernel, jax.ShapeDtypeStruct((tokens, width), BF16), [plt...  9.48 us
    ppermute x3, starting transfers between devices, send(): return lax.ppermute(value, BOTH, pairs)  6.24 us
    pallas_call x1, Pallas kernels, rotate_in(): call(rotate_in_kernel, jax.ShapeDtypeStruct((tokens, width), BF16), [pltp...  6.08 us
    ppermute x3, waiting for transfers between devices, send(): return lax.ppermute(value, BOTH, pairs)  4 us
  transfers between devices with their start and end apart: 4, of which 2 were waited for; matrix products, arithmetic and copies ran while one was open for 0% of the time, Pallas kernels for 7%

profile of v8, /device:TPU:50, one launch (start us, length us, event | category | flops | bytes accessed | tf_op | source)
XLA Modules:
  0.0 165.3 jit_solution(14358969329831676026)
XLA Ops:
  6.5 0.0 copy-start
  6.5 0.0 all-gather.2.cloned.1.call-start
  6.6 1.0 copy-done
  7.6 0.0 copy-start.1
  7.6 1.1 fusion.11
  8.7 0.0 copy-start.2
  8.7 0.0 copy-done.1
  8.8 1.0 maximum_maximum_fusion
  9.7 0.0 all-gather.2.cloned.1.call-update
  9.7 0.0 copy-done.2
  9.8 14.4 %all_gather.7 = bf16[256,512]{1,0:T(8,128)(2,1)S(1)} all-gather(bf16[64,512]{1,0:T(8,128)(2,1)S(1)} %copy-done.2), channel_id=1, replica_groups={{0,16,32,48},{8,24,40,56},{64,80,96,112},{72,88,104,120},{128,144,160,1..., dimensions={0}, use_global_device_ids=true | all-gather | bytes 327680 | tf_op jit(solution)/shard_map/all_gather | solution.py:146
  24.2 0.2 broadcast_in_dim.4
  24.4 0.0 copy-start.3
  24.4 58.7 %all_to_all.10 = bf16[8,256,512]{2,1,0:T(8,128)(2,1)S(1)} all-to-all(bf16[8,256,512]{2,1,0:T(8,128)(2,1)S(1)} %broadcast_in_dim.4), channel_id=1, replica_groups={{0,64,128,192,256,320,384,448},{8,72,136,200,264,328,392,456},{16,80,14..., dimensions={0} | all-to-all | bytes 4194304 | tf_op jit(solution)/shard_map/all_to_all | solution.py:148
  83.1 1.9 %collective-permute-start = (bf16[2048,512]{1,0:T(8,128)(2,1)S(1)}, bf16[2048,512]{1,0:T(8,128)(2,1)}, u32[]{:S(2)}, u32[]{:S(2)}) collective-permute-start(bf16[2048,512]{1,0:T(8,128)(2,1)S(1)} %bitcast.21), channel_id=1, source_target_pairs={{0,8},{1,9},{2,10},{3,11},{4,12},{5,13},{6,14},{7,15},{8,0},{9,1},... | collective-permute-start | bytes 6291464 | tf_op jit(solution)/shard_map/ppermute | solution.py:27
  85.0 2.4 %collective-permute-start.1 = (bf16[512,1536]{1,0:T(8,128)(2,1)}, bf16[512,1536]{1,0:T(8,128)(2,1)}, u32[]{:S(2)}, u32[]{:S(2)}) collective-permute-start(bf16[512,1536]{1,0:T(8,128)(2,1)} %grads.1), channel_id=1, source_target_pairs={{0,8},{1,9},{2,10},{3,11},{4,12},{5,13},{6,14},{7,15},{8,0},{9,1},... | collective-permute-start | bytes 4718600 | tf_op jit(solution)/shard_map/ppermute | solution.py:27
  87.4 0.0 copy-done.3
  87.4 0.1 copy.11.mask
  87.6 0.1 pad_add_fusion.pos
  87.7 4.0 %collective-permute-done.1.grads = bf16[512,1536]{1,0:T(8,128)(2,1)} collective-permute-done((bf16[512,1536]{1,0:T(8,128)(2,1)}, bf16[512,1536]{1,0:T(8,128)(2,1)}, u32[]{:S(2)}, u32[]{:S(2)}) %collective-permute-start.1) | collective-permute-done | bytes 1572896 | tf_op jit(solution)/shard_map/ppermute | solution.py:27
  91.7 0.0 collective-permute-done.other
  91.7 0.1 all-gather.2.cloned.1.call-done.packed.gathered
  91.8 6.1 %shard_map.56.ins = bf16[512,512]{1,0:T(8,128)(2,1)S(1)} custom-call(s32[4]{0:T(128)S(1)} %pad_add_fusion.pos, bf16[6400,512]{1,0:T(8,128)(2,1)} %all-gather.2.cloned.1.call-done.packed.gathered, bf16[2048,512]{1,0:T(8,128)(2,1)S(1)} %bitcast.22, bf16[2048,512]{1,0:T(8,128)(2,1)} %collective-permute-done.other, f32[512,1]{1,0:T(8,128)S(1)} %copy.11.mask), custom_call_target="tpu_custom_call" | custom-call | flops 2147483648 | bytes 8912896 | tf_op jit(solution)/shard_map/pallas_call | solution.py:106
  97.9 1.9 %collective-permute-start.2 = (bf16[512,512]{1,0:T(8,128)(2,1)S(1)}, bf16[512,512]{1,0:T(8,128)(2,1)S(1)}, u32[]{:S(2)}, u32[]{:S(2)}) collective-permute-start(bf16[512,512]{1,0:T(8,128)(2,1)S(1)} %shard_map.56.ins), channel_id=1, source_target_pairs={{0,8},{1,9},{2,10},{3,11},{4,12},{5,13},{6,14},{7,15},{8,0},{9,1},... | collective-permute-start | bytes 1572872 | tf_op jit(solution)/shard_map/ppermute | solution.py:27
  99.9 4.7 %shard_map.57.outs = bf16[512,768]{1,0:T(8,128)(2,1)S(1)} custom-call(s32[4]{0:T(128)S(1)} %pad_add_fusion.pos, bf16[512,1536]{1,0:T(8,128)(2,1)} %grads.1, bf16[6400,512]{1,0:T(8,128)(2,1)} %all-gather.2.cloned.1.call-done.packed.gathered), custom_call_target="tpu_custom_call" | custom-call | flops 1207959552 | bytes 4718592 | tf_op jit(solution)/shard_map/pallas_call | solution.py:71
  104.6 1.6 shard_map.58.refs_0_
  106.2 4.7 %shard_map.55.outs = bf16[512,768]{1,0:T(8,128)(2,1)S(1)} custom-call(s32[4]{0:T(128)S(1)} %pad_add_fusion.pos, bf16[512,1536]{1,0:T(8,128)(2,1)} %collective-permute-done.1.grads, bf16[6400,512]{1,0:T(8,128)(2,1)} %all-gather.2.cloned.1.call-done.packed.gathered), custom_call_target="tpu_custom_call" | custom-call | flops 1207959552 | bytes 4718592 | tf_op jit(solution)/shard_map/pallas_call | solution.py:71
  111.0 0.0 collective-permute-done.2.ins
  111.0 1.6 shard_map.59
  112.6 1.0 reduce_max.9
  114.3 0.2 multiply_convert_fusion
  114.5 0.2 concatenate.11
  114.7 42.8 %all_to_all.11 = f16[32,104,128]{2,1,0:T(8,128)(2,1)S(1)} all-to-all(f16[32,104,128]{2,1,0:T(8,128)(2,1)S(1)} %concatenate.11), channel_id=1, replica_groups={{0,16,32,48,64,80,96,112,128,144,160,176,192,208,224,240,256,272,288,30..., dimensions={0} | all-to-all | bytes 1703936 | tf_op jit(solution)/shard_map/all_to_all | solution.py:181
  157.5 0.1 copy.13
  157.6 0.2 multiply_reduce_fusion
  157.8 0.6 broadcast_multiply_fusion
  (8 shorter events, 0.1 us)
Async XLA Ops:
  6.5 1.1 copy-start
  6.5 85.3 %all-gather.2.cloned.1.call-start = ((), (), s32[]{:S(2)}) async-start(), calls=%async_computation.2 | async-start | bytes 7372800 | tf_op jit(solution)/shard_map/all_gather | solution.py:156
  7.6 1.1 copy-start.1
  8.7 1.1 copy-start.2
  24.4 63.0 %copy-start.3 = (s32[512]{0:T(512)S(1)}, s32[512]{0:T(512)}, u32[]{:S(2)}) copy-start(s32[512]{0:T(512)} %param.9) | copy-start | bytes 6148
  83.1 8.6 %collective-permute-start = (bf16[2048,512]{1,0:T(8,128)(2,1)S(1)}, bf16[2048,512]{1,0:T(8,128)(2,1)}, u32[]{:S(2)}, u32[]{:S(2)}) collective-permute-start(bf16[2048,512]{1,0:T(8,128)(2,1)S(1)} %bitcast.21), channel_id=1, source_target_pairs={{0,8},{1,9},{2,10},{3,11},{4,12},{5,13},{6,14},{7,15},{8,0},{9,1},... | collective-permute-start | bytes 6291464 | tf_op jit(solution)/shard_map/ppermute | solution.py:27
  85.0 6.7 %collective-permute-start.1 = (bf16[512,1536]{1,0:T(8,128)(2,1)}, bf16[512,1536]{1,0:T(8,128)(2,1)}, u32[]{:S(2)}, u32[]{:S(2)}) collective-permute-start(bf16[512,1536]{1,0:T(8,128)(2,1)} %grads.1), channel_id=1, source_target_pairs={{0,8},{1,9},{2,10},{3,11},{4,12},{5,13},{6,14},{7,15},{8,0},{9,1},... | collective-permute-start | bytes 4718600 | tf_op jit(solution)/shard_map/ppermute | solution.py:27
  97.9 13.0 %collective-permute-start.2 = (bf16[512,512]{1,0:T(8,128)(2,1)S(1)}, bf16[512,512]{1,0:T(8,128)(2,1)S(1)}, u32[]{:S(2)}, u32[]{:S(2)}) collective-permute-start(bf16[512,512]{1,0:T(8,128)(2,1)S(1)} %shard_map.56.ins), channel_id=1, source_target_pairs={{0,8},{1,9},{2,10},{3,11},{4,12},{5,13},{6,14},{7,15},{8,0},{9,1},... | collective-permute-start | bytes 1572872 | tf_op jit(solution)/shard_map/ppermute | solution.py:27
Sparse Core Ops, SparseCore 0:
  9.9 81.9 all-gather.1

commit v9 on v8

v9 whole, which is shorter than its diff:
```python
import functools

import jax
import jax.numpy as jnp
import numpy as np
from jax import lax
from jax.experimental import pallas as pl
from jax.experimental.pallas import tpu as pltpu
from jax.sharding import PartitionSpec as P

SEQ = 128
NZ, NYH, NC, NYL, NX = 8, 4, 2, 2, 4
BOTH = ("wide", "narrow")
F32, BF16, F16 = jnp.float32, jnp.bfloat16, jnp.float16
VMEM = pl.BlockSpec(memory_space=pltpu.VMEM)
SMEM = pl.BlockSpec(memory_space=pltpu.SMEM)
LIMIT = 48 * 1024 * 1024


def send(value, target):
    pairs = []
    for z, yh, c, yl, x in np.ndindex(NZ, NYH, NC, NYL, NX):
        z2, yh2, c2, yl2, x2 = target(z, yh, c, yl, x)
        z2, yh2, c2, yl2, x2 = z2 % NZ, yh2 % NYH, c2 % NC, yl2 % NYL, x2 % NX
        source = (((z * NYH + yh) * NC + c) * NYL + yl) * NX + x
        pairs.append((source, (((z2 * NYH + yh2) * NC + c2) * NYL + yl2) * NX + x2))
    return lax.ppermute(value, BOTH, pairs)


def other_core(value):
    return send(value, lambda z, yh, c, yl, x: (z, yh, c + 1, yl, x))


def cost(flops, nbytes):
    return pl.CostEstimate(flops=flops, bytes_accessed=nbytes, transcendentals=0)


def rotate_in_kernel(pos, gathered, mine, other, mask, out, basis, total, plane):
    n, core = pl.program_id(0), pos[3]
    tokens, rows = out.shape[0], mine.shape[0] // NYH
    for i in range(NYH):
        for ref, c in ((mine, core), (other, 1 - core)):
            at = pl.multiple_of((i * NC + c) * rows, rows)
            plane[pl.ds(at, rows), :] = ref[i * rows : (i + 1) * rows, :]
    product = jnp.dot(gathered[:tokens, :], plane[...], preferred_element_type=F32)

    @pl.when(n == 0)
    def _():
        total[...] = product

    @pl.when(n > 0)
    def _():
        total[...] += product

    @pl.when(n == pl.num_programs(0) - 1)
    def _():
        out[...] = (total[...].astype(BF16).astype(F32) * mask[...]).astype(BF16)

    height, wide = basis.shape[0], gathered.shape[1]
    half, at = height // 2, tokens + height
    basis[:, :wide] = gathered[tokens:at, :]
    for h in range(2):
        basis[h * half : (h + 1) * half, wide:] = gathered[at:, h * wide // 2 : (h + 1) * wide // 2]


def rotate_in(pos, gathered, mine, other, mask, basis_shape):
    parts = NYL * NX
    tokens, width = mask.shape[0], mine.shape[1]
    depth = 2 * mine.shape[0]
    by_rows = lambda array: pl.BlockSpec((array.shape[0] // parts, array.shape[1]), lambda n: (n, 0))
    basis = jax.ShapeDtypeStruct(basis_shape, BF16)
    return pl.pallas_call(
        rotate_in_kernel,
        grid=(parts,),
        out_shape=[jax.ShapeDtypeStruct((tokens, width), BF16), basis],
        in_specs=[
            SMEM,
            by_rows(gathered),
            by_rows(mine),
            by_rows(other),
            pl.BlockSpec(mask.shape, lambda n: (0, 0)),
        ],
        out_specs=[pl.BlockSpec((tokens, width), lambda n: (0, 0)), by_rows(basis)],
        scratch_shapes=[pltpu.VMEM((tokens, width), F32), pltpu.VMEM((depth // parts, width), BF16)],
        compiler_params=pltpu.CompilerParams(vmem_limit_bytes=LIMIT),
        cost_estimate=cost(2 * tokens * depth * width, 2 * (gathered.size + 2 * mine.size + tokens * width)),
    )(pos, gathered, mine, other, mask)


def rotate_out_kernel(mine, theirs, basis, out_mine, out_theirs):
    width = 256
    for j in range(basis.shape[1] // width):
        cols = slice(j * width, (j + 1) * width)
        for grads, out in ((mine, out_mine), (theirs, out_theirs)):
            out[:, cols] = jnp.dot(grads[...], basis[:, cols], preferred_element_type=F32).astype(BF16)


def rotate_out(mine, theirs, basis):
    tokens, depth = mine.shape
    width = basis.shape[1]
    return pl.pallas_call(
        rotate_out_kernel,
        out_shape=[jax.ShapeDtypeStruct((tokens, width), BF16)] * 2,
        in_specs=[VMEM] * 3,
        out_specs=[VMEM] * 2,
        compiler_params=pltpu.CompilerParams(vmem_limit_bytes=LIMIT),
        cost_estimate=cost(4 * tokens * depth * width, 2 * (2 * tokens * (depth + width) + depth * width)),
    )(mine, theirs, basis)


def squares_kernel(outs_mine, outs_theirs, ins_mine, ins_theirs, out, top):
    width = 256
    for j in range(out.shape[0] // width):
        cols = slice(j * width, (j + 1) * width)
        total = None
        for outs, ins in ((outs_mine, ins_mine), (outs_theirs, ins_theirs)):
            for s in range(outs.shape[0] // SEQ):
                rows = slice(s * SEQ, (s + 1) * SEQ)
                grad = lax.dot_general(
                    outs[rows, cols], ins[rows, :], (((0,), (0,)), ((), ())), preferred_element_type=F32
                )
                total = grad * grad if total is None else total + grad * grad
        out[cols, :] = total
        largest = jnp.max(total.reshape(width // 8, 8, out.shape[1]), axis=0)
        top[...] = largest if j == 0 else jnp.maximum(top[...], largest)


def squares(outs_mine, outs_theirs, ins_mine, ins_theirs):
    tokens, width = outs_mine.shape
    columns = ins_mine.shape[1]
    return pl.pallas_call(
        squares_kernel,
        out_shape=[jax.ShapeDtypeStruct((width, columns), F32), jax.ShapeDtypeStruct((8, columns), F32)],
        in_specs=[VMEM] * 4,
        out_specs=[VMEM] * 2,
        compiler_params=pltpu.CompilerParams(vmem_limit_bytes=LIMIT),
        cost_estimate=cost(4 * tokens * width * columns, 4 * tokens * (width + columns) + 4 * width * columns),
    )(outs_mine, outs_theirs, ins_mine, ins_theirs)


def gather_in_basis(in_basis):
    along_yh = [[(z * NYH + yh) * NC + c for yh in range(NYH)] for z in range(NZ) for c in range(NC)]
    along_z = [[z * NYH * NC + r for z in range(NZ)] for r in range(NYH * NC)]
    chunk = lax.all_gather(in_basis, "wide", axis=0, tiled=True, axis_index_groups=along_yh)
    copies = jnp.broadcast_to(chunk[None], (NZ, *chunk.shape))
    return lax.all_to_all(copies, "wide", 0, 0, axis_index_groups=along_z).reshape(-1, chunk.shape[1])


def gather_packed(activations, picked):
    width = activations.shape[1]
    half = picked.shape[0] // 2
    rest = jnp.concatenate([picked[:half, width:], picked[half:, width:]], axis=1)
    packed = jnp.concatenate([activations, picked[:, :width], rest], axis=0)
    return lax.all_gather(packed, "narrow", axis=0, tiled=True)


def power_of(top):
    return jnp.maximum(jnp.floor(jnp.log2(jnp.maximum(top, 1e-30))), -100.0)


def pick(out_basis, core):
    width = out_basis.shape[1]
    own = width // (NZ * NYH * NC)
    source = lax.broadcasted_iota(jnp.int32, (width, width // NC), 0)
    place = lax.broadcasted_iota(jnp.int32, (width, width // NC), 1)
    wanted = ((place // own) * NC + core) * own + place % own
    return jnp.dot(out_basis, (source == wanted).astype(BF16), preferred_element_type=F32).astype(BF16)


def scatter_sum(total, top):
    blocks = NZ * NYH
    groups = [[zy * NC + c for zy in range(blocks)] for c in range(NC)]
    rows, columns = total.shape[0] // blocks, total.shape[1]
    tiles = (rows // 8, columns // 128)
    power = power_of(top)
    coded = (total * jnp.exp2(14.0 - power)).astype(F16)
    coded = coded.reshape(blocks, tiles[0], 8, tiles[1], 128).transpose(0, 1, 3, 2, 4).reshape(blocks, -1, 128)
    label = jnp.broadcast_to(power.astype(F16), (blocks, 8, 128))
    got = lax.all_to_all(
        jnp.concatenate([coded, label], axis=1), "wide", 0, 0, tiled=True, axis_index_groups=groups
    )
    scale = jnp.exp2(got[:, -8:-7, :1].astype(F32) - 14.0)
    summed = jnp.sum(got[:, :-8, :].astype(F32) * scale, axis=0)
    return summed.reshape(tiles[0], tiles[1], 8, 128).transpose(0, 2, 1, 3).reshape(rows, columns)


def shards(activations, out_grads, in_basis, out_basis, valid):
    wide, narrow = lax.axis_index("wide"), lax.axis_index("narrow")
    z, yh, core = wide // (NYH * NC), (wide // NC) % NYH, wide % NC
    yl, x = narrow // NX, narrow % NX
    pos = jnp.stack([z, yl, x, core]).astype(jnp.int32)
    sequences = activations.shape[0] // SEQ * lax.axis_size("wide")

    gathered = gather_packed(activations, pick(out_basis, core))
    mine = gather_in_basis(in_basis)
    grads_other = other_core(out_grads)
    other = other_core(mine)
    gathered, other, grads_other = lax.optimization_barrier((gathered, other, grads_other))
    mask = valid.astype(F32)[:, None]
    basis_shape = (out_basis.shape[1], out_basis.shape[1] // NC)
    masked_in, basis = rotate_in(pos, gathered, mine, other, mask, basis_shape)
    masked_other = other_core(masked_in)
    out_mine, out_theirs = rotate_out(out_grads, grads_other, basis)
    total, top = squares(out_mine, out_theirs, masked_in, masked_other)
    return scatter_sum(total, jnp.max(top)) / sequences


def solution(mesh):
    in_specs = (
        P("wide", "narrow"),
        P("wide", None),
        P("wide", "narrow"),
        P("narrow", None),
        P("wide"),
    )
    out_specs = P("wide", "narrow")
    return jax.shard_map(shards, mesh=mesh, in_specs=in_specs, out_specs=out_specs, check_vma=False)
```

time: 166 us -> 163 us (0.982)
  Pallas kernels: 18.8 us -> 16.3 us
    pallas_call x5 -> x3, Pallas kernels: 18.8 us -> 16.3 us  [the longest x1 9.28 us: rotate_in(): pl.pallas_call(rotate_in_kernel, grid=(parts,), out_shape=[jax.ShapeDtype...]
  transfers between devices with their start and end apart: 4 -> 4, of which waited for: 2 -> 2; matrix products, arithmetic and copies ran while one was open for 0% -> 0% of each run, Pallas kernels for 7% -> 3%
where the time goes in v9:
time: 163 us; the launch traced here: 162 us
  blocking collectives  116 us (71%)
  Pallas kernels  16.3 us (10%)
  between operations  14.4 us (9%)
  starting transfers between devices  6.23 us (4%)
  waiting for transfers between devices  4.16 us (3%)
  other arithmetic  2.73 us (2%)
  local copies, waits for them, and re-layouts  1.66 us (1%)
    all_to_all x1, blocking collectives, gather_in_basis(): lax.all_to_all(copies, 'wide', 0, 0, axis_index_groups=along_z)  58.7 us
    all_to_all x1, blocking collectives, scatter_sum(): lax.all_to_all(jnp.concatenate([coded, label], axis=1), 'wide', 0, 0, til...  42.8 us
    all_gather x1, blocking collectives, gather_in_basis(): lax.all_gather(in_basis, 'wide', axis=0, tiled=True, axis_index_groups=al...  14.4 us
    pallas_call x1, Pallas kernels, rotate_in(): pl.pallas_call(rotate_in_kernel, grid=(parts,), out_shape=[jax.ShapeDtype...  9.28 us
    ppermute x3, starting transfers between devices, send(): return lax.ppermute(value, BOTH, pairs)  6.23 us
    pallas_call x1, Pallas kernels, rotate_out(): pl.pallas_call(rotate_out_kernel, out_shape=[jax.ShapeDtypeStruct((tokens...  5.22 us
    ppermute x3, waiting for transfers between devices, send(): return lax.ppermute(value, BOTH, pairs)  4 us
  transfers between devices with their start and end apart: 4, of which 2 were waited for; matrix products, arithmetic and copies ran while one was open for 0% of the time, Pallas kernels for 3%

profile of v9, /device:TPU:50, one launch (start us, length us, event | category | flops | bytes accessed | tf_op | source)
XLA Modules:
  0.0 162.5 jit_solution(6261564387882016921)
XLA Ops:
  6.5 0.0 copy-start
  6.5 0.0 all-gather.2.cloned.1.call-start
  6.6 1.0 copy-done
  7.6 0.0 copy-start.1
  7.6 1.1 fusion.11
  8.7 0.0 copy-start.2
  8.7 0.0 copy-done.1
  8.8 1.0 maximum_maximum_fusion
  9.7 0.0 all-gather.2.cloned.1.call-update
  9.7 0.0 copy-done.2
  9.7 14.4 %all_gather.7 = bf16[256,512]{1,0:T(8,128)(2,1)S(1)} all-gather(bf16[64,512]{1,0:T(8,128)(2,1)S(1)} %copy-done.2), channel_id=1, replica_groups={{0,16,32,48},{8,24,40,56},{64,80,96,112},{72,88,104,120},{128,144,160,1..., dimensions={0}, use_global_device_ids=true | all-gather | bytes 327680 | tf_op jit(solution)/shard_map/all_gather | solution.py:144
  24.2 0.2 broadcast_in_dim.4
  24.4 0.0 copy-start.3
  24.4 58.7 %all_to_all.10 = bf16[8,256,512]{2,1,0:T(8,128)(2,1)S(1)} all-to-all(bf16[8,256,512]{2,1,0:T(8,128)(2,1)S(1)} %broadcast_in_dim.4), channel_id=1, replica_groups={{0,64,128,192,256,320,384,448},{8,72,136,200,264,328,392,456},{16,80,14..., dimensions={0} | all-to-all | bytes 4194304 | tf_op jit(solution)/shard_map/all_to_all | solution.py:146
  83.0 1.9 %collective-permute-start = (bf16[2048,512]{1,0:T(8,128)(2,1)S(1)}, bf16[2048,512]{1,0:T(8,128)(2,1)}, u32[]{:S(2)}, u32[]{:S(2)}) collective-permute-start(bf16[2048,512]{1,0:T(8,128)(2,1)S(1)} %bitcast.21), channel_id=1, source_target_pairs={{0,8},{1,9},{2,10},{3,11},{4,12},{5,13},{6,14},{7,15},{8,0},{9,1},... | collective-permute-start | bytes 6291464 | tf_op jit(solution)/shard_map/ppermute | solution.py:27
  85.0 2.4 %collective-permute-start.1 = (bf16[512,1536]{1,0:T(8,128)(2,1)}, bf16[512,1536]{1,0:T(8,128)(2,1)}, u32[]{:S(2)}, u32[]{:S(2)}) collective-permute-start(bf16[512,1536]{1,0:T(8,128)(2,1)} %mine.1), channel_id=1, source_target_pairs={{0,8},{1,9},{2,10},{3,11},{4,12},{5,13},{6,14},{7,15},{8,0},{9,1},... | collective-permute-start | bytes 4718600 | tf_op jit(solution)/shard_map/ppermute | solution.py:27
  87.4 0.0 copy-done.3
  87.4 0.1 copy.11.mask
  87.6 0.1 pad_add_fusion.pos
  87.7 4.0 %collective-permute-done.1.theirs = bf16[512,1536]{1,0:T(8,128)(2,1)} collective-permute-done((bf16[512,1536]{1,0:T(8,128)(2,1)}, bf16[512,1536]{1,0:T(8,128)(2,1)}, u32[]{:S(2)}, u32[]{:S(2)}) %collective-permute-start.1) | collective-permute-done | bytes 1572896 | tf_op jit(solution)/shard_map/ppermute | solution.py:27
  91.7 0.0 collective-permute-done.other
  91.7 0.1 all-gather.2.cloned.1.call-done.gathered
  91.8 9.3 %shard_map.55 = (bf16[512,512]{1,0:T(8,128)(2,1)S(1)}, bf16[1536,768]{1,0:T(8,128)(2,1)}) custom-call(s32[4]{0:T(128)S(1)} %pad_add_fusion.pos, bf16[6400,512]{1,0:T(8,128)(2,1)} %all-gather.2.cloned.1.call-done.gathered, bf16[2048,512]{1,0:T(8,128)(2,1)S(1)} %bitcast.22, bf16[2048,512]{1,0:T(8,128)(2,1)} %collective-permute-done.other, f32[512,1]{1,0:T(8,128)S(1)} %copy.11.mask), custom_call_target="tpu_custom_call" | custom-call | flops 2147483648 | bytes 11272192 | tf_op jit(solution)/shard_map/pallas_call | solution.py:72
  101.1 1.9 %collective-permute-start.2 = (bf16[512,512]{1,0:T(8,128)(2,1)S(1)}, bf16[512,512]{1,0:T(8,128)(2,1)S(1)}, u32[]{:S(2)}, u32[]{:S(2)}) collective-permute-start(bf16[512,512]{1,0:T(8,128)(2,1)S(1)} %get-tuple-element.20.ins_mine), channel_id=1, source_target_pairs={{0,8},{1,9},{2,10},{3,11},{4,12},{5,13},{6,14},{7,15},{8,0},{9,1},... | collective-permute-start | bytes 1572872 | tf_op jit(solution)/shard_map/ppermute | solution.py:27
  103.0 5.2 %shard_map.56 = (bf16[512,768]{1,0:T(8,128)(2,1)S(1)}, bf16[512,768]{1,0:T(8,128)(2,1)S(1)}) custom-call(bf16[512,1536]{1,0:T(8,128)(2,1)} %mine.1, bf16[512,1536]{1,0:T(8,128)(2,1)} %collective-permute-done.1.theirs, bf16[1536,768]{1,0:T(8,128)(2,1)} %get-tuple-element.17.basis), custom_call_target="tpu_custom_call" | custom-call | flops 2415919104 | bytes 7077888 | tf_op jit(solution)/shard_map/pallas_call | solution.py:101
  108.3 0.0 collective-permute-done.2.ins_theirs
  108.3 1.8 %shard_map.57 = (f32[768,512]{1,0:T(8,128)S(1)}, f32[8,512]{1,0:T(8,128)S(1)}) custom-call(bf16[512,768]{1,0:T(8,128)(2,1)S(1)} %get-tuple-element.18.outs_mine, bf16[512,768]{1,0:T(8,128)(2,1)S(1)} %get-tuple-element.19.outs_theirs, bf16[512,512]{1,0:T(8,128)(2,1)S(1)} %get-tuple-element.20.ins_mine, bf16[512,512]{1,0:T(8,128)(2,1)S(1)} %collective-permute-done.2.ins_theirs), custom_call_target="tpu_custom_call" | custom-call | flops 805306368 | bytes 4194304 | tf_op jit(solution)/shard_map/pallas_call | solution.py:131
  110.1 0.6 reduce_max.9
  111.5 0.2 multiply_convert_fusion
  111.7 0.2 concatenate.11
  111.8 42.8 %all_to_all.11 = f16[32,104,128]{2,1,0:T(8,128)(2,1)S(1)} all-to-all(f16[32,104,128]{2,1,0:T(8,128)(2,1)S(1)} %concatenate.11), channel_id=1, replica_groups={{0,16,32,48,64,80,96,112,128,144,160,176,192,208,224,240,256,272,288,30..., dimensions={0} | all-to-all | bytes 1703936 | tf_op jit(solution)/shard_map/all_to_all | solution.py:179
  154.6 0.1 copy.13
  154.8 0.2 multiply_reduce_fusion
  155.0 0.6 broadcast_multiply_fusion
  (8 shorter events, 0.1 us)
Async XLA Ops:
  6.5 1.1 copy-start
  6.5 85.3 %all-gather.2.cloned.1.call-start = ((), (), s32[]{:S(2)}) async-start(), calls=%async_computation.2 | async-start | bytes 7372800 | tf_op jit(solution)/shard_map/all_gather | solution.py:154
  7.6 1.1 copy-start.1
  8.7 1.0 copy-start.2
  24.4 63.0 %copy-start.3 = (s32[512]{0:T(512)S(1)}, s32[512]{0:T(512)}, u32[]{:S(2)}) copy-start(s32[512]{0:T(512)} %param.9) | copy-start | bytes 6148
  83.0 8.6 %collective-permute-start = (bf16[2048,512]{1,0:T(8,128)(2,1)S(1)}, bf16[2048,512]{1,0:T(8,128)(2,1)}, u32[]{:S(2)}, u32[]{:S(2)}) collective-permute-start(bf16[2048,512]{1,0:T(8,128)(2,1)S(1)} %bitcast.21), channel_id=1, source_target_pairs={{0,8},{1,9},{2,10},{3,11},{4,12},{5,13},{6,14},{7,15},{8,0},{9,1},... | collective-permute-start | bytes 6291464 | tf_op jit(solution)/shard_map/ppermute | solution.py:27
  85.0 6.7 %collective-permute-start.1 = (bf16[512,1536]{1,0:T(8,128)(2,1)}, bf16[512,1536]{1,0:T(8,128)(2,1)}, u32[]{:S(2)}, u32[]{:S(2)}) collective-permute-start(bf16[512,1536]{1,0:T(8,128)(2,1)} %mine.1), channel_id=1, source_target_pairs={{0,8},{1,9},{2,10},{3,11},{4,12},{5,13},{6,14},{7,15},{8,0},{9,1},... | collective-permute-start | bytes 4718600 | tf_op jit(solution)/shard_map/ppermute | solution.py:27
  101.1 7.1 %collective-permute-start.2 = (bf16[512,512]{1,0:T(8,128)(2,1)S(1)}, bf16[512,512]{1,0:T(8,128)(2,1)S(1)}, u32[]{:S(2)}, u32[]{:S(2)}) collective-permute-start(bf16[512,512]{1,0:T(8,128)(2,1)S(1)} %get-tuple-element.20.ins_mine), channel_id=1, source_target_pairs={{0,8},{1,9},{2,10},{3,11},{4,12},{5,13},{6,14},{7,15},{8,0},{9,1},... | collective-permute-start | bytes 1572872 | tf_op jit(solution)/shard_map/ppermute | solution.py:27
Sparse Core Ops, SparseCore 0:
  9.9 81.9 all-gather.1

commit v10 on v9

--- a/solution.py
+++ b/solution.py
@@ -14,6 +14,7 @@
 F32, BF16, F16 = jnp.float32, jnp.bfloat16, jnp.float16
 VMEM = pl.BlockSpec(memory_space=pltpu.VMEM)
 SMEM = pl.BlockSpec(memory_space=pltpu.SMEM)
+ANY = pl.BlockSpec(memory_space=pl.ANY)
 LIMIT = 48 * 1024 * 1024
 
 
@@ -35,59 +36,75 @@
     return pl.CostEstimate(flops=flops, bytes_accessed=nbytes, transcendentals=0)
 
 
-def rotate_in_kernel(pos, gathered, mine, other, mask, out, basis, total, plane):
-    n, core = pl.program_id(0), pos[3]
-    tokens, rows = out.shape[0], mine.shape[0] // NYH
-    for i in range(NYH):
+def rotate_in_kernel(pos, gathered, mine, other, mask, out, blocks, basis, sems):
+    core, parts = pos[3], blocks.shape[0]
+    stride, (tokens, depth) = gathered.shape[0] // parts, blocks.shape[1:]
+    copies = [
+        pltpu.make_async_copy(gathered.at[pl.ds(n * stride, tokens), :], blocks.at[n], sems.at[n])
+        for n in range(parts)
+    ]
+    for copy in copies:
+        copy.start()
+    rows = mine.shape[0] // (NZ * NYH)
+    for i in range(NZ * NYH):
         for ref, c in ((mine, core), (other, 1 - core)):
             at = pl.multiple_of((i * NC + c) * rows, rows)
-            plane[pl.ds(at, rows), :] = ref[i * rows : (i + 1) * rows, :]
-    product = jnp.dot(gathered[:tokens, :], plane[...], preferred_element_type=F32)
-
-    @pl.when(n == 0)
-    def _():
-        total[...] = product
-
-    @pl.when(n > 0)
-    def _():
-        total[...] += product
-
-    @pl.when(n == pl.num_programs(0) - 1)
-    def _():
-        out[...] = (total[...].astype(BF16).astype(F32) * mask[...]).astype(BF16)
-
-    height, wide = basis.shape[0], gathered.shape[1]
-    half, at = height // 2, tokens + height
-    basis[:, :wide] = gathered[tokens:at, :]
-    for h in range(2):
-        basis[h * half : (h + 1) * half, wide:] = gathered[at:, h * wide // 2 : (h + 1) * wide // 2]
-
-
-def rotate_in(pos, gathered, mine, other, mask, basis_shape):
+            basis[pl.ds(at, rows), :] = ref[i * rows : (i + 1) * rows, :]
+    half = tokens // 2
+    for part in range(2):
+        here = slice(part * half, (part + 1) * half)
+        total = jnp.zeros((half, out.shape[1]), F32)
+        for n in range(parts):
+            if part == 0:
+                copies[n].wait()
+            total += jnp.dot(
+                blocks[n, here, :], basis[n * depth : (n + 1) * depth, :], preferred_element_type=F32
+            )
+        out[here, :] = (total.astype(BF16).astype(F32) * mask[here, :]).astype(BF16)
+
+
+def rotate_in(pos, gathered, mine, other, mask):
     parts = NYL * NX
     tokens, width = mask.shape[0], mine.shape[1]
     depth = 2 * mine.shape[0]
-    by_rows = lambda array: pl.BlockSpec((array.shape[0] // parts, array.shape[1]), lambda n: (n, 0))
-    basis = jax.ShapeDtypeStruct(basis_shape, BF16)
     return pl.pallas_call(
         rotate_in_kernel,
-        grid=(parts,),
-        out_shape=[jax.ShapeDtypeStruct((tokens, width), BF16), basis],
-        in_specs=[
-            SMEM,
-            by_rows(gathered),
-            by_rows(mine),
-            by_rows(other),
-            pl.BlockSpec(mask.shape, lambda n: (0, 0)),
+        out_shape=jax.ShapeDtypeStruct((tokens, width), BF16),
+        in_specs=[SMEM, ANY, VMEM, VMEM, VMEM],
+        out_specs=VMEM,
+        scratch_shapes=[
+            pltpu.VMEM((parts, tokens, depth // parts), BF16),
+            pltpu.VMEM((depth, width), BF16),
+            pltpu.SemaphoreType.DMA((parts,)),
         ],
-        out_specs=[pl.BlockSpec((tokens, width), lambda n: (0, 0)), by_rows(basis)],
-        scratch_shapes=[pltpu.VMEM((tokens, width), F32), pltpu.VMEM((depth // parts, width), BF16)],
         compiler_params=pltpu.CompilerParams(vmem_limit_bytes=LIMIT),
-        cost_estimate=cost(2 * tokens * depth * width, 2 * (gathered.size + 2 * mine.size + tokens * width)),
+        cost_estimate=cost(2 * tokens * depth * width, 2 * (tokens * depth + depth * width + tokens * width)),
     )(pos, gathered, mine, other, mask)
 
 
-def rotate_out_kernel(mine, theirs, basis, out_mine, out_theirs):
+def rotate_out_kernel(gathered, mine, theirs, out_mine, out_theirs, basis, sems):
+    parts = NYL * NX
+    stride, wide = gathered.shape[0] // parts, gathered.shape[1]
+    height = basis.shape[0] // parts
+    half, rest = height // 2, basis.shape[1] - wide
+    copies = []
+    for n in range(parts):
+        at = (n + 1) * stride - half - height
+        pieces = [(at, height, 0, wide, n * height, 0)]
+        for h in range(2):
+            pieces.append((at + height, half, h * rest, rest, n * height + h * half, wide))
+        for row, rows, col, cols, to_row, to_col in pieces:
+            copies.append(
+                pltpu.make_async_copy(
+                    gathered.at[pl.ds(row, rows), pl.ds(col, cols)],
+                    basis.at[pl.ds(to_row, rows), pl.ds(to_col, cols)],
+                    sems.at[len(copies)],
+                )
+            )
+    for copy in copies:
+        copy.start()
+    for copy in copies:
+        copy.wait()
     width = 256
     for j in range(basis.shape[1] // width):
         cols = slice(j * width, (j + 1) * width)
@@ -95,17 +112,18 @@
             out[:, cols] = jnp.dot(grads[...], basis[:, cols], preferred_element_type=F32).astype(BF16)
 
 
-def rotate_out(mine, theirs, basis):
+def rotate_out(gathered, mine, theirs):
     tokens, depth = mine.shape
-    width = basis.shape[1]
+    width = depth // NC
     return pl.pallas_call(
         rotate_out_kernel,
         out_shape=[jax.ShapeDtypeStruct((tokens, width), BF16)] * 2,
-        in_specs=[VMEM] * 3,
+        in_specs=[ANY, VMEM, VMEM],
         out_specs=[VMEM] * 2,
+        scratch_shapes=[pltpu.VMEM((depth, width), BF16), pltpu.SemaphoreType.DMA((3 * NYL * NX,))],
         compiler_params=pltpu.CompilerParams(vmem_limit_bytes=LIMIT),
         cost_estimate=cost(4 * tokens * depth * width, 2 * (2 * tokens * (depth + width) + depth * width)),
-    )(mine, theirs, basis)
+    )(gathered, mine, theirs)
 
 
 def squares_kernel(outs_mine, outs_theirs, ins_mine, ins_theirs, out, top):
@@ -138,12 +156,14 @@
     )(outs_mine, outs_theirs, ins_mine, ins_theirs)
 
 
-def gather_in_basis(in_basis):
+def gather_in_basis(in_basis, grads):
     along_yh = [[(z * NYH + yh) * NC + c for yh in range(NYH)] for z in range(NZ) for c in range(NC)]
     along_z = [[z * NYH * NC + r for z in range(NZ)] for r in range(NYH * NC)]
     chunk = lax.all_gather(in_basis, "wide", axis=0, tiled=True, axis_index_groups=along_yh)
+    chunk, grads = lax.optimization_barrier((chunk, other_core(grads)))
     copies = jnp.broadcast_to(chunk[None], (NZ, *chunk.shape))
-    return lax.all_to_all(copies, "wide", 0, 0, axis_index_groups=along_z).reshape(-1, chunk.shape[1])
+    got = lax.all_to_all(copies, "wide", 0, 0, axis_index_groups=along_z)
+    return got.reshape(-1, chunk.shape[1]), grads
 
 
 def gather_packed(activations, picked):
@@ -192,15 +212,13 @@
     sequences = activations.shape[0] // SEQ * lax.axis_size("wide")
 
     gathered = gather_packed(activations, pick(out_basis, core))
-    mine = gather_in_basis(in_basis)
-    grads_other = other_core(out_grads)
+    mine, grads_other = gather_in_basis(in_basis, out_grads)
     other = other_core(mine)
-    gathered, other, grads_other = lax.optimization_barrier((gathered, other, grads_other))
+    gathered, other = lax.optimization_barrier((gathered, other))
     mask = valid.astype(F32)[:, None]
-    basis_shape = (out_basis.shape[1], out_basis.shape[1] // NC)
-    masked_in, basis = rotate_in(pos, gathered, mine, other, mask, basis_shape)
+    masked_in = rotate_in(pos, gathered, mine, other, mask)
     masked_other = other_core(masked_in)
-    out_mine, out_theirs = rotate_out(out_grads, grads_other, basis)
+    out_mine, out_theirs = rotate_out(gathered, out_grads, grads_other)
     total, top = squares(out_mine, out_theirs, masked_in, masked_other)
     return scatter_sum(total, jnp.max(top)) / sequences
 

time: 163 us -> 159 us (0.975)
  Pallas kernels: 16.3 us -> 12.2 us
  local copies, waits for them, and re-layouts: 1.66 us -> 3.52 us
    pallas_call x1, Pallas kernels: 9.28 us -> 5.8 us  [rotate_in(): pl.pallas_call(rotate_in_kernel, out_shape=jax.ShapeDtypeStruct((tokens,...]
    all_to_all x1, blocking collectives: 42.8 us -> 40.3 us  [scatter_sum(): lax.all_to_all(jnp.concatenate([coded, label], axis=1), 'wide', 0, 0, til...]
    unnamed x9 -> x17, local copies, waits for them, and re-layouts: 1.13 us -> 3 us
  transfers between devices with their start and end apart: 4 -> 4, of which waited for: 2 -> 1; matrix products, arithmetic and copies ran while one was open for 0% -> 0% of each run, Pallas kernels for 3% -> 3%
where the time goes in v10:
time: 159 us; the launch traced here: 158 us
  blocking collectives  115 us (72%)
  between operations  14.4 us (9%)
  Pallas kernels  12.2 us (8%)
  starting transfers between devices  5.86 us (4%)
  waiting for transfers between devices  3.97 us (2%)
  local copies, waits for them, and re-layouts  3.52 us (2%)
  other arithmetic  2.73 us (2%)
    all_to_all x1, blocking collectives, gather_in_basis(): got = lax.all_to_all(copies, 'wide', 0, 0, axis_index_groups=along_z)  59.2 us
    all_to_all x1, blocking collectives, scatter_sum(): lax.all_to_all(jnp.concatenate([coded, label], axis=1), 'wide', 0, 0, til...  40.3 us
    all_gather x1, blocking collectives, gather_in_basis(): lax.all_gather(in_basis, 'wide', axis=0, tiled=True, axis_index_groups=al...  15.1 us
    ppermute x3, starting transfers between devices, send(): return lax.ppermute(value, BOTH, pairs)  5.86 us
    pallas_call x1, Pallas kernels, rotate_in(): pl.pallas_call(rotate_in_kernel, out_shape=jax.ShapeDtypeStruct((tokens,...  5.8 us
    pallas_call x1, Pallas kernels, rotate_out(): pl.pallas_call(rotate_out_kernel, out_shape=[jax.ShapeDtypeStruct((tokens...  4.49 us
    ppermute x3, waiting for transfers between devices, send(): return lax.ppermute(value, BOTH, pairs)  3.95 us
  transfers between devices with their start and end apart: 4, of which 1 were waited for; matrix products, arithmetic and copies ran while one was open for 0% of the time, Pallas kernels for 3%

profile of v10, /device:TPU:50, one launch (start us, length us, event | category | flops | bytes accessed | tf_op | source)
XLA Modules:
  0.0 158.3 jit_solution(6647058317273025540)
XLA Ops:
  6.5 0.0 copy-start
  6.5 0.0 all-gather.2.cloned.1.call-start
  6.6 1.0 copy-done
  7.6 0.0 copy-start.5
  7.6 1.1 fusion.11
  8.7 0.0 copy-start.1
  8.7 0.0 copy-start.6
  8.8 0.0 copy-done.5
  8.8 1.0 maximum_maximum_fusion
  9.7 0.0 all-gather.2.cloned.1.call-update
  9.7 0.7 copy-done.1
  10.4 1.9 %collective-permute-start = (bf16[512,1536]{1,0:T(8,128)(2,1)S(1)}, bf16[512,1536]{1,0:T(8,128)(2,1)S(1)}, u32[]{:S(2)}, u32[]{:S(2)}) collective-permute-start(bf16[512,1536]{1,0:T(8,128)(2,1)S(1)} %copy-done.1), channel_id=1, source_target_pairs={{0,8},{1,9},{2,10},{3,11},{4,12},{5,13},{6,14},{7,15},{8,0},{9,1},... | collective-permute-start | bytes 4718600 | tf_op jit(solution)/shard_map/ppermute | solution.py:28
  12.3 0.0 copy-done.6
  12.3 15.1 %all_gather.7 = bf16[256,512]{1,0:T(8,128)(2,1)S(1)} all-gather(bf16[64,512]{1,0:T(8,128)(2,1)S(1)} %copy-done.6), channel_id=1, replica_groups={{0,16,32,48},{8,24,40,56},{64,80,96,112},{72,88,104,120},{128,144,160,1..., dimensions={0}, use_global_device_ids=true | all-gather | bytes 327680 | tf_op jit(solution)/shard_map/all_gather | solution.py:162
  27.4 0.0 collective-permute-done.theirs
  27.4 0.0 copy-start.3
  27.4 1.2 copy-done.3
  28.6 0.2 broadcast_in_dim.4
  28.8 0.0 copy-start.7
  28.8 59.2 %all_to_all.10 = bf16[8,256,512]{2,1,0:T(8,128)(2,1)S(1)} all-to-all(bf16[8,256,512]{2,1,0:T(8,128)(2,1)S(1)} %broadcast_in_dim.4), channel_id=1, replica_groups={{0,64,128,192,256,320,384,448},{8,72,136,200,264,328,392,456},{16,80,14..., dimensions={0} | all-to-all | bytes 4194304 | tf_op jit(solution)/shard_map/all_to_all | solution.py:165
  88.0 1.9 %collective-permute-start.1 = (bf16[2048,512]{1,0:T(8,128)(2,1)S(1)}, bf16[2048,512]{1,0:T(8,128)(2,1)}, u32[]{:S(2)}, u32[]{:S(2)}) collective-permute-start(bf16[2048,512]{1,0:T(8,128)(2,1)S(1)} %bitcast.21), channel_id=1, source_target_pairs={{0,8},{1,9},{2,10},{3,11},{4,12},{5,13},{6,14},{7,15},{8,0},{9,1},... | collective-permute-start | bytes 6291464 | tf_op jit(solution)/shard_map/ppermute | solution.py:28
  90.0 0.0 copy-done.7
  90.0 0.1 copy.11.mask
  90.1 0.1 pad_add_fusion.pos
  90.2 3.9 %collective-permute-done.1.other = bf16[2048,512]{1,0:T(8,128)(2,1)} collective-permute-done((bf16[2048,512]{1,0:T(8,128)(2,1)S(1)}, bf16[2048,512]{1,0:T(8,128)(2,1)}, u32[]{:S(2)}, u32[]{:S(2)}) %collective-permute-start.1) | collective-permute-done | bytes 2097184 | tf_op jit(solution)/shard_map/ppermute | solution.py:28
  94.2 0.0 all-gather.2.cloned.1.call-done.gathered
  94.2 0.0 copy-start.2
  94.2 0.0 copy-start.4
  94.2 5.8 %shard_map.56.ins_mine = bf16[512,512]{1,0:T(8,128)(2,1)S(1)} custom-call(s32[4]{0:T(128)S(1)} %pad_add_fusion.pos, bf16[6400,512]{1,0:T(8,128)(2,1)} %all-gather.2.cloned.1.call-done.gathered, bf16[2048,512]{1,0:T(8,128)(2,1)S(1)} %bitcast.22, bf16[2048,512]{1,0:T(8,128)(2,1)} %collective-permute-done.1.other, f32[512,1]{1,0:T(8,128)S(1)} %copy.11.mask), custom_call_target="tpu_custom_call" | custom-call | flops 2147483648 | bytes 8912896 | tf_op jit(solution)/shard_map/pallas_call | solution.py:70
  100.0 2.0 %collective-permute-start.2 = (bf16[512,512]{1,0:T(8,128)(2,1)S(1)}, bf16[512,512]{1,0:T(8,128)(2,1)S(1)}, u32[]{:S(2)}, u32[]{:S(2)}) collective-permute-start(bf16[512,512]{1,0:T(8,128)(2,1)S(1)} %shard_map.56.ins_mine), channel_id=1, source_target_pairs={{0,8},{1,9},{2,10},{3,11},{4,12},{5,13},{6,14},{7,15},{8,0},{9,1},... | collective-permute-start | bytes 1572872 | tf_op jit(solution)/shard_map/ppermute | solution.py:28
  102.0 0.0 copy-done.2
  102.0 0.0 copy-done.4
  102.1 4.5 %shard_map.55 = (bf16[512,768]{1,0:T(8,128)(2,1)S(1)}, bf16[512,768]{1,0:T(8,128)(2,1)S(1)}) custom-call(bf16[6400,512]{1,0:T(8,128)(2,1)} %all-gather.2.cloned.1.call-done.gathered, bf16[512,1536]{1,0:T(8,128)(2,1)S(1)} %copy-done.2, bf16[512,1536]{1,0:T(8,128)(2,1)S(1)} %copy-done.4), custom_call_target="tpu_custom_call" | custom-call | flops 2415919104 | bytes 7077888 | tf_op jit(solution)/shard_map/pallas_call | solution.py:118
  106.6 0.0 collective-permute-done.2.ins_theirs
  106.6 1.9 %shard_map.57 = (f32[768,512]{1,0:T(8,128)S(1)}, f32[8,512]{1,0:T(8,128)S(1)}) custom-call(bf16[512,768]{1,0:T(8,128)(2,1)S(1)} %get-tuple-element.16.outs_mine, bf16[512,768]{1,0:T(8,128)(2,1)S(1)} %get-tuple-element.17.outs_theirs, bf16[512,512]{1,0:T(8,128)(2,1)S(1)} %shard_map.56.ins_mine, bf16[512,512]{1,0:T(8,128)(2,1)S(1)} %collective-permute-done.2.ins_theirs), custom_call_target="tpu_custom_call" | custom-call | flops 805306368 | bytes 4194304 | tf_op jit(solution)/shard_map/pallas_call | solution.py:149
  108.4 0.6 reduce_max.9
  109.8 0.2 multiply_convert_fusion
  110.0 0.2 concatenate.11
  110.2 40.3 %all_to_all.11 = f16[32,104,128]{2,1,0:T(8,128)(2,1)S(1)} all-to-all(f16[32,104,128]{2,1,0:T(8,128)(2,1)S(1)} %concatenate.11), channel_id=1, replica_groups={{0,16,32,48,64,80,96,112,128,144,160,176,192,208,224,240,256,272,288,30..., dimensions={0} | all-to-all | bytes 1703936 | tf_op jit(solution)/shard_map/all_to_all | solution.py:199
  150.5 0.1 copy.13
  150.6 0.2 multiply_reduce_fusion
  150.9 0.6 broadcast_multiply_fusion
  (8 shorter events, 0.1 us)
Async XLA Ops:
  6.5 1.1 copy-start
  6.5 87.6 %all-gather.2.cloned.1.call-start = ((), (), s32[]{:S(2)}) async-start(), calls=%async_computation.2 | async-start | bytes 7372800 | tf_op jit(solution)/shard_map/all_gather | solution.py:174
  7.6 1.2 copy-start.5
  8.7 1.7 %copy-start.1 = (bf16[512,1536]{1,0:T(8,128)(2,1)S(1)}, bf16[512,1536]{1,0:T(8,128)(2,1)}, u32[]{:S(2)}) copy-start(bf16[512,1536]{1,0:T(8,128)(2,1)} %mine.1) | copy-start | bytes 4718596
  8.7 3.6 %copy-start.6 = (bf16[64,512]{1,0:T(8,128)(2,1)S(1)}, bf16[64,512]{1,0:T(8,128)(2,1)}, u32[]{:S(2)}) copy-start(bf16[64,512]{1,0:T(8,128)(2,1)} %param.7) | copy-start | bytes 196612
  10.4 17.0 %collective-permute-start = (bf16[512,1536]{1,0:T(8,128)(2,1)S(1)}, bf16[512,1536]{1,0:T(8,128)(2,1)S(1)}, u32[]{:S(2)}, u32[]{:S(2)}) collective-permute-start(bf16[512,1536]{1,0:T(8,128)(2,1)S(1)} %copy-done.1), channel_id=1, source_target_pairs={{0,8},{1,9},{2,10},{3,11},{4,12},{5,13},{6,14},{7,15},{8,0},{9,1},... | collective-permute-start | bytes 4718600 | tf_op jit(solution)/shard_map/ppermute | solution.py:28
  27.4 1.2 copy-start.3
  28.8 61.2 %copy-start.7 = (s32[512]{0:T(512)S(1)}, s32[512]{0:T(512)}, u32[]{:S(2)}) copy-start(s32[512]{0:T(512)} %param.9) | copy-start | bytes 6148
  88.0 6.2 %collective-permute-start.1 = (bf16[2048,512]{1,0:T(8,128)(2,1)S(1)}, bf16[2048,512]{1,0:T(8,128)(2,1)}, u32[]{:S(2)}, u32[]{:S(2)}) collective-permute-start(bf16[2048,512]{1,0:T(8,128)(2,1)S(1)} %bitcast.21), channel_id=1, source_target_pairs={{0,8},{1,9},{2,10},{3,11},{4,12},{5,13},{6,14},{7,15},{8,0},{9,1},... | collective-permute-start | bytes 6291464 | tf_op jit(solution)/shard_map/ppermute | solution.py:28
  94.2 7.9 %copy-start.2 = (bf16[512,1536]{1,0:T(8,128)(2,1)S(1)}, bf16[512,1536]{1,0:T(8,128)(2,1)}, u32[]{:S(2)}) copy-start(bf16[512,1536]{1,0:T(8,128)(2,1)} %mine.1) | copy-start | bytes 4718596
  94.2 7.9 %copy-start.4 = (bf16[512,1536]{1,0:T(8,128)(2,1)S(1)}, bf16[512,1536]{1,0:T(8,128)(2,1)}, u32[]{:S(2)}) copy-start(bf16[512,1536]{1,0:T(8,128)(2,1)} %copy-done.3) | copy-start | bytes 4718596
  100.0 6.6 %collective-permute-start.2 = (bf16[512,512]{1,0:T(8,128)(2,1)S(1)}, bf16[512,512]{1,0:T(8,128)(2,1)S(1)}, u32[]{:S(2)}, u32[]{:S(2)}) collective-permute-start(bf16[512,512]{1,0:T(8,128)(2,1)S(1)} %shard_map.56.ins_mine), channel_id=1, source_target_pairs={{0,8},{1,9},{2,10},{3,11},{4,12},{5,13},{6,14},{7,15},{8,0},{9,1},... | collective-permute-start | bytes 1572872 | tf_op jit(solution)/shard_map/ppermute | solution.py:28
Sparse Core Ops, SparseCore 0:
  9.9 81.9 all-gather.1

commit v11 on v10

--- a/solution.py
+++ b/solution.py
@@ -36,8 +36,8 @@
     return pl.CostEstimate(flops=flops, bytes_accessed=nbytes, transcendentals=0)
 
 
-def rotate_in_kernel(pos, gathered, mine, other, mask, out, blocks, basis, sems):
-    core, parts = pos[3], blocks.shape[0]
+def rotate_in_kernel(pos, gathered, mine, mine_next, other, other_next, mask, out, blocks, basis, sems):
+    parity, core, parts = lax.rem(pos[0], 2), pos[3], blocks.shape[0]
     stride, (tokens, depth) = gathered.shape[0] // parts, blocks.shape[1:]
     copies = [
         pltpu.make_async_copy(gathered.at[pl.ds(n * stride, tokens), :], blocks.at[n], sems.at[n])
@@ -45,32 +45,32 @@
     ]
     for copy in copies:
         copy.start()
-    rows = mine.shape[0] // (NZ * NYH)
-    for i in range(NZ * NYH):
-        for ref, c in ((mine, core), (other, 1 - core)):
-            at = pl.multiple_of((i * NC + c) * rows, rows)
+    rows = basis.shape[0] // (NZ * NYH * NC)
+    for ref, c, first in ((mine, core, 0), (mine_next, core, 1), (other, 1 - core, 0), (other_next, 1 - core, 1)):
+        odd = lax.rem(parity + first, 2)
+        for i in range(NZ // 2 * NYH):
+            z, yh = 2 * (i // NYH) + odd, i % NYH
+            at = pl.multiple_of(((z * NYH + yh) * NC + c) * rows, rows)
             basis[pl.ds(at, rows), :] = ref[i * rows : (i + 1) * rows, :]
-    half = tokens // 2
-    for part in range(2):
-        here = slice(part * half, (part + 1) * half)
-        total = jnp.zeros((half, out.shape[1]), F32)
+    width = 256
+    for j in range(out.shape[1] // width):
+        cols = slice(j * width, (j + 1) * width)
+        total = jnp.zeros((tokens, width), F32)
         for n in range(parts):
-            if part == 0:
+            if j == 0:
                 copies[n].wait()
-            total += jnp.dot(
-                blocks[n, here, :], basis[n * depth : (n + 1) * depth, :], preferred_element_type=F32
-            )
-        out[here, :] = (total.astype(BF16).astype(F32) * mask[here, :]).astype(BF16)
-
-
-def rotate_in(pos, gathered, mine, other, mask):
+            total += jnp.dot(blocks[n], basis[n * depth : (n + 1) * depth, cols], preferred_element_type=F32)
+        out[:, cols] = (total.astype(BF16).astype(F32) * mask[...]).astype(BF16)
+
+
+def rotate_in(pos, gathered, planes, mask):
     parts = NYL * NX
-    tokens, width = mask.shape[0], mine.shape[1]
-    depth = 2 * mine.shape[0]
+    tokens, width = mask.shape[0], planes[0].shape[1]
+    depth = len(planes) * planes[0].shape[0]
     return pl.pallas_call(
         rotate_in_kernel,
         out_shape=jax.ShapeDtypeStruct((tokens, width), BF16),
-        in_specs=[SMEM, ANY, VMEM, VMEM, VMEM],
+        in_specs=[SMEM, ANY] + [VMEM] * 5,
         out_specs=VMEM,
         scratch_shapes=[
             pltpu.VMEM((parts, tokens, depth // parts), BF16),
@@ -79,28 +79,34 @@
         ],
         compiler_params=pltpu.CompilerParams(vmem_limit_bytes=LIMIT),
         cost_estimate=cost(2 * tokens * depth * width, 2 * (tokens * depth + depth * width + tokens * width)),
-    )(pos, gathered, mine, other, mask)
-
-
-def rotate_out_kernel(gathered, mine, theirs, out_mine, out_theirs, basis, sems):
-    parts = NYL * NX
-    stride, wide = gathered.shape[0] // parts, gathered.shape[1]
-    height = basis.shape[0] // parts
+    )(pos, gathered, *planes, mask)
+
+
+def rotate_out_kernel(pos, gathered, below, above, mine, theirs, out_mine, out_theirs, basis, sems):
+    parity, parts = lax.rem(pos[0], 2), NYL * NX
+    wide = gathered.shape[1]
+    height = basis.shape[0] // parts // 2
     half, rest = height // 2, basis.shape[1] - wide
+    stride, packed = gathered.shape[0] // parts, height + half
     copies = []
     for n in range(parts):
-        at = (n + 1) * stride - half - height
-        pieces = [(at, height, 0, wide, n * height, 0)]
-        for h in range(2):
-            pieces.append((at + height, half, h * rest, rest, n * height + h * half, wide))
-        for row, rows, col, cols, to_row, to_col in pieces:
-            copies.append(
-                pltpu.make_async_copy(
-                    gathered.at[pl.ds(row, rows), pl.ds(col, cols)],
-                    basis.at[pl.ds(to_row, rows), pl.ds(to_col, cols)],
-                    sems.at[len(copies)],
+        near = below if n < parts // 2 else above
+        for ref, at, q in (
+            (gathered, (n + 1) * stride - packed, parity),
+            (near, n % (parts // 2) * packed, 1 - parity),
+        ):
+            top = (2 * n + q) * height
+            pieces = [(at, height, 0, wide, top, 0)]
+            for h in range(2):
+                pieces.append((at + height, half, h * rest, rest, top + h * half, wide))
+            for row, rows, col, cols, to_row, to_col in pieces:
+                copies.append(
+                    pltpu.make_async_copy(
+                        ref.at[pl.ds(row, rows), pl.ds(col, cols)],
+                        basis.at[pl.ds(pl.multiple_of(to_row, 16), rows), pl.ds(to_col, cols)],
+                        sems.at[len(copies)],
+                    )
                 )
-            )
     for copy in copies:
         copy.start()
     for copy in copies:
@@ -112,18 +118,18 @@
             out[:, cols] = jnp.dot(grads[...], basis[:, cols], preferred_element_type=F32).astype(BF16)
 
 
-def rotate_out(gathered, mine, theirs):
+def rotate_out(pos, gathered, below, above, mine, theirs):
     tokens, depth = mine.shape
     width = depth // NC
     return pl.pallas_call(
         rotate_out_kernel,
         out_shape=[jax.ShapeDtypeStruct((tokens, width), BF16)] * 2,
-        in_specs=[ANY, VMEM, VMEM],
+        in_specs=[SMEM, ANY, ANY, ANY, VMEM, VMEM],
         out_specs=[VMEM] * 2,
-        scratch_shapes=[pltpu.VMEM((depth, width), BF16), pltpu.SemaphoreType.DMA((3 * NYL * NX,))],
+        scratch_shapes=[pltpu.VMEM((depth, width), BF16), pltpu.SemaphoreType.DMA((6 * NYL * NX,))],
         compiler_params=pltpu.CompilerParams(vmem_limit_bytes=LIMIT),
         cost_estimate=cost(4 * tokens * depth * width, 2 * (2 * tokens * (depth + width) + depth * width)),
-    )(gathered, mine, theirs)
+    )(pos, gathered, below, above, mine, theirs)
 
 
 def squares_kernel(outs_mine, outs_theirs, ins_mine, ins_theirs, out, top):
@@ -156,14 +162,26 @@
     )(outs_mine, outs_theirs, ins_mine, ins_theirs)
 
 
+def to_all(value, groups):
+    copies = jnp.broadcast_to(value[None], (len(groups[0]), *value.shape))
+    return lax.all_to_all(copies, "wide", 0, 0, axis_index_groups=groups).reshape(-1, value.shape[1])
+
+
+def from_z_neighbours(value):
+    half = value.shape[0] // 2
+    below = send(value[:half], lambda z, yh, c, yl, x: (z + 1, yh, c, yl, x))
+    above = send(value[half:], lambda z, yh, c, yl, x: (z - 1, yh, c, yl, x))
+    return below, above
+
+
 def gather_in_basis(in_basis, grads):
     along_yh = [[(z * NYH + yh) * NC + c for yh in range(NYH)] for z in range(NZ) for c in range(NC)]
-    along_z = [[z * NYH * NC + r for z in range(NZ)] for r in range(NYH * NC)]
-    chunk = lax.all_gather(in_basis, "wide", axis=0, tiled=True, axis_index_groups=along_yh)
+    along_z = [[z * NYH * NC + r for z in range(p, NZ, 2)] for p in range(2) for r in range(NYH * NC)]
+    chunk = to_all(in_basis, along_yh)
     chunk, grads = lax.optimization_barrier((chunk, other_core(grads)))
-    copies = jnp.broadcast_to(chunk[None], (NZ, *chunk.shape))
-    got = lax.all_to_all(copies, "wide", 0, 0, axis_index_groups=along_z)
-    return got.reshape(-1, chunk.shape[1]), grads
+    planes = to_all(chunk, along_z)
+    following = jnp.concatenate(from_z_neighbours(planes), axis=0)
+    return (planes, following, other_core(planes), other_core(following)), grads
 
 
 def gather_packed(activations, picked):
@@ -211,14 +229,16 @@
     pos = jnp.stack([z, yl, x, core]).astype(jnp.int32)
     sequences = activations.shape[0] // SEQ * lax.axis_size("wide")
 
-    gathered = gather_packed(activations, pick(out_basis, core))
-    mine, grads_other = gather_in_basis(in_basis, out_grads)
-    other = other_core(mine)
-    gathered, other = lax.optimization_barrier((gathered, other))
+    height = out_basis.shape[0] // 2
+    parity_rows = lax.dynamic_slice_in_dim(out_basis, lax.rem(z, 2) * height, height, 0)
+    gathered = gather_packed(activations, pick(parity_rows, core))
+    planes, grads_other = gather_in_basis(in_basis, out_grads)
+    basis = gathered.reshape(NYL * NX, -1, gathered.shape[1])[:, activations.shape[0] :]
+    below, above = from_z_neighbours(basis.reshape(-1, gathered.shape[1]))
     mask = valid.astype(F32)[:, None]
-    masked_in = rotate_in(pos, gathered, mine, other, mask)
+    masked_in = rotate_in(pos, gathered, planes, mask)
     masked_other = other_core(masked_in)
-    out_mine, out_theirs = rotate_out(gathered, out_grads, grads_other)
+    out_mine, out_theirs = rotate_out(pos, gathered, below, above, out_grads, grads_other)
     total, top = squares(out_mine, out_theirs, masked_in, masked_other)
     return scatter_sum(total, jnp.max(top)) / sequences
 

time: 159 us -> 163 us (1.025)
  the two profiles are of different devices: /device:TPU:50 before, /device:TPU:64 now
where the time goes in v11:
time: 163 us; the launch traced here: 162 us
  blocking collectives  92.1 us (57%)
  starting transfers between devices  19.4 us (12%)
  between operations  14.5 us (9%)
  Pallas kernels  14.4 us (9%)
  waiting for transfers between devices  13.1 us (8%)
  local copies, waits for them, and re-layouts  4.9 us (3%)
  other arithmetic  2.66 us (2%)
    all_to_all x2, blocking collectives, to_all(): lax.all_to_all(copies, 'wide', 0, 0, axis_index_groups=groups)  54.3 us
    all_to_all x1, blocking collectives, scatter_sum(): lax.all_to_all(jnp.concatenate([coded, label], axis=1), 'wide', 0, 0, til...  37.8 us
    ppermute x8, starting transfers between devices, send(): return lax.ppermute(value, BOTH, pairs)  19.4 us
    ppermute x8, waiting for transfers between devices, send(): return lax.ppermute(value, BOTH, pairs)  13.1 us
    pallas_call x1, Pallas kernels, rotate_in(): pl.pallas_call(rotate_in_kernel, out_shape=jax.ShapeDtypeStruct((tokens,...  7.57 us
    pallas_call x1, Pallas kernels, rotate_out(): pl.pallas_call(rotate_out_kernel, out_shape=[jax.ShapeDtypeStruct((tokens...  4.98 us
  transfers between devices with their start and end apart: 9, of which 4 were waited for; matrix products, arithmetic and copies ran while one was open for 1% of the time, Pallas kernels for 8%

profile of v11, /device:TPU:64, one launch (start us, length us, event | category | flops | bytes accessed | tf_op | source)
XLA Modules:
  0.0 162.1 jit_solution(394561759898850388)
XLA Ops:
  6.5 0.0 copy-start
  6.5 0.0 all-gather.2.cloned.1.call-start
  6.6 1.0 copy-done
  7.6 0.0 copy-start.5
  7.6 1.1 fusion.10
  8.7 0.0 copy-start.1
  8.7 0.0 copy-start.6
  8.7 0.0 copy-done.5
  8.7 0.9 maximum_maximum_fusion
  9.6 0.0 all-gather.2.cloned.1.call-update
  9.6 0.7 copy-done.1
  10.3 1.9 %collective-permute-start.2 = (bf16[512,1536]{1,0:T(8,128)(2,1)S(1)}, bf16[512,1536]{1,0:T(8,128)(2,1)S(1)}, u32[]{:S(2)}, u32[]{:S(2)}) collective-permute-start(bf16[512,1536]{1,0:T(8,128)(2,1)S(1)} %copy-done.1), channel_id=1, source_target_pairs={{0,8},{1,9},{2,10},{3,11},{4,12},{5,13},{6,14},{7,15},{8,0},{9,1},... | collective-permute-start | bytes 4718600 | tf_op jit(solution)/shard_map/ppermute | solution.py:28
  12.2 0.0 copy-done.6
  12.3 18.3 %all_to_all.15 = bf16[4,64,512]{2,1,0:T(8,128)(2,1)S(1)} all-to-all(bf16[4,64,512]{2,1,0:T(8,128)(2,1)S(1)} %broadcast_in_dim.6), channel_id=1, replica_groups={{0,16,32,48},{8,24,40,56},{64,80,96,112},{72,88,104,120},{128,144,160,1..., dimensions={0} | all-to-all | bytes 524288 | tf_op jit(solution)/shard_map/all_to_all | solution.py:167
  30.6 0.0 collective-permute-done.2.theirs
  30.6 0.0 copy-start.3
  30.6 1.2 copy-done.3
  31.8 0.1 broadcast_in_dim.7
  31.9 35.9 %all_to_all.16 = bf16[4,256,512]{2,1,0:T(8,128)(2,1)S(1)} all-to-all(bf16[4,256,512]{2,1,0:T(8,128)(2,1)S(1)} %broadcast_in_dim.7), channel_id=1, replica_groups={{0,128,256,384},{8,136,264,392},{16,144,272,400},{24,152,280,408},{32,1..., dimensions={0} | all-to-all | bytes 2097152 | tf_op jit(solution)/shard_map/all_to_all | solution.py:167
  67.8 0.1 fusion.22
  67.9 0.0 copy-start.7
  67.9 2.2 %collective-permute-start.3 = (bf16[512,512]{1,0:T(8,128)(2,1)S(1)}, bf16[512,512]{1,0:T(8,128)(2,1)S(1)}, u32[]{:S(2)}, u32[]{:S(2)}) collective-permute-start(bf16[512,512]{1,0:T(8,128)(2,1)S(1)} %bitcast.32), channel_id=1, source_target_pairs={{0,64},{1,65},{2,66},{3,67},{4,68},{5,69},{6,70},{7,71},{8,72},{9,... | collective-permute-start | bytes 1572872 | tf_op jit(solution)/shard_map/ppermute | solution.py:28
  70.1 3.6 %collective-permute-start.4 = (bf16[512,512]{1,0:T(8,128)(2,1)S(1)}, bf16[512,512]{1,0:T(8,128)(2,1)S(1)}, u32[]{:S(2)}, u32[]{:S(2)}) collective-permute-start(bf16[512,512]{1,0:T(8,128)(2,1)S(1)} %bitcast.31), channel_id=1, source_target_pairs={{0,448},{1,449},{2,450},{3,451},{4,452},{5,453},{6,454},{7,455},{8... | collective-permute-start | bytes 1572872 | tf_op jit(solution)/shard_map/ppermute | solution.py:28
  73.7 1.9 %collective-permute-start.5 = (bf16[1024,512]{1,0:T(8,128)(2,1)S(1)}, bf16[1024,512]{1,0:T(8,128)(2,1)}, u32[]{:S(2)}, u32[]{:S(2)}) collective-permute-start(bf16[1024,512]{1,0:T(8,128)(2,1)S(1)} %bitcast.24), channel_id=1, source_target_pairs={{0,8},{1,9},{2,10},{3,11},{4,12},{5,13},{6,14},{7,15},{8,0},{9,1},... | collective-permute-start | bytes 3145736 | tf_op jit(solution)/shard_map/ppermute | solution.py:28
  75.7 7.1 %collective-permute-done.3 = bf16[512,512]{1,0:T(8,128)(2,1)S(1)} collective-permute-done((bf16[512,512]{1,0:T(8,128)(2,1)S(1)}, bf16[512,512]{1,0:T(8,128)(2,1)S(1)}, u32[]{:S(2)}, u32[]{:S(2)}) %collective-permute-start.3) | collective-permute-done | bytes 524320 | tf_op jit(solution)/shard_map/ppermute | solution.py:28
  82.8 1.9 %collective-permute-done.4 = bf16[512,512]{1,0:T(8,128)(2,1)S(1)} collective-permute-done((bf16[512,512]{1,0:T(8,128)(2,1)S(1)}, bf16[512,512]{1,0:T(8,128)(2,1)S(1)}, u32[]{:S(2)}, u32[]{:S(2)}) %collective-permute-start.4) | collective-permute-done | bytes 524320 | tf_op jit(solution)/shard_map/ppermute | solution.py:28
  84.8 1.9 %collective-permute-start.6 = (bf16[1024,512]{1,0:T(8,128)(2,1)S(1)}, bf16[1024,512]{1,0:T(8,128)(2,1)}, u32[]{:S(2)}, u32[]{:S(2)}) collective-permute-start(bf16[1024,512]{1,0:T(8,128)(2,1)S(1)} %constant_dynamic-update-slice_fusion.mine_next), channel_id=1, source_target_pairs={{0,8},{1,9},{2,10},{3,11},{4,12},{5,13},{6,14},{7,15},{8,0},{9,1},... | collective-permute-start | bytes 3145736 | tf_op jit(solution)/shard_map/ppermute | solution.py:28
  86.7 0.0 copy-done.7
  86.7 0.1 copy.11.mask
  86.9 0.0 all-gather.2.cloned.1.call-done.gathered
  86.9 1.3 fusion.21
  88.3 1.9 %collective-permute-start = (bf16[576,512]{1,0:T(8,128)(2,1)S(1)}, bf16[576,512]{1,0:T(8,128)(2,1)S(1)}, u32[]{:S(2)}, u32[]{:S(2)}) collective-permute-start(bf16[576,512]{1,0:T(8,128)(2,1)S(1)} %bitcast.30), channel_id=1, source_target_pairs={{0,64},{1,65},{2,66},{3,67},{4,68},{5,69},{6,70},{7,71},{8,72},{9,... | collective-permute-start | bytes 1769480 | tf_op jit(solution)/shard_map/ppermute | solution.py:28
  90.2 3.9 %collective-permute-start.1 = (bf16[576,512]{1,0:T(8,128)(2,1)S(1)}, bf16[576,512]{1,0:T(8,128)(2,1)S(1)}, u32[]{:S(2)}, u32[]{:S(2)}) collective-permute-start(bf16[576,512]{1,0:T(8,128)(2,1)S(1)} %bitcast.29), channel_id=1, source_target_pairs={{0,448},{1,449},{2,450},{3,451},{4,452},{5,453},{6,454},{7,455},{8... | collective-permute-start | bytes 1769480 | tf_op jit(solution)/shard_map/ppermute | solution.py:28
  94.1 0.1 pad_add_fusion.pos
  94.2 0.0 copy-start.2
  94.2 0.0 copy-start.4
  94.2 0.0 collective-permute-done.5.other
  94.2 0.0 collective-permute-done.6.other_next
  94.2 7.6 %shard_map.56.ins_mine = bf16[512,512]{1,0:T(8,128)(2,1)S(1)} custom-call(s32[4]{0:T(128)S(1)} %pad_add_fusion.pos, bf16[5248,512]{1,0:T(8,128)(2,1)} %all-gather.2.cloned.1.call-done.gathered, bf16[1024,512]{1,0:T(8,128)(2,1)S(1)} %bitcast.25, bf16[1024,512]{1,0:T(8,128)(2,1)S(1)} %constant_dynamic-update-slice_fusion.mine_next, ...), custom_call_target="tpu_custom_call" | custom-call | flops 2147483648 | bytes 8912896 | tf_op jit(solution)/shard_map/pallas_call | solution.py:70
  101.8 1.9 %collective-permute-start.7 = (bf16[512,512]{1,0:T(8,128)(2,1)S(1)}, bf16[512,512]{1,0:T(8,128)(2,1)S(1)}, u32[]{:S(2)}, u32[]{:S(2)}) collective-permute-start(bf16[512,512]{1,0:T(8,128)(2,1)S(1)} %shard_map.56.ins_mine), channel_id=1, source_target_pairs={{0,8},{1,9},{2,10},{3,11},{4,12},{5,13},{6,14},{7,15},{8,0},{9,1},... | collective-permute-start | bytes 1572872 | tf_op jit(solution)/shard_map/ppermute | solution.py:28
  103.7 2.2 %collective-permute-done.below = bf16[576,512]{1,0:T(8,128)(2,1)S(1)} collective-permute-done((bf16[576,512]{1,0:T(8,128)(2,1)S(1)}, bf16[576,512]{1,0:T(8,128)(2,1)S(1)}, u32[]{:S(2)}, u32[]{:S(2)}) %collective-permute-start) | collective-permute-done | bytes 589856 | tf_op jit(solution)/shard_map/ppermute | solution.py:28
  105.9 1.9 %collective-permute-done.1.above = bf16[576,512]{1,0:T(8,128)(2,1)S(1)} collective-permute-done((bf16[576,512]{1,0:T(8,128)(2,1)S(1)}, bf16[576,512]{1,0:T(8,128)(2,1)S(1)}, u32[]{:S(2)}, u32[]{:S(2)}) %collective-permute-start.1) | collective-permute-done | bytes 589856 | tf_op jit(solution)/shard_map/ppermute | solution.py:28
  107.8 0.0 copy-done.2
  107.8 0.0 copy-done.4
  107.8 5.0 %shard_map.55 = (bf16[512,768]{1,0:T(8,128)(2,1)S(1)}, bf16[512,768]{1,0:T(8,128)(2,1)S(1)}) custom-call(s32[4]{0:T(128)S(1)} %pad_add_fusion.pos, bf16[5248,512]{1,0:T(8,128)(2,1)} %all-gather.2.cloned.1.call-done.gathered, bf16[576,512]{1,0:T(8,128)(2,1)S(1)} %collective-permute-done.below, bf16[576,512]{1,0:T(8,128)(2,1)S(1)} %collective-permute-done.1.above, ...), custom_call_target="tpu_custom_call" | custom-call | flops 2415919104 | bytes 7077888 | tf_op jit(solution)/shard_map/pallas_call | solution.py:124
  112.8 0.0 collective-permute-done.7.ins_theirs
  112.8 1.8 %shard_map.57 = (f32[768,512]{1,0:T(8,128)S(1)}, f32[8,512]{1,0:T(8,128)S(1)}) custom-call(bf16[512,768]{1,0:T(8,128)(2,1)S(1)} %get-tuple-element.12.outs_mine, bf16[512,768]{1,0:T(8,128)(2,1)S(1)} %get-tuple-element.13.outs_theirs, bf16[512,512]{1,0:T(8,128)(2,1)S(1)} %shard_map.56.ins_mine, bf16[512,512]{1,0:T(8,128)(2,1)S(1)} %collective-permute-done.7.ins_theirs), custom_call_target="tpu_custom_call" | custom-call | flops 805306368 | bytes 4194304 | tf_op jit(solution)/shard_map/pallas_call | solution.py:155
  114.7 0.6 reduce_max.9
  116.0 0.2 multiply_convert_fusion
  116.2 0.2 concatenate.15
  116.4 37.8 %all_to_all.17 = f16[32,104,128]{2,1,0:T(8,128)(2,1)S(1)} all-to-all(f16[32,104,128]{2,1,0:T(8,128)(2,1)S(1)} %concatenate.15), channel_id=1, replica_groups={{0,16,32,48,64,80,96,112,128,144,160,176,192,208,224,240,256,272,288,30..., dimensions={0} | all-to-all | bytes 1703936 | tf_op jit(solution)/shard_map/all_to_all | solution.py:217
  154.3 0.1 copy.13
  154.4 0.2 multiply_reduce_fusion
  154.6 0.6 broadcast_multiply_fusion
  (11 shorter events, 0.2 us)
Async XLA Ops:
  6.5 1.1 copy-start
  6.5 80.4 %all-gather.2.cloned.1.call-start = ((), (), s32[]{:S(2)}) async-start(), calls=%async_computation.3 | async-start | bytes 6045696 | tf_op jit(solution)/shard_map/all_gather | solution.py:192
  7.6 1.1 copy-start.5
  8.7 1.7 %copy-start.1 = (bf16[512,1536]{1,0:T(8,128)(2,1)S(1)}, bf16[512,1536]{1,0:T(8,128)(2,1)}, u32[]{:S(2)}) copy-start(bf16[512,1536]{1,0:T(8,128)(2,1)} %mine.1) | copy-start | bytes 4718596
  8.7 3.6 %copy-start.6 = (bf16[64,512]{1,0:T(8,128)(2,1)S(1)}, bf16[64,512]{1,0:T(8,128)(2,1)}, u32[]{:S(2)}) copy-start(bf16[64,512]{1,0:T(8,128)(2,1)} %param.7) | copy-start | bytes 196612
  10.3 20.3 %collective-permute-start.2 = (bf16[512,1536]{1,0:T(8,128)(2,1)S(1)}, bf16[512,1536]{1,0:T(8,128)(2,1)S(1)}, u32[]{:S(2)}, u32[]{:S(2)}) collective-permute-start(bf16[512,1536]{1,0:T(8,128)(2,1)S(1)} %copy-done.1), channel_id=1, source_target_pairs={{0,8},{1,9},{2,10},{3,11},{4,12},{5,13},{6,14},{7,15},{8,0},{9,1},... | collective-permute-start | bytes 4718600 | tf_op jit(solution)/shard_map/ppermute | solution.py:28
  30.6 1.2 copy-start.3
  67.9 18.8 %copy-start.7 = (s32[512]{0:T(512)S(1)}, s32[512]{0:T(512)}, u32[]{:S(2)}) copy-start(s32[512]{0:T(512)} %param.9) | copy-start | bytes 6148
  67.9 14.9 %collective-permute-start.3 = (bf16[512,512]{1,0:T(8,128)(2,1)S(1)}, bf16[512,512]{1,0:T(8,128)(2,1)S(1)}, u32[]{:S(2)}, u32[]{:S(2)}) collective-permute-start(bf16[512,512]{1,0:T(8,128)(2,1)S(1)} %bitcast.32), channel_id=1, source_target_pairs={{0,64},{1,65},{2,66},{3,67},{4,68},{5,69},{6,70},{7,71},{8,72},{9,... | collective-permute-start | bytes 1572872 | tf_op jit(solution)/shard_map/ppermute | solution.py:28
  70.1 14.6 %collective-permute-start.4 = (bf16[512,512]{1,0:T(8,128)(2,1)S(1)}, bf16[512,512]{1,0:T(8,128)(2,1)S(1)}, u32[]{:S(2)}, u32[]{:S(2)}) collective-permute-start(bf16[512,512]{1,0:T(8,128)(2,1)S(1)} %bitcast.31), channel_id=1, source_target_pairs={{0,448},{1,449},{2,450},{3,451},{4,452},{5,453},{6,454},{7,455},{8... | collective-permute-start | bytes 1572872 | tf_op jit(solution)/shard_map/ppermute | solution.py:28
  73.7 20.5 %collective-permute-start.5 = (bf16[1024,512]{1,0:T(8,128)(2,1)S(1)}, bf16[1024,512]{1,0:T(8,128)(2,1)}, u32[]{:S(2)}, u32[]{:S(2)}) collective-permute-start(bf16[1024,512]{1,0:T(8,128)(2,1)S(1)} %bitcast.24), channel_id=1, source_target_pairs={{0,8},{1,9},{2,10},{3,11},{4,12},{5,13},{6,14},{7,15},{8,0},{9,1},... | collective-permute-start | bytes 3145736 | tf_op jit(solution)/shard_map/ppermute | solution.py:28
  84.8 9.4 %collective-permute-start.6 = (bf16[1024,512]{1,0:T(8,128)(2,1)S(1)}, bf16[1024,512]{1,0:T(8,128)(2,1)}, u32[]{:S(2)}, u32[]{:S(2)}) collective-permute-start(bf16[1024,512]{1,0:T(8,128)(2,1)S(1)} %constant_dynamic-update-slice_fusion.mine_next), channel_id=1, source_target_pairs={{0,8},{1,9},{2,10},{3,11},{4,12},{5,13},{6,14},{7,15},{8,0},{9,1},... | collective-permute-start | bytes 3145736 | tf_op jit(solution)/shard_map/ppermute | solution.py:28
  88.3 17.6 %collective-permute-start = (bf16[576,512]{1,0:T(8,128)(2,1)S(1)}, bf16[576,512]{1,0:T(8,128)(2,1)S(1)}, u32[]{:S(2)}, u32[]{:S(2)}) collective-permute-start(bf16[576,512]{1,0:T(8,128)(2,1)S(1)} %bitcast.30), channel_id=1, source_target_pairs={{0,64},{1,65},{2,66},{3,67},{4,68},{5,69},{6,70},{7,71},{8,72},{9,... | collective-permute-start | bytes 1769480 | tf_op jit(solution)/shard_map/ppermute | solution.py:28
  90.2 17.6 %collective-permute-start.1 = (bf16[576,512]{1,0:T(8,128)(2,1)S(1)}, bf16[576,512]{1,0:T(8,128)(2,1)S(1)}, u32[]{:S(2)}, u32[]{:S(2)}) collective-permute-start(bf16[576,512]{1,0:T(8,128)(2,1)S(1)} %bitcast.29), channel_id=1, source_target_pairs={{0,448},{1,449},{2,450},{3,451},{4,452},{5,453},{6,454},{7,455},{8... | collective-permute-start | bytes 1769480 | tf_op jit(solution)/shard_map/ppermute | solution.py:28
  94.2 13.6 %copy-start.2 = (bf16[512,1536]{1,0:T(8,128)(2,1)S(1)}, bf16[512,1536]{1,0:T(8,128)(2,1)}, u32[]{:S(2)}) copy-start(bf16[512,1536]{1,0:T(8,128)(2,1)} %mine.1) | copy-start | bytes 4718596
  94.2 13.6 %copy-start.4 = (bf16[512,1536]{1,0:T(8,128)(2,1)S(1)}, bf16[512,1536]{1,0:T(8,128)(2,1)}, u32[]{:S(2)}) copy-start(bf16[512,1536]{1,0:T(8,128)(2,1)} %copy-done.3) | copy-start | bytes 4718596
  101.8 11.0 %collective-permute-start.7 = (bf16[512,512]{1,0:T(8,128)(2,1)S(1)}, bf16[512,512]{1,0:T(8,128)(2,1)S(1)}, u32[]{:S(2)}, u32[]{:S(2)}) collective-permute-start(bf16[512,512]{1,0:T(8,128)(2,1)S(1)} %shard_map.56.ins_mine), channel_id=1, source_target_pairs={{0,8},{1,9},{2,10},{3,11},{4,12},{5,13},{6,14},{7,15},{8,0},{9,1},... | collective-permute-start | bytes 1572872 | tf_op jit(solution)/shard_map/ppermute | solution.py:28
Sparse Core Ops, SparseCore 0:
  9.8 72.8 all-gather.1

commit v12 on v11

--- a/solution.py
+++ b/solution.py
@@ -52,15 +52,17 @@
             z, yh = 2 * (i // NYH) + odd, i % NYH
             at = pl.multiple_of(((z * NYH + yh) * NC + c) * rows, rows)
             basis[pl.ds(at, rows), :] = ref[i * rows : (i + 1) * rows, :]
-    width = 256
-    for j in range(out.shape[1] // width):
-        cols = slice(j * width, (j + 1) * width)
-        total = jnp.zeros((tokens, width), F32)
+    half = tokens // 2
+    for part in range(2):
+        here = slice(part * half, (part + 1) * half)
+        total = jnp.zeros((half, out.shape[1]), F32)
         for n in range(parts):
-            if j == 0:
+            if part == 0:
                 copies[n].wait()
-            total += jnp.dot(blocks[n], basis[n * depth : (n + 1) * depth, cols], preferred_element_type=F32)
-        out[:, cols] = (total.astype(BF16).astype(F32) * mask[...]).astype(BF16)
+            total += jnp.dot(
+                blocks[n, here, :], basis[n * depth : (n + 1) * depth, :], preferred_element_type=F32
+            )
+        out[here, :] = (total.astype(BF16).astype(F32) * mask[here, :]).astype(BF16)
 
 
 def rotate_in(pos, gathered, planes, mask):
@@ -181,7 +183,7 @@
     chunk, grads = lax.optimization_barrier((chunk, other_core(grads)))
     planes = to_all(chunk, along_z)
     following = jnp.concatenate(from_z_neighbours(planes), axis=0)
-    return (planes, following, other_core(planes), other_core(following)), grads
+    return planes, following, other_core(planes), grads
 
 
 def gather_packed(activations, picked):
@@ -232,9 +234,11 @@
     height = out_basis.shape[0] // 2
     parity_rows = lax.dynamic_slice_in_dim(out_basis, lax.rem(z, 2) * height, height, 0)
     gathered = gather_packed(activations, pick(parity_rows, core))
-    planes, grads_other = gather_in_basis(in_basis, out_grads)
+    planes, following, planes_other, grads_other = gather_in_basis(in_basis, out_grads)
     basis = gathered.reshape(NYL * NX, -1, gathered.shape[1])[:, activations.shape[0] :]
-    below, above = from_z_neighbours(basis.reshape(-1, gathered.shape[1]))
+    basis, following = lax.optimization_barrier((basis.reshape(-1, gathered.shape[1]), following))
+    below, above = from_z_neighbours(basis)
+    planes = (planes, following, planes_other, other_core(following))
     mask = valid.astype(F32)[:, None]
     masked_in = rotate_in(pos, gathered, planes, mask)
     masked_other = other_core(masked_in)

time: 163 us -> 167 us (1.025)
  the two profiles are of different devices: /device:TPU:64 before, /device:TPU:66 now
where the time goes in v12:
time: 167 us; the launch traced here: 166 us
  blocking collectives  92.4 us (55%)
  starting transfers between devices  20.5 us (12%)
  waiting for transfers between devices  15.1 us (9%)
  between operations  14.5 us (9%)
  Pallas kernels  12.6 us (8%)
  local copies, waits for them, and re-layouts  7.22 us (4%)
  other arithmetic  2.72 us (2%)
    all_to_all x2, blocking collectives, to_all(): lax.all_to_all(copies, 'wide', 0, 0, axis_index_groups=groups)  54.2 us
    all_to_all x1, blocking collectives, scatter_sum(): lax.all_to_all(jnp.concatenate([coded, label], axis=1), 'wide', 0, 0, til...  38.2 us
    ppermute x8, starting transfers between devices, send(): return lax.ppermute(value, BOTH, pairs)  20.5 us
    ppermute x8, waiting for transfers between devices, send(): return lax.ppermute(value, BOTH, pairs)  15.1 us
    pallas_call x1, Pallas kernels, rotate_in(): pl.pallas_call(rotate_in_kernel, out_shape=jax.ShapeDtypeStruct((tokens,...  5.81 us
    pallas_call x1, Pallas kernels, rotate_out(): pl.pallas_call(rotate_out_kernel, out_shape=[jax.ShapeDtypeStruct((tokens...  4.98 us
  transfers between devices with their start and end apart: 9, of which 4 were waited for; matrix products, arithmetic and copies ran while one was open for 3% of the time, Pallas kernels for 6%

profile of v12, /device:TPU:66, one launch (start us, length us, event | category | flops | bytes accessed | tf_op | source)
XLA Modules:
  0.0 166.2 jit_solution(12977715032570613099)
XLA Ops:
  6.5 0.0 copy-start
  6.5 0.0 all-gather.2.cloned.1.call-start
  6.6 1.0 copy-done
  7.6 0.0 copy-start.5
  7.6 1.1 fusion.10
  8.7 0.0 copy-start.1
  8.7 0.0 copy-start.6
  8.7 0.0 copy-done.5
  8.7 0.9 maximum_maximum_fusion
  9.6 0.0 all-gather.2.cloned.1.call-update
  9.6 0.7 copy-done.1
  10.3 1.9 %collective-permute-start = (bf16[512,1536]{1,0:T(8,128)(2,1)S(1)}, bf16[512,1536]{1,0:T(8,128)(2,1)S(1)}, u32[]{:S(2)}, u32[]{:S(2)}) collective-permute-start(bf16[512,1536]{1,0:T(8,128)(2,1)S(1)} %copy-done.1), channel_id=1, source_target_pairs={{0,8},{1,9},{2,10},{3,11},{4,12},{5,13},{6,14},{7,15},{8,0},{9,1},... | collective-permute-start | bytes 4718600 | tf_op jit(solution)/shard_map/ppermute | solution.py:28
  12.2 0.0 copy-done.6
  12.3 18.3 %all_to_all.15 = bf16[4,64,512]{2,1,0:T(8,128)(2,1)S(1)} all-to-all(bf16[4,64,512]{2,1,0:T(8,128)(2,1)S(1)} %broadcast_in_dim.6), channel_id=1, replica_groups={{0,16,32,48},{8,24,40,56},{64,80,96,112},{72,88,104,120},{128,144,160,1..., dimensions={0} | all-to-all | bytes 524288 | tf_op jit(solution)/shard_map/all_to_all | solution.py:169
  30.6 0.0 collective-permute-done.theirs
  30.6 0.0 copy-start.3
  30.6 1.2 copy-done.3
  31.8 0.1 broadcast_in_dim.7
  31.9 35.9 %all_to_all.16 = bf16[4,256,512]{2,1,0:T(8,128)(2,1)S(1)} all-to-all(bf16[4,256,512]{2,1,0:T(8,128)(2,1)S(1)} %broadcast_in_dim.7), channel_id=1, replica_groups={{0,128,256,384},{8,136,264,392},{16,144,272,400},{24,152,280,408},{32,1..., dimensions={0} | all-to-all | bytes 2097152 | tf_op jit(solution)/shard_map/all_to_all | solution.py:169
  67.8 0.1 fusion.22
  67.9 1.9 %collective-permute-start.2 = (bf16[512,512]{1,0:T(8,128)(2,1)S(1)}, bf16[512,512]{1,0:T(8,128)(2,1)S(1)}, u32[]{:S(2)}, u32[]{:S(2)}) collective-permute-start(bf16[512,512]{1,0:T(8,128)(2,1)S(1)} %bitcast.30), channel_id=1, source_target_pairs={{0,448},{1,449},{2,450},{3,451},{4,452},{5,453},{6,454},{7,455},{8... | collective-permute-start | bytes 1572872 | tf_op jit(solution)/shard_map/ppermute | solution.py:28
  69.8 3.9 %collective-permute-start.1 = (bf16[512,512]{1,0:T(8,128)(2,1)S(1)}, bf16[512,512]{1,0:T(8,128)(2,1)S(1)}, u32[]{:S(2)}, u32[]{:S(2)}) collective-permute-start(bf16[512,512]{1,0:T(8,128)(2,1)S(1)} %bitcast.29), channel_id=1, source_target_pairs={{0,64},{1,65},{2,66},{3,67},{4,68},{5,69},{6,70},{7,71},{8,72},{9,... | collective-permute-start | bytes 1572872 | tf_op jit(solution)/shard_map/ppermute | solution.py:28
  73.7 1.9 %collective-permute-start.5 = (bf16[1024,512]{1,0:T(8,128)(2,1)S(1)}, bf16[1024,512]{1,0:T(8,128)(2,1)}, u32[]{:S(2)}, u32[]{:S(2)}) collective-permute-start(bf16[1024,512]{1,0:T(8,128)(2,1)S(1)} %bitcast.23), channel_id=1, source_target_pairs={{0,8},{1,9},{2,10},{3,11},{4,12},{5,13},{6,14},{7,15},{8,0},{9,1},... | collective-permute-start | bytes 3145736 | tf_op jit(solution)/shard_map/ppermute | solution.py:28
  75.7 7.0 %collective-permute-done.2 = bf16[512,512]{1,0:T(8,128)(2,1)S(1)} collective-permute-done((bf16[512,512]{1,0:T(8,128)(2,1)S(1)}, bf16[512,512]{1,0:T(8,128)(2,1)S(1)}, u32[]{:S(2)}, u32[]{:S(2)}) %collective-permute-start.2) | collective-permute-done | bytes 524320 | tf_op jit(solution)/shard_map/ppermute | solution.py:28
  82.7 2.6 %collective-permute-done.1 = bf16[512,512]{1,0:T(8,128)(2,1)S(1)} collective-permute-done((bf16[512,512]{1,0:T(8,128)(2,1)S(1)}, bf16[512,512]{1,0:T(8,128)(2,1)S(1)}, u32[]{:S(2)}, u32[]{:S(2)}) %collective-permute-start.1) | collective-permute-done | bytes 524320 | tf_op jit(solution)/shard_map/ppermute | solution.py:28
  85.3 0.1 pad_maximum_fusion.mine_next
  85.3 0.0 copy-start.7
  85.4 0.0 all-gather.2.cloned.1.call-done.gathered
  85.4 2.4 %slice.51 = bf16[8,144,512]{2,1,0:T(8,128)(2,1)} slice(bf16[8,656,512]{2,1,0:T(8,128)(2,1)} %bitcast.25), slice={[0:8], [512:656], [0:512]} | slice | bytes 2359296 | tf_op jit(solution)/shard_map/slice | solution.py:238
  87.8 1.9 %collective-permute-start.6 = (bf16[1024,512]{1,0:T(8,128)(2,1)S(1)}, bf16[1024,512]{1,0:T(8,128)(2,1)}, u32[]{:S(2)}, u32[]{:S(2)}) collective-permute-start(bf16[1024,512]{1,0:T(8,128)(2,1)S(1)} %pad_maximum_fusion.mine_next), channel_id=1, source_target_pairs={{0,8},{1,9},{2,10},{3,11},{4,12},{5,13},{6,14},{7,15},{8,0},{9,1},... | collective-permute-start | bytes 3145736 | tf_op jit(solution)/shard_map/ppermute | solution.py:28
  89.7 0.0 copy-done.7
  89.7 0.1 copy.11.mask
  89.9 1.3 fusion.21
  91.2 3.0 %collective-permute-start.3 = (bf16[576,512]{1,0:T(8,128)(2,1)S(1)}, bf16[576,512]{1,0:T(8,128)(2,1)S(1)}, u32[]{:S(2)}, u32[]{:S(2)}) collective-permute-start(bf16[576,512]{1,0:T(8,128)(2,1)S(1)} %get-tuple-element.22), channel_id=1, source_target_pairs={{0,64},{1,65},{2,66},{3,67},{4,68},{5,69},{6,70},{7,71},{8,72},{9,... | collective-permute-start | bytes 1769480 | tf_op jit(solution)/shard_map/ppermute | solution.py:28
  94.2 3.8 %collective-permute-start.4 = (bf16[576,512]{1,0:T(8,128)(2,1)S(1)}, bf16[576,512]{1,0:T(8,128)(2,1)S(1)}, u32[]{:S(2)}, u32[]{:S(2)}) collective-permute-start(bf16[576,512]{1,0:T(8,128)(2,1)S(1)} %get-tuple-element.21), channel_id=1, source_target_pairs={{0,448},{1,449},{2,450},{3,451},{4,452},{5,453},{6,454},{7,455},{8... | collective-permute-start | bytes 1769480 | tf_op jit(solution)/shard_map/ppermute | solution.py:28
  98.0 0.1 pad_add_fusion.pos
  98.1 0.0 copy-start.2
  98.1 0.0 copy-start.4
  98.1 0.0 collective-permute-done.5.other
  98.1 0.0 collective-permute-done.6.other_next
  98.1 5.8 %shard_map.56.ins_mine = bf16[512,512]{1,0:T(8,128)(2,1)S(1)} custom-call(s32[4]{0:T(128)S(1)} %pad_add_fusion.pos, bf16[5248,512]{1,0:T(8,128)(2,1)} %all-gather.2.cloned.1.call-done.gathered, bf16[1024,512]{1,0:T(8,128)(2,1)S(1)} %bitcast.24, bf16[1024,512]{1,0:T(8,128)(2,1)S(1)} %pad_maximum_fusion.mine_next, ...), custom_call_target="tpu_custom_call" | custom-call | flops 2147483648 | bytes 8912896 | tf_op jit(solution)/shard_map/pallas_call | solution.py:72
  103.9 2.1 %collective-permute-start.7 = (bf16[512,512]{1,0:T(8,128)(2,1)S(1)}, bf16[512,512]{1,0:T(8,128)(2,1)S(1)}, u32[]{:S(2)}, u32[]{:S(2)}) collective-permute-start(bf16[512,512]{1,0:T(8,128)(2,1)S(1)} %shard_map.56.ins_mine), channel_id=1, source_target_pairs={{0,8},{1,9},{2,10},{3,11},{4,12},{5,13},{6,14},{7,15},{8,0},{9,1},... | collective-permute-start | bytes 1572872 | tf_op jit(solution)/shard_map/ppermute | solution.py:28
  106.1 4.0 %collective-permute-done.3.below = bf16[576,512]{1,0:T(8,128)(2,1)S(1)} collective-permute-done((bf16[576,512]{1,0:T(8,128)(2,1)S(1)}, bf16[576,512]{1,0:T(8,128)(2,1)S(1)}, u32[]{:S(2)}, u32[]{:S(2)}) %collective-permute-start.3) | collective-permute-done | bytes 589856 | tf_op jit(solution)/shard_map/ppermute | solution.py:28
  110.1 1.5 collective-permute-done.4.above
  111.6 0.0 copy-done.2
  111.6 0.0 copy-done.4
  111.6 5.0 %shard_map.55 = (bf16[512,768]{1,0:T(8,128)(2,1)S(1)}, bf16[512,768]{1,0:T(8,128)(2,1)S(1)}) custom-call(s32[4]{0:T(128)S(1)} %pad_add_fusion.pos, bf16[5248,512]{1,0:T(8,128)(2,1)} %all-gather.2.cloned.1.call-done.gathered, bf16[576,512]{1,0:T(8,128)(2,1)S(1)} %collective-permute-done.3.below, bf16[576,512]{1,0:T(8,128)(2,1)S(1)} %collective-permute-done.4.above, ...), custom_call_target="tpu_custom_call" | custom-call | flops 2415919104 | bytes 7077888 | tf_op jit(solution)/shard_map/pallas_call | solution.py:126
  116.5 0.0 collective-permute-done.7.ins_theirs
  116.6 1.8 %shard_map.57 = (f32[768,512]{1,0:T(8,128)S(1)}, f32[8,512]{1,0:T(8,128)S(1)}) custom-call(bf16[512,768]{1,0:T(8,128)(2,1)S(1)} %get-tuple-element.16.outs_mine, bf16[512,768]{1,0:T(8,128)(2,1)S(1)} %get-tuple-element.17.outs_theirs, bf16[512,512]{1,0:T(8,128)(2,1)S(1)} %shard_map.56.ins_mine, bf16[512,512]{1,0:T(8,128)(2,1)S(1)} %collective-permute-done.7.ins_theirs), custom_call_target="tpu_custom_call" | custom-call | flops 805306368 | bytes 4194304 | tf_op jit(solution)/shard_map/pallas_call | solution.py:157
  118.4 0.6 reduce_max.9
  119.8 0.2 multiply_convert_fusion
  120.0 0.2 concatenate.15
  120.2 38.2 %all_to_all.17 = f16[32,104,128]{2,1,0:T(8,128)(2,1)S(1)} all-to-all(f16[32,104,128]{2,1,0:T(8,128)(2,1)S(1)} %concatenate.15), channel_id=1, replica_groups={{0,16,32,48,64,80,96,112,128,144,160,176,192,208,224,240,256,272,288,30..., dimensions={0} | all-to-all | bytes 1703936 | tf_op jit(solution)/shard_map/all_to_all | solution.py:219
  158.3 0.1 copy.13
  158.5 0.2 multiply_reduce_fusion
  158.7 0.6 broadcast_multiply_fusion
  (9 shorter events, 0.1 us)
Async XLA Ops:
  6.5 1.1 copy-start
  6.5 78.8 %all-gather.2.cloned.1.call-start = ((), (), s32[]{:S(2)}) async-start(), calls=%async_computation.3 | async-start | bytes 6045696 | tf_op jit(solution)/shard_map/all_gather | solution.py:194
  7.6 1.1 copy-start.5
  8.7 1.7 copy-start.1
  8.7 3.6 %copy-start.6 = (bf16[64,512]{1,0:T(8,128)(2,1)S(1)}, bf16[64,512]{1,0:T(8,128)(2,1)}, u32[]{:S(2)}) copy-start(bf16[64,512]{1,0:T(8,128)(2,1)} %param.7) | copy-start | bytes 196612
  10.3 20.3 %collective-permute-start = (bf16[512,1536]{1,0:T(8,128)(2,1)S(1)}, bf16[512,1536]{1,0:T(8,128)(2,1)S(1)}, u32[]{:S(2)}, u32[]{:S(2)}) collective-permute-start(bf16[512,1536]{1,0:T(8,128)(2,1)S(1)} %copy-done.1), channel_id=1, source_target_pairs={{0,8},{1,9},{2,10},{3,11},{4,12},{5,13},{6,14},{7,15},{8,0},{9,1},... | collective-permute-start | bytes 4718600 | tf_op jit(solution)/shard_map/ppermute | solution.py:28
  30.6 1.2 copy-start.3
  67.9 14.8 %collective-permute-start.2 = (bf16[512,512]{1,0:T(8,128)(2,1)S(1)}, bf16[512,512]{1,0:T(8,128)(2,1)S(1)}, u32[]{:S(2)}, u32[]{:S(2)}) collective-permute-start(bf16[512,512]{1,0:T(8,128)(2,1)S(1)} %bitcast.30), channel_id=1, source_target_pairs={{0,448},{1,449},{2,450},{3,451},{4,452},{5,453},{6,454},{7,455},{8... | collective-permute-start | bytes 1572872 | tf_op jit(solution)/shard_map/ppermute | solution.py:28
  69.8 15.5 %collective-permute-start.1 = (bf16[512,512]{1,0:T(8,128)(2,1)S(1)}, bf16[512,512]{1,0:T(8,128)(2,1)S(1)}, u32[]{:S(2)}, u32[]{:S(2)}) collective-permute-start(bf16[512,512]{1,0:T(8,128)(2,1)S(1)} %bitcast.29), channel_id=1, source_target_pairs={{0,64},{1,65},{2,66},{3,67},{4,68},{5,69},{6,70},{7,71},{8,72},{9,... | collective-permute-start | bytes 1572872 | tf_op jit(solution)/shard_map/ppermute | solution.py:28
  73.7 24.4 %collective-permute-start.5 = (bf16[1024,512]{1,0:T(8,128)(2,1)S(1)}, bf16[1024,512]{1,0:T(8,128)(2,1)}, u32[]{:S(2)}, u32[]{:S(2)}) collective-permute-start(bf16[1024,512]{1,0:T(8,128)(2,1)S(1)} %bitcast.23), channel_id=1, source_target_pairs={{0,8},{1,9},{2,10},{3,11},{4,12},{5,13},{6,14},{7,15},{8,0},{9,1},... | collective-permute-start | bytes 3145736 | tf_op jit(solution)/shard_map/ppermute | solution.py:28
  85.3 4.4 %copy-start.7 = (s32[512]{0:T(512)S(1)}, s32[512]{0:T(512)}, u32[]{:S(2)}) copy-start(s32[512]{0:T(512)} %param.9) | copy-start | bytes 6148
  87.8 10.3 %collective-permute-start.6 = (bf16[1024,512]{1,0:T(8,128)(2,1)S(1)}, bf16[1024,512]{1,0:T(8,128)(2,1)}, u32[]{:S(2)}, u32[]{:S(2)}) collective-permute-start(bf16[1024,512]{1,0:T(8,128)(2,1)S(1)} %pad_maximum_fusion.mine_next), channel_id=1, source_target_pairs={{0,8},{1,9},{2,10},{3,11},{4,12},{5,13},{6,14},{7,15},{8,0},{9,1},... | collective-permute-start | bytes 3145736 | tf_op jit(solution)/shard_map/ppermute | solution.py:28
  91.2 18.8 %collective-permute-start.3 = (bf16[576,512]{1,0:T(8,128)(2,1)S(1)}, bf16[576,512]{1,0:T(8,128)(2,1)S(1)}, u32[]{:S(2)}, u32[]{:S(2)}) collective-permute-start(bf16[576,512]{1,0:T(8,128)(2,1)S(1)} %get-tuple-element.22), channel_id=1, source_target_pairs={{0,64},{1,65},{2,66},{3,67},{4,68},{5,69},{6,70},{7,71},{8,72},{9,... | collective-permute-start | bytes 1769480 | tf_op jit(solution)/shard_map/ppermute | solution.py:28
  94.2 17.3 %collective-permute-start.4 = (bf16[576,512]{1,0:T(8,128)(2,1)S(1)}, bf16[576,512]{1,0:T(8,128)(2,1)S(1)}, u32[]{:S(2)}, u32[]{:S(2)}) collective-permute-start(bf16[576,512]{1,0:T(8,128)(2,1)S(1)} %get-tuple-element.21), channel_id=1, source_target_pairs={{0,448},{1,449},{2,450},{3,451},{4,452},{5,453},{6,454},{7,455},{8... | collective-permute-start | bytes 1769480 | tf_op jit(solution)/shard_map/ppermute | solution.py:28
  98.1 13.5 %copy-start.2 = (bf16[512,1536]{1,0:T(8,128)(2,1)S(1)}, bf16[512,1536]{1,0:T(8,128)(2,1)}, u32[]{:S(2)}) copy-start(bf16[512,1536]{1,0:T(8,128)(2,1)} %mine.1) | copy-start | bytes 4718596
  98.1 13.5 %copy-start.4 = (bf16[512,1536]{1,0:T(8,128)(2,1)S(1)}, bf16[512,1536]{1,0:T(8,128)(2,1)}, u32[]{:S(2)}) copy-start(bf16[512,1536]{1,0:T(8,128)(2,1)} %copy-done.3) | copy-start | bytes 4718596
  103.9 12.6 %collective-permute-start.7 = (bf16[512,512]{1,0:T(8,128)(2,1)S(1)}, bf16[512,512]{1,0:T(8,128)(2,1)S(1)}, u32[]{:S(2)}, u32[]{:S(2)}) collective-permute-start(bf16[512,512]{1,0:T(8,128)(2,1)S(1)} %shard_map.56.ins_mine), channel_id=1, source_target_pairs={{0,8},{1,9},{2,10},{3,11},{4,12},{5,13},{6,14},{7,15},{8,0},{9,1},... | collective-permute-start | bytes 1572872 | tf_op jit(solution)/shard_map/ppermute | solution.py:28
Sparse Core Ops, SparseCore 0:
  9.8 70.6 all-gather.1

commit v13 on v10

--- a/solution.py
+++ b/solution.py
@@ -160,9 +160,10 @@
     along_yh = [[(z * NYH + yh) * NC + c for yh in range(NYH)] for z in range(NZ) for c in range(NC)]
     along_z = [[z * NYH * NC + r for z in range(NZ)] for r in range(NYH * NC)]
     chunk = lax.all_gather(in_basis, "wide", axis=0, tiled=True, axis_index_groups=along_yh)
-    chunk, grads = lax.optimization_barrier((chunk, other_core(grads)))
+    chunk, grads = lax.optimization_barrier((chunk, grads))
     copies = jnp.broadcast_to(chunk[None], (NZ, *chunk.shape))
     got = lax.all_to_all(copies, "wide", 0, 0, axis_index_groups=along_z)
+    got, grads = lax.optimization_barrier((got, other_core(grads)))
     return got.reshape(-1, chunk.shape[1]), grads
 
 

time: 159 us -> 159 us (level)
  blocking collectives: 115 us -> 57.2 us
  waiting for transfers between devices: 3.97 us -> 50.3 us
  starting transfers between devices: 5.86 us -> 16.2 us
    all_to_all x1 -> x0, blocking collectives: 59.2 us -> none  [gather_in_basis(): got = lax.all_to_all(copies, 'wide', 0, 0, axis_index_groups=along_z)]
    all_to_all x0 -> x1, waiting for transfers between devices: none -> 41.9 us  [gather_in_basis(): got = lax.all_to_all(copies, 'wide', 0, 0, axis_index_groups=along_z)]
    all_to_all x0 -> x1, starting transfers between devices: none -> 10.4 us  [gather_in_basis(): got = lax.all_to_all(copies, 'wide', 0, 0, axis_index_groups=along_z)]
    ppermute x3, waiting for transfers between devices: 3.95 us -> 7.54 us  [send(): return lax.ppermute(value, BOTH, pairs)]
    all_to_all x1, blocking collectives: 40.3 us -> 42.8 us  [scatter_sum(): lax.all_to_all(jnp.concatenate([coded, label], axis=1), 'wide', 0, 0, til...]
  transfers between devices with their start and end apart: 4 -> 5, of which waited for: 1 -> 4; matrix products, arithmetic and copies ran while one was open for 0% -> 1% of each run, Pallas kernels for 3% -> 3%
where the time goes in v13:
time: 159 us; the launch traced here: 158 us
  blocking collectives  57.2 us (36%)
  waiting for transfers between devices  50.3 us (32%)
  starting transfers between devices  16.2 us (10%)
  between operations  14.4 us (9%)
  Pallas kernels  12.1 us (8%)
  local copies, waits for them, and re-layouts  4.25 us (3%)
  other arithmetic  2.72 us (2%)
    all_to_all x1, blocking collectives, scatter_sum(): lax.all_to_all(jnp.concatenate([coded, label], axis=1), 'wide', 0, 0, til...  42.8 us
    all_to_all x1, waiting for transfers between devices, gather_in_basis(): got = lax.all_to_all(copies, 'wide', 0, 0, axis_index_groups=along_z)  41.9 us
    all_gather x1, blocking collectives, gather_in_basis(): lax.all_gather(in_basis, 'wide', axis=0, tiled=True, axis_index_groups=al...  14.4 us
    all_to_all x1, starting transfers between devices, gather_in_basis(): got = lax.all_to_all(copies, 'wide', 0, 0, axis_index_groups=along_z)  10.4 us
    ppermute x3, waiting for transfers between devices, send(): return lax.ppermute(value, BOTH, pairs)  7.54 us
    pallas_call x1, Pallas kernels, rotate_in(): pl.pallas_call(rotate_in_kernel, out_shape=jax.ShapeDtypeStruct((tokens,...  5.79 us
    ppermute x3, starting transfers between devices, send(): return lax.ppermute(value, BOTH, pairs)  5.74 us
    pallas_call x1, Pallas kernels, rotate_out(): pl.pallas_call(rotate_out_kernel, out_shape=[jax.ShapeDtypeStruct((tokens...  4.49 us
  transfers between devices with their start and end apart: 5, of which 4 were waited for; matrix products, arithmetic and copies ran while one was open for 1% of the time, Pallas kernels for 3%

profile of v13, /device:TPU:50, one launch (start us, length us, event | category | flops | bytes accessed | tf_op | source)
XLA Modules:
  0.0 158.3 jit_solution(15119027464140540254)
XLA Ops:
  6.5 0.0 copy-start
  6.5 0.0 all-gather.2.cloned.1.call-start
  6.6 1.0 copy-done
  7.6 0.0 copy-start.4
  7.6 1.1 fusion.11
  8.7 0.0 copy-start.5
  8.7 0.0 copy-done.4
  8.8 0.9 maximum_maximum_fusion
  9.7 0.0 all-gather.2.cloned.1.call-update
  9.7 0.0 copy-done.5
  9.7 14.4 %all_gather.7 = bf16[256,512]{1,0:T(8,128)(2,1)S(1)} all-gather(bf16[64,512]{1,0:T(8,128)(2,1)S(1)} %copy-done.5), channel_id=1, replica_groups={{0,16,32,48},{8,24,40,56},{64,80,96,112},{72,88,104,120},{128,144,160,1..., dimensions={0}, use_global_device_ids=true | all-gather | bytes 327680 | tf_op jit(solution)/shard_map/all_gather | solution.py:162
  24.2 1.6 broadcast_in_dim.4
  25.8 0.0 copy-start.6
  25.8 10.4 %all-to-all-start = ((bf16[8,256,512]{2,1,0:T(8,128)(2,1)}), bf16[8,256,512]{2,1,0:T(8,128)(2,1)S(1)}, u32[]{:S(2)}, u32[]{:S(2)}) async-start(bf16[8,256,512]{2,1,0:T(8,128)(2,1)} %broadcast_in_dim.4), calls=%async_computation | async-start | bytes 4194304 | tf_op jit(solution)/shard_map/all_to_all | solution.py:165
  36.2 1.9 %collective-permute-start = (bf16[512,1536]{1,0:T(8,128)(2,1)}, bf16[512,1536]{1,0:T(8,128)(2,1)S(1)}, u32[]{:S(2)}, u32[]{:S(2)}) collective-permute-start(bf16[512,1536]{1,0:T(8,128)(2,1)} %mine.1), channel_id=1, source_target_pairs={{0,8},{1,9},{2,10},{3,11},{4,12},{5,13},{6,14},{7,15},{8,0},{9,1},... | collective-permute-start | bytes 4718600 | tf_op jit(solution)/shard_map/ppermute | solution.py:28
  38.1 3.6 %collective-permute-done.theirs = bf16[512,1536]{1,0:T(8,128)(2,1)S(1)} collective-permute-done((bf16[512,1536]{1,0:T(8,128)(2,1)}, bf16[512,1536]{1,0:T(8,128)(2,1)S(1)}, u32[]{:S(2)}, u32[]{:S(2)}) %collective-permute-start) | collective-permute-done | bytes 1572896 | tf_op jit(solution)/shard_map/ppermute | solution.py:28
  41.7 0.0 copy-start.2
  41.7 1.2 copy-done.2
  42.9 41.9 %all-to-all-done = bf16[8,256,512]{2,1,0:T(8,128)(2,1)S(1)} async-done(((bf16[8,256,512]{2,1,0:T(8,128)(2,1)}), bf16[8,256,512]{2,1,0:T(8,128)(2,1)S(1)}, u32[]{:S(2)}, u32[]{:S(2)}) %all-to-all-start) | async-done | bytes 2097184 | tf_op jit(solution)/shard_map/all_to_all | solution.py:165
  84.8 1.9 %collective-permute-start.1 = (bf16[2048,512]{1,0:T(8,128)(2,1)S(1)}, bf16[2048,512]{1,0:T(8,128)(2,1)}, u32[]{:S(2)}, u32[]{:S(2)}) collective-permute-start(bf16[2048,512]{1,0:T(8,128)(2,1)S(1)} %bitcast.21), channel_id=1, source_target_pairs={{0,8},{1,9},{2,10},{3,11},{4,12},{5,13},{6,14},{7,15},{8,0},{9,1},... | collective-permute-start | bytes 6291464 | tf_op jit(solution)/shard_map/ppermute | solution.py:28
  86.7 0.0 copy-done.6
  86.7 0.1 copy.11.mask
  86.9 0.1 pad_add_fusion.pos
  87.0 3.9 %collective-permute-done.1.other = bf16[2048,512]{1,0:T(8,128)(2,1)} collective-permute-done((bf16[2048,512]{1,0:T(8,128)(2,1)S(1)}, bf16[2048,512]{1,0:T(8,128)(2,1)}, u32[]{:S(2)}, u32[]{:S(2)}) %collective-permute-start.1) | collective-permute-done | bytes 2097184 | tf_op jit(solution)/shard_map/ppermute | solution.py:28
  90.9 0.9 all-gather.2.cloned.1.call-done.gathered
  91.8 0.0 copy-start.1
  91.8 0.0 copy-start.3
  91.8 5.8 %shard_map.56.ins_mine = bf16[512,512]{1,0:T(8,128)(2,1)S(1)} custom-call(s32[4]{0:T(128)S(1)} %pad_add_fusion.pos, bf16[6400,512]{1,0:T(8,128)(2,1)} %all-gather.2.cloned.1.call-done.gathered, bf16[2048,512]{1,0:T(8,128)(2,1)S(1)} %bitcast.22, bf16[2048,512]{1,0:T(8,128)(2,1)} %collective-permute-done.1.other, f32[512,1]{1,0:T(8,128)S(1)} %copy.11.mask), custom_call_target="tpu_custom_call" | custom-call | flops 2147483648 | bytes 8912896 | tf_op jit(solution)/shard_map/pallas_call | solution.py:70
  97.6 1.9 %collective-permute-start.2 = (bf16[512,512]{1,0:T(8,128)(2,1)S(1)}, bf16[512,512]{1,0:T(8,128)(2,1)S(1)}, u32[]{:S(2)}, u32[]{:S(2)}) collective-permute-start(bf16[512,512]{1,0:T(8,128)(2,1)S(1)} %shard_map.56.ins_mine), channel_id=1, source_target_pairs={{0,8},{1,9},{2,10},{3,11},{4,12},{5,13},{6,14},{7,15},{8,0},{9,1},... | collective-permute-start | bytes 1572872 | tf_op jit(solution)/shard_map/ppermute | solution.py:28
  99.6 0.0 copy-done.1
  99.6 0.0 copy-done.3
  99.6 4.5 %shard_map.55 = (bf16[512,768]{1,0:T(8,128)(2,1)S(1)}, bf16[512,768]{1,0:T(8,128)(2,1)S(1)}) custom-call(bf16[6400,512]{1,0:T(8,128)(2,1)} %all-gather.2.cloned.1.call-done.gathered, bf16[512,1536]{1,0:T(8,128)(2,1)S(1)} %copy-done.1, bf16[512,1536]{1,0:T(8,128)(2,1)S(1)} %copy-done.3), custom_call_target="tpu_custom_call" | custom-call | flops 2415919104 | bytes 7077888 | tf_op jit(solution)/shard_map/pallas_call | solution.py:118
  104.1 0.0 collective-permute-done.2.ins_theirs
  104.1 1.8 %shard_map.57 = (f32[768,512]{1,0:T(8,128)S(1)}, f32[8,512]{1,0:T(8,128)S(1)}) custom-call(bf16[512,768]{1,0:T(8,128)(2,1)S(1)} %get-tuple-element.20.outs_mine, bf16[512,768]{1,0:T(8,128)(2,1)S(1)} %get-tuple-element.21.outs_theirs, bf16[512,512]{1,0:T(8,128)(2,1)S(1)} %shard_map.56.ins_mine, bf16[512,512]{1,0:T(8,128)(2,1)S(1)} %collective-permute-done.2.ins_theirs), custom_call_target="tpu_custom_call" | custom-call | flops 805306368 | bytes 4194304 | tf_op jit(solution)/shard_map/pallas_call | solution.py:149
  105.9 0.6 reduce_max.9
  107.3 0.2 multiply_convert_fusion
  107.5 0.2 concatenate.11
  107.7 42.8 %all_to_all.10 = f16[32,104,128]{2,1,0:T(8,128)(2,1)S(1)} all-to-all(f16[32,104,128]{2,1,0:T(8,128)(2,1)S(1)} %concatenate.11), channel_id=1, replica_groups={{0,16,32,48,64,80,96,112,128,144,160,176,192,208,224,240,256,272,288,30..., dimensions={0} | all-to-all | bytes 1703936 | tf_op jit(solution)/shard_map/all_to_all | solution.py:200
  150.5 0.1 copy.13
  150.6 0.2 multiply_reduce_fusion
  150.8 0.6 broadcast_multiply_fusion
  (8 shorter events, 0.1 us)
Async XLA Ops:
  6.5 1.1 copy-start
  6.5 85.3 %all-gather.2.cloned.1.call-start = ((), (), s32[]{:S(2)}) async-start(), calls=%async_computation.2 | async-start | bytes 7372800 | tf_op jit(solution)/shard_map/all_gather | solution.py:175
  7.6 1.1 copy-start.4
  8.7 1.0 copy-start.5
  25.8 60.9 %copy-start.6 = (s32[512]{0:T(512)S(1)}, s32[512]{0:T(512)}, u32[]{:S(2)}) copy-start(s32[512]{0:T(512)} %param.9) | copy-start | bytes 6148
  25.8 59.0 %all-to-all-start = ((bf16[8,256,512]{2,1,0:T(8,128)(2,1)}), bf16[8,256,512]{2,1,0:T(8,128)(2,1)S(1)}, u32[]{:S(2)}, u32[]{:S(2)}) async-start(bf16[8,256,512]{2,1,0:T(8,128)(2,1)} %broadcast_in_dim.4), calls=%async_computation | async-start | bytes 4194304 | tf_op jit(solution)/shard_map/all_to_all | solution.py:165
  36.2 5.5 %collective-permute-start = (bf16[512,1536]{1,0:T(8,128)(2,1)}, bf16[512,1536]{1,0:T(8,128)(2,1)S(1)}, u32[]{:S(2)}, u32[]{:S(2)}) collective-permute-start(bf16[512,1536]{1,0:T(8,128)(2,1)} %mine.1), channel_id=1, source_target_pairs={{0,8},{1,9},{2,10},{3,11},{4,12},{5,13},{6,14},{7,15},{8,0},{9,1},... | collective-permute-start | bytes 4718600 | tf_op jit(solution)/shard_map/ppermute | solution.py:28
  41.7 1.2 copy-start.2
  84.8 6.2 %collective-permute-start.1 = (bf16[2048,512]{1,0:T(8,128)(2,1)S(1)}, bf16[2048,512]{1,0:T(8,128)(2,1)}, u32[]{:S(2)}, u32[]{:S(2)}) collective-permute-start(bf16[2048,512]{1,0:T(8,128)(2,1)S(1)} %bitcast.21), channel_id=1, source_target_pairs={{0,8},{1,9},{2,10},{3,11},{4,12},{5,13},{6,14},{7,15},{8,0},{9,1},... | collective-permute-start | bytes 6291464 | tf_op jit(solution)/shard_map/ppermute | solution.py:28
  91.8 7.7 %copy-start.1 = (bf16[512,1536]{1,0:T(8,128)(2,1)S(1)}, bf16[512,1536]{1,0:T(8,128)(2,1)}, u32[]{:S(2)}) copy-start(bf16[512,1536]{1,0:T(8,128)(2,1)} %mine.1) | copy-start | bytes 4718596
  91.8 7.7 %copy-start.3 = (bf16[512,1536]{1,0:T(8,128)(2,1)S(1)}, bf16[512,1536]{1,0:T(8,128)(2,1)}, u32[]{:S(2)}) copy-start(bf16[512,1536]{1,0:T(8,128)(2,1)} %copy-done.2) | copy-start | bytes 4718596
  97.6 6.4 %collective-permute-start.2 = (bf16[512,512]{1,0:T(8,128)(2,1)S(1)}, bf16[512,512]{1,0:T(8,128)(2,1)S(1)}, u32[]{:S(2)}, u32[]{:S(2)}) collective-permute-start(bf16[512,512]{1,0:T(8,128)(2,1)S(1)} %shard_map.56.ins_mine), channel_id=1, source_target_pairs={{0,8},{1,9},{2,10},{3,11},{4,12},{5,13},{6,14},{7,15},{8,0},{9,1},... | collective-permute-start | bytes 1572872 | tf_op jit(solution)/shard_map/ppermute | solution.py:28
Sparse Core Ops, SparseCore 0:
  9.8 81.9 all-gather.1
